TPU v7x, 32 devices: a whole 2x2x4 slice. The times are simulated.
32 devices in a mesh: narrow: 4 (over z), wide: 8 (over y, x, core).
Axes of the slice: x: 2, y: 2, z: 4, core: 2. Of those that a mesh axis runs over, the one named last changes fastest.
Arguments:
- field: float32 [32, 128, 1024], P('narrow', 'wide'), may hold values from -12 to 12
- start_block: float32 [1024, 128], replicated, may hold values from -6 to 6
Outputs:
- mode2_gram: float32 [32, 32], P('narrow', 'wide')
All inputs are finite; a program needn't handle non-finite values.
Results may differ from a plain program's by a relative error of at most 0.0001.
Values sent between devices are 32-bit elements; how exact they have to be, the bound alone decides.
No kernel may reach another device: no remote copies, remote signals or barrier semaphores. Data moves between devices by JAX's collectives and lax.ppermute only.
A program may use at most 64 MiB of HBM per device.

v0:
```python
import functools
import jax
import jax.numpy as jnp
from jax import lax
from jax.experimental import pallas as pl
from jax.experimental.pallas import tpu as pltpu
from jax.sharding import PartitionSpec as P

ITERS = 4
BLOCK = 128
PANEL = 8
HIGHEST = lax.Precision.HIGHEST
NN = (((1,), (0,)), ((), ()))
NT = (((1,), (1,)), ((), ()))
SCALARS = pl.BlockSpec(memory_space=pltpu.SMEM)
VMEM = pl.BlockSpec(memory_space=pltpu.VMEM)


def split(values):
    high = values.astype(jnp.bfloat16)
    return high, (values - high.astype(jnp.float32)).astype(jnp.bfloat16)


def dot_bf16(left, right, dims):
    return lax.dot_general(left, right, dims, preferred_element_type=jnp.float32)


def dot_split(left, right, dims):
    (left_high, left_low), (right_high, right_low) = left, right
    return (
        dot_bf16(left_high, right_high, dims)
        + (dot_bf16(left_low, right_high, dims) + dot_bf16(left_high, right_low, dims))
    )


def dot_full(left, right, dims):
    return lax.dot_general(left, right, dims, precision=HIGHEST, preferred_element_type=jnp.float32)


def inverse_factor(matrix, out_ref):
    order = matrix.shape[0]
    panels = order // PANEL
    tiles = [matrix[PANEL * i : PANEL * (i + 1), :] for i in range(panels)]
    lane = lax.broadcasted_iota(jnp.int32, (PANEL, order), 1)

    def full(part):
        return jnp.broadcast_to(part, (PANEL, order))

    for p in range(panels):
        tile, start = tiles[p], PANEL * p
        inside = (lane >= start) & (lane < start + PANEL)
        columns = [full(tile[:, start + c : start + c + 1]) for c in range(PANEL)]
        pivot = {(r, c): full(columns[c][r : r + 1, :]) for c in range(PANEL) for r in range(c, PANEL)}
        rows = [
            jnp.where(inside, jnp.where(lane == start + c, 1.0, 0.0), full(tile[c : c + 1, :]))
            for c in range(PANEL)
        ]
        lower, inverse = {}, {}
        for c in range(PANEL):
            scale = lax.rsqrt(pivot[c, c])
            inverse[c, c] = scale
            for r in range(c + 1, PANEL):
                lower[r, c] = pivot[r, c] * scale
            for d in range(c + 1, PANEL):
                for r in range(d, PANEL):
                    pivot[r, d] = pivot[r, d] - lower[r, c] * lower[d, c]
        for c in range(PANEL):
            for r in range(c + 1, PANEL):
                total = lower[r, c] * inverse[c, c]
                for k in range(c + 1, r):
                    total = total + lower[r, k] * inverse[k, c]
                inverse[r, c] = -(inverse[r, r] * total)
        solved = []
        for r in range(PANEL):
            total = inverse[r, 0] * rows[0]
            for c in range(1, r + 1):
                total = total + inverse[r, c] * rows[c]
            solved.append(total)
            out_ref[start + r : start + r + 1, :] = jnp.where(lane < start + PANEL, total, 0.0)[0:1, :]
        if p == panels - 1:
            break
        eliminate = []
        for c in range(PANEL):
            total = inverse[PANEL - 1, c] * solved[PANEL - 1]
            for r in range(c, PANEL - 1):
                total = total + inverse[r, c] * solved[r]
            eliminate.append(total)
        for i in range(p + 1, panels):
            total = jnp.where(inside, 0.0, tiles[i])
            for c in range(PANEL):
                total = total - full(tiles[i][:, start + c : start + c + 1]) * eliminate[c]
            tiles[i] = total


def start_kernel(start_ref, out_ref, factor_ref):
    rows = start_ref[...].T
    inverse_factor(dot_full(rows, rows, NT), factor_ref)
    out_ref[...] = dot_full(factor_ref[...], rows, NN)


def gram_kernel(blocks, where_ref, own_ref, other_ref, *refs):
    outs, (high_ref, low_ref) = refs[:-2], refs[-2:]
    band = outs[0].shape[1]
    order = own_ref.shape[1]
    rows = own_ref.shape[0]
    for part, ref in enumerate((own_ref, other_ref)):
        high, low = split(ref[...])
        for target, values in ((high_ref, high), (low_ref, low)):
            target[rows * part : rows * (part + 1), 0:order] = values
            target[rows * part : rows * (part + 1), order : order + band - BLOCK] = values[:, : band - BLOCK]
    group, core = where_ref[0], where_ref[1]
    for k, out in enumerate(outs):
        first = pl.multiple_of((2 * jnp.bitwise_xor(group, k) + core) * BLOCK, BLOCK)
        left = [ref[:, pl.ds(first, BLOCK)].astype(jnp.float32).T.astype(jnp.bfloat16) for ref in (high_ref, low_ref)]
        right = [ref[:, pl.ds(first, band)] for ref in (high_ref, low_ref)]
        out[...] = dot_split(left, right, NN)


def cut_kernel(count, where_ref, *refs):
    terms, outs = refs[: len(refs) - count], refs[len(refs) - count :]
    rows = outs[0].shape[0]
    plane = where_ref[2]
    for k, out in enumerate(outs):
        piece = pl.ds(pl.multiple_of(jnp.bitwise_xor(plane, k) * rows, rows), rows)
        total = terms[0][piece, :]
        for term in terms[1:]:
            total = total + term[piece, :]
        out[...] = total


def add_kernel(*refs):
    total = refs[0][...]
    for term in refs[1:-1]:
        total = total + term[...]
    refs[-1][...] = total


def join_kernel(where_ref, *refs):
    pieces, out = refs[:-1], refs[-1]
    rows = pieces[0].shape[0]
    plane = where_ref[2]
    for k, piece in enumerate(pieces):
        out[pl.ds(pl.multiple_of(jnp.bitwise_xor(plane, k) * rows, rows), rows), :] = piece[...]


def sweep(basis, gram_high, gram_low, factor_ref):
    image = dot_split(split(basis), (gram_high, gram_low), NN)
    inverse_factor(dot_full(image, image, NT), factor_ref)
    return dot_full(factor_ref[...], image, NN)


def sweeps_and_core(basis_ref, field_ref, core_ref, high_ref, low_ref, factor_ref, basis_scratch):
    basis_scratch[...] = basis_ref[...]

    def body(step, carry):
        basis_scratch[...] = sweep(basis_scratch[...], high_ref[...], low_ref[...], factor_ref)
        return carry

    lax.fori_loop(0, ITERS, body, 0)
    core_ref[...] = dot_full(field_ref[...], basis_scratch[...], NT)


def banded_kernel(blocks, where_ref, basis_ref, field_ref, *refs):
    bands, (core_ref, high_ref, low_ref, factor_ref, basis_scratch) = refs[:-5], refs[-5:]
    group, core = where_ref[0], where_ref[1]
    half = len(bands) // 2
    for place, band in enumerate(bands):
        side = core if place < half else 1 - core
        row = 2 * jnp.bitwise_xor(group, place % half) + side
        rows = pl.ds(pl.multiple_of(row * BLOCK, BLOCK), BLOCK)
        for k in range(blocks // 2 + 1):
            column = lax.rem(row + k, blocks)
            columns = pl.ds(pl.multiple_of(column * BLOCK, BLOCK), BLOCK)
            part = band[:, BLOCK * k : BLOCK * (k + 1)]
            high_ref[rows, columns], low_ref[rows, columns] = split(part)
            if 0 < k < blocks // 2:
                high_ref[columns, rows], low_ref[columns, rows] = split(part.T)
    sweeps_and_core(basis_ref, field_ref, core_ref, high_ref, low_ref, factor_ref, basis_scratch)


def whole_kernel(basis_ref, field_ref, gram_ref, core_ref, high_ref, low_ref, factor_ref, basis_scratch):
    high_ref[...], low_ref[...] = split(gram_ref[...])
    sweeps_and_core(basis_ref, field_ref, core_ref, high_ref, low_ref, factor_ref, basis_scratch)


def pair_kernel(cells_three, where_ref, own_ref, *refs):
    cores, out_ref = refs[:-1], refs[-1]
    size = own_ref.shape[0]
    cells_two = size // cells_three
    row = lax.broadcasted_iota(jnp.int32, (size, size), 0)
    column = lax.broadcasted_iota(jnp.int32, (size, size), 1)
    same = lax.rem(row, cells_three) == lax.rem(column, cells_three)
    rows = jnp.where(
        lax.broadcasted_iota(jnp.int32, (cells_two, size), 0)
        == lax.broadcasted_iota(jnp.int32, (cells_two, size), 1) // cells_three,
        1.0,
        0.0,
    )
    width = out_ref.shape[1]
    target = lax.broadcasted_iota(jnp.int32, (size, width), 1)
    source = lax.broadcasted_iota(jnp.int32, (size, width), 0) // cells_three
    plane = where_ref[2]
    total = jnp.zeros(out_ref.shape, jnp.float32)
    for k, core in enumerate((own_ref, *cores)):
        product = jnp.where(same, dot_full(own_ref[...], core[...], NT), 0.0)
        place = jnp.where(target == source + jnp.bitwise_xor(plane, k) * cells_two, 1.0, 0.0)
        total = total + dot_full(dot_full(rows, product, NN), place, NN)
    out_ref[...] = total


def call(kernel, outs, name, operands, scratch=(), scalars=0, flops=0, limit=32):
    shapes = [jax.ShapeDtypeStruct(shape, jnp.float32) for shape in outs]
    touched = sum(operand.size for operand in operands) + sum(shape.size for shape in shapes)
    result = pl.pallas_call(
        kernel,
        out_shape=shapes,
        in_specs=[SCALARS] * scalars + [VMEM] * (len(operands) - scalars),
        out_specs=[VMEM] * len(shapes),
        scratch_shapes=list(scratch),
        compiler_params=pltpu.CompilerParams(vmem_limit_bytes=limit * 2**20),
        cost_estimate=pl.CostEstimate(flops=flops, bytes_accessed=4 * touched, transcendentals=0),
        name=name,
    )(*operands)
    return result if len(outs) > 1 else result[0]


def swap(array, axis, mask):
    return lax.ppermute(array, axis, [(i, i ^ mask) for i in range(lax.axis_size(axis))])


def shards(field, start_block):
    cells_two, cells_three, order = field.shape
    rank = start_block.shape[1]
    narrow, wide = lax.axis_size("narrow"), lax.axis_size("wide")
    unfolded = field.reshape(cells_two * cells_three, order)
    cells = unfolded.shape[0]
    place, plane = lax.axis_index("wide"), lax.axis_index("narrow")
    where = jnp.stack([place // 2, place % 2, plane]).astype(jnp.int32)
    basis = call(
        start_kernel, [(rank, order)], "orth_start", [start_block], [pltpu.VMEM((rank, rank), jnp.float32)], flops=10**9
    )
    scratch = [
        pltpu.VMEM((order, order), jnp.bfloat16),
        pltpu.VMEM((order, order), jnp.bfloat16),
        pltpu.VMEM((rank, rank), jnp.float32),
        pltpu.VMEM((rank, order), jnp.float32),
    ]
    blocks = order // BLOCK
    if wide == blocks and narrow & (narrow - 1) == 0 and BLOCK % (8 * narrow) == 0:
        groups = wide // 2
        band = BLOCK * (blocks // 2 + 1)
        other = swap(unfolded, "wide", 1)
        parts = call(
            functools.partial(gram_kernel, blocks),
            [(BLOCK, band)] * groups,
            "gram_band",
            [where, unfolded, other],
            [pltpu.VMEM((2 * cells, order + band - BLOCK), jnp.bfloat16)] * 2,
            scalars=1,
        )
        arrived = [swap(parts[k], "wide", 2 * k) for k in range(1, groups)]
        cuts = call(
            functools.partial(cut_kernel, narrow),
            [(BLOCK // narrow, band)] * narrow,
            "sum_groups",
            [where, parts[0], *arrived],
            scalars=1,
        )
        arrived = [swap(cuts[k], "narrow", k) for k in range(1, narrow)]
        piece = call(add_kernel, [(BLOCK // narrow, band)], "sum_planes", [cuts[0], *arrived])
        arrived = [swap(piece, "narrow", k) for k in range(1, narrow)]
        joined = call(join_kernel, [(BLOCK, band)], "join_planes", [where, piece, *arrived], scalars=1)
        bands = [joined] + [swap(joined, "wide", 2 * k) for k in range(1, groups)]
        bands = bands + [swap(part, "wide", 1) for part in bands]
        core = call(
            functools.partial(banded_kernel, blocks),
            [(cells, rank)],
            "sweeps",
            [where, basis, unfolded, *bands],
            scratch,
            scalars=1,
        )
    else:
        gram = lax.psum(lax.dot_general(unfolded, unfolded, (((0,), (0,)), ((), ())), precision=HIGHEST), ("narrow", "wide"))
        core = call(whole_kernel, [(cells, rank)], "sweeps", [basis, unfolded, gram], scratch)
    if narrow & (narrow - 1) == 0 and wide & (wide - 1) == 0:
        cores = [swap(core, "narrow", k) for k in range(1, narrow)]
        width = -(-narrow * cells_two // BLOCK) * BLOCK
        total = call(
            functools.partial(pair_kernel, cells_three),
            [(cells_two, width)],
            "pair_gram",
            [where, core, *cores],
            scalars=1,
        )
        mask = 1
        while mask < wide:
            total = total + swap(total, "wide", mask)
            mask *= 2
        columns = narrow * cells_two // wide
        finished = lax.dynamic_slice_in_dim(total, place * columns, columns, 1)
    else:
        merged = core.reshape(cells_two, cells_three * rank)
        everyone = lax.all_gather(merged, "narrow", axis=0, tiled=True)
        part = lax.dot_general(merged, everyone, NT, precision=HIGHEST)
        finished = lax.psum_scatter(part, "wide", scatter_dimension=1, tiled=True)
    return finished / (rank * cells_three * wide)


def solution(mesh):
    return jax.shard_map(
        shards,
        mesh=mesh,
        in_specs=(P("narrow", "wide", None), P()),
        out_specs=P("narrow", "wide"),
        check_vma=False,
    )
```

profile of v0, /device:TPU:0, one launch (start us, length us, event | category | flops | bytes accessed | tf_op | source)
XLA Modules:
  0.0 121.8 jit_solution(432935916886242311)
XLA Ops:
  0.0 0.5 collective-permute-start
  0.5 0.1 pad_add_fusion.where_ref
  0.5 1.7 %collective-permute-done.other_ref = f32[128,1024]{1,0:T(8,128)S(1)} collective-permute-done((f32[128,1024]{1,0:T(8,128)}, f32[128,1024]{1,0:T(8,128)S(1)}, u32[]{:S(2)}, u32[]{:S(2)}) %collective-permute-start) | collective-permute-done | bytes 524320 | tf_op jit(solution)/shard_map/ppermute | solution.py:228
  2.2 1.0 copy-done
  3.2 1.6 %gram_band.1 = (f32[128,640]{1,0:T(8,128)S(1)}, f32[128,640]{1,0:T(8,128)S(1)}, f32[128,640]{1,0:T(8,128)S(1)}, f32[128,640]{1,0:T(8,128)S(1)}) custom-call(s32[3]{0:T(128)S(1)} %pad_add_fusion.where_ref, f32[128,1024]{1,0:T(8,128)S(1)} %bitcast.5, f32[128,1024]{1,0:T(8,128)S(1)} %collective-permute-done.other_ref), custom_call_target="tpu_custom_call" | custom-call | bytes 2359308 | tf_op jit(solution)/shard_map/gram_band/pallas_call | solution.py:214
  4.8 2.9 %collective-permute-start.1 = (f32[128,640]{1,0:T(8,128)S(1)}, f32[128,640]{1,0:T(8,128)S(1)}, u32[]{:S(2)}, u32[]{:S(2)}) collective-permute-start(f32[128,640]{1,0:T(8,128)S(1)} %get-tuple-element.14), channel_id=1, source_target_pairs={{0,2},{1,3},{2,0},{3,1},{4,6},{5,7},{6,4},{7,5},{8,10},{9,11},{10,... | collective-permute-start | bytes 983048 | tf_op jit(solution)/shard_map/ppermute | solution.py:228
  7.8 1.5 %collective-permute-start.2 = (f32[128,640]{1,0:T(8,128)S(1)}, f32[128,640]{1,0:T(8,128)S(1)}, u32[]{:S(2)}, u32[]{:S(2)}) collective-permute-start(f32[128,640]{1,0:T(8,128)S(1)} %get-tuple-element.15), channel_id=1, source_target_pairs={{0,4},{1,5},{2,6},{3,7},{4,0},{5,1},{6,2},{7,3},{8,12},{9,13},{10,... | collective-permute-start | bytes 983048 | tf_op jit(solution)/shard_map/ppermute | solution.py:228
  9.3 0.0 collective-permute-start.3
  9.3 7.0 %collective-permute-done.1.refs_1_ = f32[128,640]{1,0:T(8,128)S(1)} collective-permute-done((f32[128,640]{1,0:T(8,128)S(1)}, f32[128,640]{1,0:T(8,128)S(1)}, u32[]{:S(2)}, u32[]{:S(2)}) %collective-permute-start.1) | collective-permute-done | bytes 327712 | tf_op jit(solution)/shard_map/ppermute | solution.py:228
  16.3 8.0 %collective-permute-done.2.refs_2_ = f32[128,640]{1,0:T(8,128)S(1)} collective-permute-done((f32[128,640]{1,0:T(8,128)S(1)}, f32[128,640]{1,0:T(8,128)S(1)}, u32[]{:S(2)}, u32[]{:S(2)}) %collective-permute-start.2) | collective-permute-done | bytes 327712 | tf_op jit(solution)/shard_map/ppermute | solution.py:228
  24.3 0.0 collective-permute-done.3.refs_3_
  24.3 0.6 sum_groups.1
  24.9 1.6 %collective-permute-start.4 = (f32[32,640]{1,0:T(8,128)S(1)}, f32[32,640]{1,0:T(8,128)S(1)}, u32[]{:S(2)}, u32[]{:S(2)}) collective-permute-start(f32[32,640]{1,0:T(8,128)S(1)} %get-tuple-element.18), channel_id=1, source_target_pairs={{0,8},{8,0},{16,24},{24,16},{1,9},{9,1},{17,25},{25,17},{2,10},{10... | collective-permute-start | bytes 245768 | tf_op jit(solution)/shard_map/ppermute | solution.py:228
  26.5 2.6 %collective-permute-start.5 = (f32[32,640]{1,0:T(8,128)S(1)}, f32[32,640]{1,0:T(8,128)S(1)}, u32[]{:S(2)}, u32[]{:S(2)}) collective-permute-start(f32[32,640]{1,0:T(8,128)S(1)} %get-tuple-element.19), channel_id=1, source_target_pairs={{0,16},{8,24},{16,0},{24,8},{1,17},{9,25},{17,1},{25,9},{2,18},{10... | collective-permute-start | bytes 245768 | tf_op jit(solution)/shard_map/ppermute | solution.py:228
  29.1 0.2 collective-permute-start.6
  29.3 0.8 collective-permute-done.4.refs_1_
  30.2 3.9 %collective-permute-done.5.refs_2_ = f32[32,640]{1,0:T(8,128)S(1)} collective-permute-done((f32[32,640]{1,0:T(8,128)S(1)}, f32[32,640]{1,0:T(8,128)S(1)}, u32[]{:S(2)}, u32[]{:S(2)}) %collective-permute-start.5) | collective-permute-done | bytes 81952 | tf_op jit(solution)/shard_map/ppermute | solution.py:228
  34.1 1.4 %collective-permute-done.6.refs_3_ = f32[32,640]{1,0:T(8,128)S(1)} collective-permute-done((f32[32,640]{1,0:T(8,128)S(1)}, f32[32,640]{1,0:T(8,128)S(1)}, u32[]{:S(2)}, u32[]{:S(2)}) %collective-permute-start.6) | collective-permute-done | bytes 81952 | tf_op jit(solution)/shard_map/ppermute | solution.py:228
  35.5 2.1 %collective-permute-start.9 = (f32[32,640]{1,0:T(8,128)S(1)}, f32[32,640]{1,0:T(8,128)S(1)}, u32[]{:S(2)}, u32[]{:S(2)}) collective-permute-start(f32[32,640]{1,0:T(8,128)S(1)} %sum_planes.1.refs_0_), channel_id=1, source_target_pairs={{0,24},{8,16},{16,8},{24,0},{1,25},{9,17},{17,9},{25,1},{2,26},{10... | collective-permute-start | bytes 245768 | tf_op jit(solution)/shard_map/ppermute | solution.py:228
  37.5 0.4 collective-permute-start.8
  38.0 2.0 %collective-permute-start.7 = (f32[32,640]{1,0:T(8,128)S(1)}, f32[32,640]{1,0:T(8,128)S(1)}, u32[]{:S(2)}, u32[]{:S(2)}) collective-permute-start(f32[32,640]{1,0:T(8,128)S(1)} %sum_planes.1.refs_0_), channel_id=1, source_target_pairs={{0,8},{8,0},{16,24},{24,16},{1,9},{9,1},{17,25},{25,17},{2,10},{10... | collective-permute-start | bytes 245768 | tf_op jit(solution)/shard_map/ppermute | solution.py:228
  39.9 2.0 %collective-permute-done.9.refs_3_ = f32[32,640]{1,0:T(8,128)S(1)} collective-permute-done((f32[32,640]{1,0:T(8,128)S(1)}, f32[32,640]{1,0:T(8,128)S(1)}, u32[]{:S(2)}, u32[]{:S(2)}) %collective-permute-start.9) | collective-permute-done | bytes 81952 | tf_op jit(solution)/shard_map/ppermute | solution.py:228
  41.9 1.8 %collective-permute-done.8.refs_2_ = f32[32,640]{1,0:T(8,128)S(1)} collective-permute-done((f32[32,640]{1,0:T(8,128)S(1)}, f32[32,640]{1,0:T(8,128)S(1)}, u32[]{:S(2)}, u32[]{:S(2)}) %collective-permute-start.8) | collective-permute-done | bytes 81952 | tf_op jit(solution)/shard_map/ppermute | solution.py:228
  43.7 0.0 collective-permute-done.7.refs_1_
  43.7 0.6 join_planes.1.refs_0_
  44.3 0.0 copy-start.1
  44.3 1.5 %collective-permute-start.12 = (f32[128,640]{1,0:T(8,128)S(1)}, f32[128,640]{1,0:T(8,128)S(1)}, u32[]{:S(2)}, u32[]{:S(2)}) collective-permute-start(f32[128,640]{1,0:T(8,128)S(1)} %join_planes.1.refs_0_), channel_id=1, source_target_pairs={{0,6},{1,7},{2,4},{3,5},{4,2},{5,3},{6,0},{7,1},{8,14},{9,15},{10,... | collective-permute-start | bytes 983048 | tf_op jit(solution)/shard_map/ppermute | solution.py:228
  45.9 1.6 %collective-permute-start.11 = (f32[128,640]{1,0:T(8,128)S(1)}, f32[128,640]{1,0:T(8,128)S(1)}, u32[]{:S(2)}, u32[]{:S(2)}) collective-permute-start(f32[128,640]{1,0:T(8,128)S(1)} %join_planes.1.refs_0_), channel_id=1, source_target_pairs={{0,4},{1,5},{2,6},{3,7},{4,0},{5,1},{6,2},{7,3},{8,12},{9,13},{10,... | collective-permute-start | bytes 983048 | tf_op jit(solution)/shard_map/ppermute | solution.py:228
  47.4 0.4 collective-permute-start.10
  47.9 0.0 collective-permute-start.13
  47.9 7.1 %collective-permute-done.12.refs_3_ = f32[128,640]{1,0:T(8,128)S(1)} collective-permute-done((f32[128,640]{1,0:T(8,128)S(1)}, f32[128,640]{1,0:T(8,128)S(1)}, u32[]{:S(2)}, u32[]{:S(2)}) %collective-permute-start.12) | collective-permute-done | bytes 327712 | tf_op jit(solution)/shard_map/ppermute | solution.py:228
  55.0 3.4 %collective-permute-done.11.refs_2_ = f32[128,640]{1,0:T(8,128)S(1)} collective-permute-done((f32[128,640]{1,0:T(8,128)S(1)}, f32[128,640]{1,0:T(8,128)S(1)}, u32[]{:S(2)}, u32[]{:S(2)}) %collective-permute-start.11) | collective-permute-done | bytes 327712 | tf_op jit(solution)/shard_map/ppermute | solution.py:228
  58.4 0.5 collective-permute-done.10.refs_1_
  58.9 7.2 %orth_start.1.basis_ref = f32[128,1024]{1,0:T(8,128)S(1)} custom-call(f32[1024,128]{1,0:T(8,128)S(1)} %copy-done.2), custom_call_target="tpu_custom_call" | custom-call | flops 1000000000 | bytes 1048576 | tf_op jit(solution)/shard_map/orth_start/pallas_call | solution.py:214
  66.2 34.5 %sweeps.1.own_ref = f32[128,128]{1,0:T(8,128)S(1)} custom-call(s32[3]{0:T(128)S(1)} %pad_add_fusion.where_ref, f32[128,1024]{1,0:T(8,128)S(1)} %orth_start.1.basis_ref, f32[128,1024]{1,0:T(8,128)S(1)} %bitcast.6, f32[128,640]{1,0:T(8,128)S(1)} %join_planes.1.refs_0_, f32[128,640]{1,0:T(8,128)S(1)} %collective-permute-done.10.refs_1_, ...), custom_call_target="tpu_custom_call" | custom-call | bytes 3735564 | tf_op jit(solution)/shard_map/sweeps/pallas_call | solution.py:214
  100.7 4.0 %collective-permute-start.19 = (f32[128,128]{1,0:T(8,128)S(1)}, f32[128,128]{1,0:T(8,128)S(1)}, u32[]{:S(2)}, u32[]{:S(2)}) collective-permute-start(f32[128,128]{1,0:T(8,128)S(1)} %sweeps.1.own_ref), channel_id=1, source_target_pairs={{0,24},{8,16},{16,8},{24,0},{1,25},{9,17},{17,9},{25,1},{2,26},{10... | collective-permute-start | bytes 196616 | tf_op jit(solution)/shard_map/ppermute | solution.py:228
  104.7 0.6 collective-permute-start.17
  105.3 2.3 %collective-permute-done.19.refs_2_ = f32[128,128]{1,0:T(8,128)S(1)} collective-permute-done((f32[128,128]{1,0:T(8,128)S(1)}, f32[128,128]{1,0:T(8,128)S(1)}, u32[]{:S(2)}, u32[]{:S(2)}) %collective-permute-start.19) | collective-permute-done | bytes 65568 | tf_op jit(solution)/shard_map/ppermute | solution.py:228
  107.6 2.7 %collective-permute-done.18.refs_1_ = f32[128,128]{1,0:T(8,128)S(1)} collective-permute-done((f32[128,128]{1,0:T(8,128)S(1)}, f32[128,128]{1,0:T(8,128)S(1)}, u32[]{:S(2)}, u32[]{:S(2)}) %collective-permute-start.18) | collective-permute-done | bytes 65568 | tf_op jit(solution)/shard_map/ppermute | solution.py:228
  110.3 0.0 collective-permute-done.17.refs_0_
  110.4 2.3 %pair_gram.1 = f32[8,128]{1,0:T(8,128)S(1)} custom-call(s32[3]{0:T(128)S(1)} %pad_add_fusion.where_ref, f32[128,128]{1,0:T(8,128)S(1)} %sweeps.1.own_ref, f32[128,128]{1,0:T(8,128)S(1)} %collective-permute-done.17.refs_0_, f32[128,128]{1,0:T(8,128)S(1)} %collective-permute-done.18.refs_1_, f32[128,128]{1,0:T(8,128)S(1)} %collective-permute-done.19.refs_2_), custom_call_target="tpu_custom_call" | custom-call | bytes 266252 | tf_op jit(solution)/shard_map/pair_gram/pallas_call | solution.py:214
  112.7 1.2 collective-permute-done.20
  113.9 0.8 collective-permute-start.21
  114.7 2.8 %collective-permute-done.21 = f32[8,128]{1,0:T(8,128)S(1)} collective-permute-done((f32[8,128]{1,0:T(8,128)S(1)}, f32[8,128]{1,0:T(8,128)S(1)}, u32[]{:S(2)}, u32[]{:S(2)}) %collective-permute-start.21) | collective-permute-done | bytes 4128 | tf_op jit(solution)/shard_map/ppermute | solution.py:228
  117.5 1.1 collective-permute-start.22
  118.6 2.5 %collective-permute-done.22 = f32[8,128]{1,0:T(8,128)S(1)} collective-permute-done((f32[8,128]{1,0:T(8,128)S(1)}, f32[8,128]{1,0:T(8,128)S(1)}, u32[]{:S(2)}, u32[]{:S(2)}) %collective-permute-start.22) | collective-permute-done | bytes 4128 | tf_op jit(solution)/shard_map/ppermute | solution.py:228
  121.1 0.1 dynamic-slice_multiply_fusion
  121.2 0.7 copy.3
  (17 shorter events, 0.1 us)
Async XLA Ops:
  0.0 2.2 %collective-permute-start = (f32[128,1024]{1,0:T(8,128)}, f32[128,1024]{1,0:T(8,128)S(1)}, u32[]{:S(2)}, u32[]{:S(2)}) collective-permute-start(f32[128,1024]{1,0:T(8,128)} %bitcast.4), channel_id=1, source_target_pairs={{0,1},{1,0},{2,3},{3,2},{4,5},{5,4},{6,7},{7,6},{8,9},{9,8},{10,11... | collective-permute-start | bytes 1572872 | tf_op jit(solution)/shard_map/ppermute | solution.py:228
  2.2 1.0 copy-start
  4.8 11.4 %collective-permute-start.1 = (f32[128,640]{1,0:T(8,128)S(1)}, f32[128,640]{1,0:T(8,128)S(1)}, u32[]{:S(2)}, u32[]{:S(2)}) collective-permute-start(f32[128,640]{1,0:T(8,128)S(1)} %get-tuple-element.14), channel_id=1, source_target_pairs={{0,2},{1,3},{2,0},{3,1},{4,6},{5,7},{6,4},{7,5},{8,10},{9,11},{10,... | collective-permute-start | bytes 983048 | tf_op jit(solution)/shard_map/ppermute | solution.py:228
  7.8 16.5 %collective-permute-start.2 = (f32[128,640]{1,0:T(8,128)S(1)}, f32[128,640]{1,0:T(8,128)S(1)}, u32[]{:S(2)}, u32[]{:S(2)}) collective-permute-start(f32[128,640]{1,0:T(8,128)S(1)} %get-tuple-element.15), channel_id=1, source_target_pairs={{0,4},{1,5},{2,6},{3,7},{4,0},{5,1},{6,2},{7,3},{8,12},{9,13},{10,... | collective-permute-start | bytes 983048 | tf_op jit(solution)/shard_map/ppermute | solution.py:228
  9.3 15.0 %collective-permute-start.3 = (f32[128,640]{1,0:T(8,128)S(1)}, f32[128,640]{1,0:T(8,128)S(1)}, u32[]{:S(2)}, u32[]{:S(2)}) collective-permute-start(f32[128,640]{1,0:T(8,128)S(1)} %get-tuple-element.16), channel_id=1, source_target_pairs={{0,6},{1,7},{2,4},{3,5},{4,2},{5,3},{6,0},{7,1},{8,14},{9,15},{10,... | collective-permute-start | bytes 983048 | tf_op jit(solution)/shard_map/ppermute | solution.py:228
  24.9 5.3 %collective-permute-start.4 = (f32[32,640]{1,0:T(8,128)S(1)}, f32[32,640]{1,0:T(8,128)S(1)}, u32[]{:S(2)}, u32[]{:S(2)}) collective-permute-start(f32[32,640]{1,0:T(8,128)S(1)} %get-tuple-element.18), channel_id=1, source_target_pairs={{0,8},{8,0},{16,24},{24,16},{1,9},{9,1},{17,25},{25,17},{2,10},{10... | collective-permute-start | bytes 245768 | tf_op jit(solution)/shard_map/ppermute | solution.py:228
  26.5 7.6 %collective-permute-start.5 = (f32[32,640]{1,0:T(8,128)S(1)}, f32[32,640]{1,0:T(8,128)S(1)}, u32[]{:S(2)}, u32[]{:S(2)}) collective-permute-start(f32[32,640]{1,0:T(8,128)S(1)} %get-tuple-element.19), channel_id=1, source_target_pairs={{0,16},{8,24},{16,0},{24,8},{1,17},{9,25},{17,1},{25,9},{2,18},{10... | collective-permute-start | bytes 245768 | tf_op jit(solution)/shard_map/ppermute | solution.py:228
  29.1 6.3 %collective-permute-start.6 = (f32[32,640]{1,0:T(8,128)S(1)}, f32[32,640]{1,0:T(8,128)S(1)}, u32[]{:S(2)}, u32[]{:S(2)}) collective-permute-start(f32[32,640]{1,0:T(8,128)S(1)} %get-tuple-element.20), channel_id=1, source_target_pairs={{0,24},{8,16},{16,8},{24,0},{1,25},{9,17},{17,9},{25,1},{2,26},{10... | collective-permute-start | bytes 245768 | tf_op jit(solution)/shard_map/ppermute | solution.py:228
  35.5 23.5 %copy-start.2 = (f32[1024,128]{1,0:T(8,128)S(1)}, f32[1024,128]{1,0:T(8,128)}, u32[]{:S(2)}) copy-start(f32[1024,128]{1,0:T(8,128)} %start_ref.1) | copy-start | bytes 1572868
  35.5 6.4 %collective-permute-start.9 = (f32[32,640]{1,0:T(8,128)S(1)}, f32[32,640]{1,0:T(8,128)S(1)}, u32[]{:S(2)}, u32[]{:S(2)}) collective-permute-start(f32[32,640]{1,0:T(8,128)S(1)} %sum_planes.1.refs_0_), channel_id=1, source_target_pairs={{0,24},{8,16},{16,8},{24,0},{1,25},{9,17},{17,9},{25,1},{2,26},{10... | collective-permute-start | bytes 245768 | tf_op jit(solution)/shard_map/ppermute | solution.py:228
  37.5 6.2 %collective-permute-start.8 = (f32[32,640]{1,0:T(8,128)S(1)}, f32[32,640]{1,0:T(8,128)S(1)}, u32[]{:S(2)}, u32[]{:S(2)}) collective-permute-start(f32[32,640]{1,0:T(8,128)S(1)} %sum_planes.1.refs_0_), channel_id=1, source_target_pairs={{0,16},{8,24},{16,0},{24,8},{1,17},{9,25},{17,1},{25,9},{2,18},{10... | collective-permute-start | bytes 245768 | tf_op jit(solution)/shard_map/ppermute | solution.py:228
  38.0 5.8 %collective-permute-start.7 = (f32[32,640]{1,0:T(8,128)S(1)}, f32[32,640]{1,0:T(8,128)S(1)}, u32[]{:S(2)}, u32[]{:S(2)}) collective-permute-start(f32[32,640]{1,0:T(8,128)S(1)} %sum_planes.1.refs_0_), channel_id=1, source_target_pairs={{0,8},{8,0},{16,24},{24,16},{1,9},{9,1},{17,25},{25,17},{2,10},{10... | collective-permute-start | bytes 245768 | tf_op jit(solution)/shard_map/ppermute | solution.py:228
  44.3 21.9 %copy-start.1 = (f32[8,16,1024]{2,1,0:T(8,128)S(1)}, f32[8,16,1024]{2,1,0:T(8,128)}, u32[]{:S(2)}) copy-start(f32[8,16,1024]{2,1,0:T(8,128)} %param.2) | copy-start | bytes 1572868
  44.3 10.7 %collective-permute-start.12 = (f32[128,640]{1,0:T(8,128)S(1)}, f32[128,640]{1,0:T(8,128)S(1)}, u32[]{:S(2)}, u32[]{:S(2)}) collective-permute-start(f32[128,640]{1,0:T(8,128)S(1)} %join_planes.1.refs_0_), channel_id=1, source_target_pairs={{0,6},{1,7},{2,4},{3,5},{4,2},{5,3},{6,0},{7,1},{8,14},{9,15},{10,... | collective-permute-start | bytes 983048 | tf_op jit(solution)/shard_map/ppermute | solution.py:228
  45.9 12.5 %collective-permute-start.11 = (f32[128,640]{1,0:T(8,128)S(1)}, f32[128,640]{1,0:T(8,128)S(1)}, u32[]{:S(2)}, u32[]{:S(2)}) collective-permute-start(f32[128,640]{1,0:T(8,128)S(1)} %join_planes.1.refs_0_), channel_id=1, source_target_pairs={{0,4},{1,5},{2,6},{3,7},{4,0},{5,1},{6,2},{7,3},{8,12},{9,13},{10,... | collective-permute-start | bytes 983048 | tf_op jit(solution)/shard_map/ppermute | solution.py:228
  47.4 11.5 %collective-permute-start.10 = (f32[128,640]{1,0:T(8,128)S(1)}, f32[128,640]{1,0:T(8,128)S(1)}, u32[]{:S(2)}, u32[]{:S(2)}) collective-permute-start(f32[128,640]{1,0:T(8,128)S(1)} %join_planes.1.refs_0_), channel_id=1, source_target_pairs={{0,2},{1,3},{2,0},{3,1},{4,6},{5,7},{6,4},{7,5},{8,10},{9,11},{10,... | collective-permute-start | bytes 983048 | tf_op jit(solution)/shard_map/ppermute | solution.py:228
  47.9 18.2 %collective-permute-start.13 = (f32[128,640]{1,0:T(8,128)S(1)}, f32[128,640]{1,0:T(8,128)S(1)}, u32[]{:S(2)}, u32[]{:S(2)}) collective-permute-start(f32[128,640]{1,0:T(8,128)S(1)} %join_planes.1.refs_0_), channel_id=1, source_target_pairs={{0,1},{1,0},{2,3},{3,2},{4,5},{5,4},{6,7},{7,6},{8,9},{9,8},{10,11... | collective-permute-start | bytes 983048 | tf_op jit(solution)/shard_map/ppermute | solution.py:228
  55.0 11.1 %collective-permute-start.16 = (f32[128,640]{1,0:T(8,128)S(1)}, f32[128,640]{1,0:T(8,128)S(1)}, u32[]{:S(2)}, u32[]{:S(2)}) collective-permute-start(f32[128,640]{1,0:T(8,128)S(1)} %collective-permute-done.12.refs_3_), channel_id=1, source_target_pairs={{0,1},{1,0},{2,3},{3,2},{4,5},{5,4},{6,7},{7,6},{8,9},{9,8},{10,11... | collective-permute-start | bytes 983048 | tf_op jit(solution)/shard_map/ppermute | solution.py:228
  58.4 7.8 %collective-permute-start.15 = (f32[128,640]{1,0:T(8,128)S(1)}, f32[128,640]{1,0:T(8,128)S(1)}, u32[]{:S(2)}, u32[]{:S(2)}) collective-permute-start(f32[128,640]{1,0:T(8,128)S(1)} %collective-permute-done.11.refs_2_), channel_id=1, source_target_pairs={{0,1},{1,0},{2,3},{3,2},{4,5},{5,4},{6,7},{7,6},{8,9},{9,8},{10,11... | collective-permute-start | bytes 983048 | tf_op jit(solution)/shard_map/ppermute | solution.py:228
  58.9 7.2 %collective-permute-start.14 = (f32[128,640]{1,0:T(8,128)S(1)}, f32[128,640]{1,0:T(8,128)S(1)}, u32[]{:S(2)}, u32[]{:S(2)}) collective-permute-start(f32[128,640]{1,0:T(8,128)S(1)} %collective-permute-done.10.refs_1_), channel_id=1, source_target_pairs={{0,1},{1,0},{2,3},{3,2},{4,5},{5,4},{6,7},{7,6},{8,9},{9,8},{10,11... | collective-permute-start | bytes 983048 | tf_op jit(solution)/shard_map/ppermute | solution.py:228
  100.7 6.9 %collective-permute-start.19 = (f32[128,128]{1,0:T(8,128)S(1)}, f32[128,128]{1,0:T(8,128)S(1)}, u32[]{:S(2)}, u32[]{:S(2)}) collective-permute-start(f32[128,128]{1,0:T(8,128)S(1)} %sweeps.1.own_ref), channel_id=1, source_target_pairs={{0,24},{8,16},{16,8},{24,0},{1,25},{9,17},{17,9},{25,1},{2,26},{10... | collective-permute-start | bytes 196616 | tf_op jit(solution)/shard_map/ppermute | solution.py:228
  104.7 5.7 %collective-permute-start.18 = (f32[128,128]{1,0:T(8,128)S(1)}, f32[128,128]{1,0:T(8,128)S(1)}, u32[]{:S(2)}, u32[]{:S(2)}) collective-permute-start(f32[128,128]{1,0:T(8,128)S(1)} %sweeps.1.own_ref), channel_id=1, source_target_pairs={{0,16},{8,24},{16,0},{24,8},{1,17},{9,25},{17,1},{25,9},{2,18},{10... | collective-permute-start | bytes 196616 | tf_op jit(solution)/shard_map/ppermute | solution.py:228
  104.7 5.7 %collective-permute-start.17 = (f32[128,128]{1,0:T(8,128)S(1)}, f32[128,128]{1,0:T(8,128)S(1)}, u32[]{:S(2)}, u32[]{:S(2)}) collective-permute-start(f32[128,128]{1,0:T(8,128)S(1)} %sweeps.1.own_ref), channel_id=1, source_target_pairs={{0,8},{8,0},{16,24},{24,16},{1,9},{9,1},{17,25},{25,17},{2,10},{10... | collective-permute-start | bytes 196616 | tf_op jit(solution)/shard_map/ppermute | solution.py:228
  112.7 1.2 collective-permute-start.20
  113.9 3.6 %collective-permute-start.21 = (f32[8,128]{1,0:T(8,128)S(1)}, f32[8,128]{1,0:T(8,128)S(1)}, u32[]{:S(2)}, u32[]{:S(2)}) collective-permute-start(f32[8,128]{1,0:T(8,128)S(1)} %add.18), channel_id=1, source_target_pairs={{0,2},{1,3},{2,0},{3,1},{4,6},{5,7},{6,4},{7,5},{8,10},{9,11},{10,... | collective-permute-start | bytes 12296 | tf_op jit(solution)/shard_map/ppermute | solution.py:228
  117.5 3.6 %collective-permute-start.22 = (f32[8,128]{1,0:T(8,128)S(1)}, f32[8,128]{1,0:T(8,128)S(1)}, u32[]{:S(2)}, u32[]{:S(2)}) collective-permute-start(f32[8,128]{1,0:T(8,128)S(1)} %add.19), channel_id=1, source_target_pairs={{0,4},{1,5},{2,6},{3,7},{4,0},{5,1},{6,2},{7,3},{8,12},{9,13},{10,... | collective-permute-start | bytes 12296 | tf_op jit(solution)/shard_map/ppermute | solution.py:228
where the time goes:
time: 122 us
  waiting for transfers between devices  49.1 us (40%)
  Pallas kernels  46.8 us (38%)
  starting transfers between devices  24 us (20%)
  local copies, waits for them, and re-layouts  1.71 us (1%)
    ppermute x23, waiting for transfers between devices, swap(): lax.ppermute(array, axis, [(i, i ^ mask) for i in range(lax.axis_size(axi...  49.1 us
    pallas_call x7, Pallas kernels, call(): pl.pallas_call(kernel, out_shape=shapes, in_specs=[SCALARS] * scalars + [...  46.8 us
    ppermute x23, starting transfers between devices, swap(): lax.ppermute(array, axis, [(i, i ^ mask) for i in range(lax.axis_size(axi...  24 us
  transfers between devices with their start and end apart: 23, of which 16 were waited for; matrix products, arithmetic and copies ran while one was open for 0% of the time, Pallas kernels for 6%

commit v1 on v0

v1 whole, which is shorter than its diff:
```python
import functools
import jax
import jax.numpy as jnp
from jax import lax
from jax.experimental import pallas as pl
from jax.experimental.pallas import tpu as pltpu
from jax.sharding import PartitionSpec as P

ITERS = 4
BLOCK = 128
PANEL = 8
HIGHEST = lax.Precision.HIGHEST
NN = (((1,), (0,)), ((), ()))
NT = (((1,), (1,)), ((), ()))
SCALARS = pl.BlockSpec(memory_space=pltpu.SMEM)
VMEM = pl.BlockSpec(memory_space=pltpu.VMEM)


def split(values):
    high = values.astype(jnp.bfloat16)
    return high, (values - high.astype(jnp.float32)).astype(jnp.bfloat16)


def dot_bf16(left, right, dims):
    return lax.dot_general(left, right, dims, preferred_element_type=jnp.float32)


def dot_split(left, right, dims):
    (left_high, left_low), (right_high, right_low) = left, right
    return (
        dot_bf16(left_high, right_high, dims)
        + (dot_bf16(left_low, right_high, dims) + dot_bf16(left_high, right_low, dims))
    )


def dot_full(left, right, dims):
    return lax.dot_general(left, right, dims, precision=HIGHEST, preferred_element_type=jnp.float32)


def add_pairs(terms):
    terms = list(terms)
    while len(terms) > 1:
        pairs = [terms[i] + terms[i + 1] for i in range(0, len(terms) - 1, 2)]
        terms = pairs + terms[2 * len(pairs) :]
    return terms[0]


def inverse_factor(matrix, out_ref, scratch):
    order = matrix.shape[0]
    panels = order // PANEL
    tiles = [matrix[PANEL * i : PANEL * (i + 1), :] for i in range(panels)]
    lane = lax.broadcasted_iota(jnp.int32, (PANEL, order), 1)

    def full(part):
        return jnp.broadcast_to(part, (PANEL, order))

    for p in range(panels):
        tile, start = tiles[p], PANEL * p
        base = PANEL * PANEL * (p % 2)
        inside = (lane >= start) & (lane < start + PANEL)
        for c in range(PANEL):
            scratch[base + PANEL * c : base + PANEL * (c + 1), :] = full(tile[:, start + c : start + c + 1])
        pivot = {
            (r, c): full(scratch[base + PANEL * c + r : base + PANEL * c + r + 1, :])
            for c in range(PANEL)
            for r in range(c, PANEL)
        }
        rows = [
            jnp.where(inside, jnp.where(lane == start + c, 1.0, 0.0), full(tile[c : c + 1, :]))
            for c in range(PANEL)
        ]
        reciprocal, inverse = {}, {}
        for c in range(PANEL):
            reciprocal[c] = 1.0 / pivot[c, c]
            lower = {r: pivot[r, c] * reciprocal[c] for r in range(c + 1, PANEL)}
            for d in range(c + 1, PANEL):
                for r in range(d, PANEL):
                    if r == c + 1:
                        pivot[r, d] = pivot[r, d] - (pivot[r, c] * pivot[d, c]) * reciprocal[c]
                    else:
                        pivot[r, d] = pivot[r, d] - lower[r] * pivot[d, c]
            for r in range(c + 1, PANEL):
                rows[r] = rows[r] - lower[r] * rows[c]
                for k in range(c):
                    inverse[r, k] = inverse[r, k] - lower[r] * inverse[c, k]
                inverse[r, c] = -lower[r]
        for r in range(PANEL):
            done = jnp.where(lane < start + PANEL, rows[r], 0.0) * lax.rsqrt(pivot[r, r])
            out_ref[start + r : start + r + 1, :] = done[0:1, :]
        if p == panels - 1:
            break
        scaled = [rows[r] * reciprocal[r] for r in range(PANEL)]
        eliminate = []
        for c in range(PANEL):
            total = scaled[c]
            for r in range(c + 1, PANEL):
                total = total + inverse[r, c] * scaled[r]
            eliminate.append(total)
        for i in range(p + 1, panels):
            steps = [full(tiles[i][:, start + c : start + c + 1]) * eliminate[c] for c in range(PANEL)]
            tiles[i] = jnp.where(inside, 0.0, tiles[i]) - add_pairs(steps)


def start_kernel(after_ref, start_ref, out_ref, factor_ref, spread_ref):
    del after_ref
    rows = start_ref[...].T
    inverse_factor(dot_full(rows, rows, NT), factor_ref, spread_ref)
    out_ref[...] = dot_full(factor_ref[...], rows, NN)


def split_kernel(rows_ref, high_ref, low_ref):
    order = rows_ref.shape[1]
    extra = high_ref.shape[1] - order
    for target, values in zip((high_ref, low_ref), split(rows_ref[...])):
        target[:, 0:order] = values
        target[:, order : order + extra] = values[:, :extra]


def gram_kernel(where_ref, own_high, own_low, other_ref, *refs):
    outs, (high_ref, low_ref) = refs[:-2], refs[-2:]
    band = outs[0].shape[1]
    rows, order = other_ref.shape
    extra = high_ref.shape[1] - order
    for own, target, values in zip((own_high, own_low), (high_ref, low_ref), split(other_ref[...])):
        target[0:rows, :] = own[...]
        target[rows : 2 * rows, 0:order] = values
        target[rows : 2 * rows, order : order + extra] = values[:, :extra]
    group, core = where_ref[0], where_ref[1]
    for k, out in enumerate(outs):
        first = pl.multiple_of((2 * jnp.bitwise_xor(group, k) + core) * BLOCK, BLOCK)
        left = [ref[:, pl.ds(first, BLOCK)].astype(jnp.float32).T.astype(jnp.bfloat16) for ref in (high_ref, low_ref)]
        right = [ref[:, pl.ds(first, band)] for ref in (high_ref, low_ref)]
        out[...] = dot_split(left, right, NN)


def cut_kernel(count, where_ref, after_ref, *refs):
    del after_ref
    terms, outs = refs[: len(refs) - count], refs[len(refs) - count :]
    rows = outs[0].shape[0]
    plane = where_ref[2]
    for k, out in enumerate(outs):
        piece = pl.ds(pl.multiple_of(jnp.bitwise_xor(plane, k) * rows, rows), rows)
        total = terms[0][piece, :]
        for term in terms[1:]:
            total = total + term[piece, :]
        out[...] = total


def add_kernel(*refs):
    total = refs[0][...]
    for term in refs[1:-1]:
        total = total + term[...]
    refs[-1][...] = total


def join_kernel(where_ref, *refs):
    pieces, out = refs[:-1], refs[-1]
    rows = pieces[0].shape[0]
    plane = where_ref[2]
    for k, piece in enumerate(pieces):
        out[pl.ds(pl.multiple_of(jnp.bitwise_xor(plane, k) * rows, rows), rows), :] = piece[...]


def sweeps_and_core(basis_ref, field_ref, core_ref, last_ref, high_ref, low_ref, factor_ref, spread_ref, image_ref):
    def times_gram(rows):
        return dot_split(split(rows), (high_ref[...], low_ref[...]), NN)

    def body(step, carry):
        image = image_ref[...]
        halves = split(image)
        inner = dot_split(halves, halves, NT)
        following = times_gram(image)
        inverse_factor(inner, factor_ref, spread_ref)
        image_ref[...] = dot_split(split(factor_ref[...]), split(following), NN)
        return carry

    image_ref[...] = times_gram(basis_ref[...])
    lax.fori_loop(0, ITERS - 1, body, 0)
    image = image_ref[...]
    last_ref[...] = dot_full(image, image, NT)
    core_ref[...] = dot_full(field_ref[...], image, NT)


def last_kernel(matrix_ref, out_ref, spread_ref):
    inverse_factor(matrix_ref[...], out_ref, spread_ref)


def banded_kernel(blocks, where_ref, basis_ref, field_ref, *refs):
    bands, rest = refs[:-7], refs[-7:]
    high_ref, low_ref = rest[2:4]
    group, core = where_ref[0], where_ref[1]
    half = len(bands) // 2
    for place, band in enumerate(bands):
        side = core if place < half else 1 - core
        row = 2 * jnp.bitwise_xor(group, place % half) + side
        rows = pl.ds(pl.multiple_of(row * BLOCK, BLOCK), BLOCK)
        for k in range(blocks // 2 + 1):
            column = lax.rem(row + k, blocks)
            columns = pl.ds(pl.multiple_of(column * BLOCK, BLOCK), BLOCK)
            part = band[:, BLOCK * k : BLOCK * (k + 1)]
            high_ref[rows, columns], low_ref[rows, columns] = split(part)
            if 0 < k < blocks // 2:
                high_ref[columns, rows], low_ref[columns, rows] = split(part.T)
    sweeps_and_core(basis_ref, field_ref, *rest)


def whole_kernel(basis_ref, field_ref, gram_ref, *rest):
    rest[2][...], rest[3][...] = split(gram_ref[...])
    sweeps_and_core(basis_ref, field_ref, *rest)


def pair_kernel(cells_three, where_ref, factor_ref, *refs):
    images, out_ref = refs[:-1], refs[-1]
    size = images[0].shape[0]
    cells_two = size // cells_three
    cores = [dot_full(image[...], factor_ref[...], NT) for image in images]
    row = lax.broadcasted_iota(jnp.int32, (size, size), 0)
    column = lax.broadcasted_iota(jnp.int32, (size, size), 1)
    same = lax.rem(row, cells_three) == lax.rem(column, cells_three)
    width = out_ref.shape[1]
    target = lax.broadcasted_iota(jnp.int32, (size, width), 1)
    source = lax.broadcasted_iota(jnp.int32, (size, width), 0) // cells_three
    plane = where_ref[2]
    total = jnp.zeros(out_ref.shape, jnp.float32)
    for k, core in enumerate(cores):
        product = jnp.where(same, dot_full(cores[0], core, NT), 0.0)
        summed = jnp.sum(product.reshape(cells_two, cells_three, size), axis=1)
        place = jnp.where(target == source + jnp.bitwise_xor(plane, k) * cells_two, 1.0, 0.0)
        total = total + dot_full(summed, place, NN)
    out_ref[...] = total


def call(kernel, outs, name, operands, scratch=(), scalars=0, order_only=(), flops=0, dtype=jnp.float32):
    shapes = [jax.ShapeDtypeStruct(shape, dtype) for shape in outs]
    touched = sum(operand.size for operand in operands) + sum(shape.size for shape in shapes)
    result = pl.pallas_call(
        kernel,
        out_shape=shapes,
        in_specs=[SCALARS] * scalars
        + [pl.BlockSpec(memory_space=pl.ANY)] * len(order_only)
        + [VMEM] * (len(operands) - scalars),
        out_specs=[VMEM] * len(shapes),
        scratch_shapes=list(scratch),
        compiler_params=pltpu.CompilerParams(vmem_limit_bytes=32 * 2**20),
        cost_estimate=pl.CostEstimate(flops=flops, bytes_accessed=4 * touched, transcendentals=0),
        name=name,
    )(*operands[:scalars], *order_only, *operands[scalars:])
    return result if len(outs) > 1 else result[0]


def swap(array, axis, mask):
    return lax.ppermute(array, axis, [(i, i ^ mask) for i in range(lax.axis_size(axis))])


def shards(field, start_block):
    cells_two, cells_three, order = field.shape
    rank = start_block.shape[1]
    narrow, wide = lax.axis_size("narrow"), lax.axis_size("wide")
    unfolded = field.reshape(cells_two * cells_three, order)
    cells = unfolded.shape[0]
    place, plane = lax.axis_index("wide"), lax.axis_index("narrow")
    where = jnp.stack([place // 2, place % 2, plane]).astype(jnp.int32)
    spread = pltpu.VMEM((2 * PANEL * PANEL, rank), jnp.float32)

    def orthonormal_start(after):
        return call(
            start_kernel,
            [(rank, order)],
            "orth_start",
            [start_block],
            [pltpu.VMEM((rank, rank), jnp.float32), spread],
            order_only=[after],
            flops=10**9,
        )

    scratch = [
        pltpu.VMEM((order, order), jnp.bfloat16),
        pltpu.VMEM((order, order), jnp.bfloat16),
        pltpu.VMEM((rank, rank), jnp.float32),
        spread,
        pltpu.VMEM((rank, order), jnp.float32),
    ]
    results = [(cells, rank), (rank, rank)]
    blocks = order // BLOCK
    if wide == blocks and narrow & (narrow - 1) == 0 and BLOCK % (8 * narrow) == 0:
        groups = wide // 2
        band = BLOCK * (blocks // 2 + 1)
        extended = (cells, order + band - BLOCK)
        other = swap(unfolded, "wide", 1)
        own = call(split_kernel, [extended] * 2, "split_field", [unfolded], dtype=jnp.bfloat16)
        parts = call(
            gram_kernel,
            [(BLOCK, band)] * groups,
            "gram_band",
            [where, *own, other],
            [pltpu.VMEM((2 * cells, extended[1]), jnp.bfloat16)] * 2,
            scalars=1,
        )
        arrived = [swap(parts[k], "wide", 2 * k) for k in range(1, groups)]
        basis = orthonormal_start(parts[0])
        cuts = call(
            functools.partial(cut_kernel, narrow),
            [(BLOCK // narrow, band)] * narrow,
            "sum_groups",
            [where, parts[0], *arrived],
            scalars=1,
            order_only=[basis],
        )
        arrived = [swap(cuts[k], "narrow", k) for k in range(1, narrow)]
        piece = call(add_kernel, [(BLOCK // narrow, band)], "sum_planes", [cuts[0], *arrived])
        arrived = [swap(piece, "narrow", k) for k in range(1, narrow)]
        joined = call(join_kernel, [(BLOCK, band)], "join_planes", [where, piece, *arrived], scalars=1)
        bands = [joined] + [swap(joined, "wide", 2 * k) for k in range(1, groups)]
        bands = bands + [swap(part, "wide", 1) for part in bands]
        image, inner = call(
            functools.partial(banded_kernel, blocks),
            results,
            "sweeps",
            [where, basis, unfolded, *bands],
            scratch,
            scalars=1,
        )
    else:
        basis = orthonormal_start(start_block)
        gram = lax.dot_general(unfolded, unfolded, (((0,), (0,)), ((), ())), precision=HIGHEST)
        gram = lax.psum(gram, ("narrow", "wide"))
        image, inner = call(whole_kernel, results, "sweeps", [basis, unfolded, gram], scratch)
    factor = call(last_kernel, [(rank, rank)], "last_factor", [inner], [spread], flops=10**9)
    if narrow & (narrow - 1) == 0 and wide & (wide - 1) == 0:
        images = [image] + [swap(image, "narrow", k) for k in range(1, narrow)]
        width = -(-narrow * cells_two // BLOCK) * BLOCK
        total = call(
            functools.partial(pair_kernel, cells_three),
            [(cells_two, width)],
            "pair_gram",
            [where, factor, *images],
            scalars=1,
        )
        mask = 1
        while mask < wide:
            total = total + swap(total, "wide", mask)
            mask *= 2
        columns = narrow * cells_two // wide
        finished = lax.dynamic_slice_in_dim(total, place * columns, columns, 1)
    else:
        core = lax.dot_general(image, factor, NT, precision=HIGHEST)
        merged = core.reshape(cells_two, cells_three * rank)
        everyone = lax.all_gather(merged, "narrow", axis=0, tiled=True)
        part = lax.dot_general(merged, everyone, NT, precision=HIGHEST)
        finished = lax.psum_scatter(part, "wide", scatter_dimension=1, tiled=True)
    return finished / (rank * cells_three * wide)


def solution(mesh):
    return jax.shard_map(
        shards,
        mesh=mesh,
        in_specs=(P("narrow", "wide", None), P()),
        out_specs=P("narrow", "wide"),
        check_vma=False,
    )
```

time: 122 us -> 97.9 us (0.80)
  Pallas kernels: 46.8 us -> 30.6 us
  waiting for transfers between devices: 49.1 us -> 41 us
    pallas_call x7 -> x9, Pallas kernels: 46.8 us -> 30.6 us  [call(): pl.pallas_call(kernel, out_shape=shapes, in_specs=[SCALARS] * scalars + [...]
    ppermute x23, waiting for transfers between devices: 49.1 us -> 41 us  [swap(): lax.ppermute(array, axis, [(i, i ^ mask) for i in range(lax.axis_size(axi...]
  transfers between devices with their start and end apart: 23 -> 23, of which waited for: 16 -> 18; matrix products, arithmetic and copies ran while one was open for 0% -> 0% of each run, Pallas kernels for 6% -> 9%
where the time goes in v1:
time: 97.9 us; the launch traced here: 97.7 us
  waiting for transfers between devices  41 us (42%)
  Pallas kernels  30.6 us (31%)
  starting transfers between devices  24.1 us (25%)
  local copies, waits for them, and re-layouts  1.7 us (2%)
    ppermute x23, waiting for transfers between devices, swap(): lax.ppermute(array, axis, [(i, i ^ mask) for i in range(lax.axis_size(axi...  41 us
    pallas_call x9, Pallas kernels, call(): pl.pallas_call(kernel, out_shape=shapes, in_specs=[SCALARS] * scalars + [...  30.6 us
    ppermute x23, starting transfers between devices, swap(): lax.ppermute(array, axis, [(i, i ^ mask) for i in range(lax.axis_size(axi...  24.1 us
  transfers between devices with their start and end apart: 23, of which 18 were waited for; matrix products, arithmetic and copies ran while one was open for 0% of the time, Pallas kernels for 9%

profile of v1, /device:TPU:0, one launch (start us, length us, event | category | flops | bytes accessed | tf_op | source)
XLA Modules:
  0.0 97.7 jit_solution(10851936867691162600)
XLA Ops:
  0.0 0.5 collective-permute-start
  0.5 1.0 %copy-done = f32[8,16,1024]{2,1,0:T(8,128)S(1)} copy-done((f32[8,16,1024]{2,1,0:T(8,128)S(1)}, f32[8,16,1024]{2,1,0:T(8,128)}, u32[]{:S(2)}) %copy-start) | copy-done | bytes 524312
  1.5 0.1 split_field.1
  1.6 0.1 pad_add_fusion.where_ref
  1.7 0.5 collective-permute-done.other_ref
  2.2 1.5 %gram_band.1 = (f32[128,640]{1,0:T(8,128)S(1)}, f32[128,640]{1,0:T(8,128)S(1)}, f32[128,640]{1,0:T(8,128)S(1)}, f32[128,640]{1,0:T(8,128)S(1)}) custom-call(s32[3]{0:T(128)S(1)} %pad_add_fusion.where_ref, bf16[128,1536]{1,0:T(8,128)(2,1)S(1)} %get-tuple-element.17.own_high, bf16[128,1536]{1,0:T(8,128)(2,1)S(1)} %get-tuple-element.18.own_low, ...), custom_call_target="tpu_custom_call" | custom-call | bytes 3407884 | tf_op jit(solution)/shard_map/gram_band/pallas_call | solution.py:236
  3.7 2.9 %collective-permute-start.1 = (f32[128,640]{1,0:T(8,128)S(1)}, f32[128,640]{1,0:T(8,128)S(1)}, u32[]{:S(2)}, u32[]{:S(2)}) collective-permute-start(f32[128,640]{1,0:T(8,128)S(1)} %get-tuple-element.20), channel_id=1, source_target_pairs={{0,2},{1,3},{2,0},{3,1},{4,6},{5,7},{6,4},{7,5},{8,10},{9,11},{10,... | collective-permute-start | bytes 983048 | tf_op jit(solution)/shard_map/ppermute | solution.py:252
  6.6 1.5 %collective-permute-start.2 = (f32[128,640]{1,0:T(8,128)S(1)}, f32[128,640]{1,0:T(8,128)S(1)}, u32[]{:S(2)}, u32[]{:S(2)}) collective-permute-start(f32[128,640]{1,0:T(8,128)S(1)} %get-tuple-element.21), channel_id=1, source_target_pairs={{0,4},{1,5},{2,6},{3,7},{4,0},{5,1},{6,2},{7,3},{8,12},{9,13},{10,... | collective-permute-start | bytes 983048 | tf_op jit(solution)/shard_map/ppermute | solution.py:252
  8.2 0.0 collective-permute-start.3
  8.2 5.1 %orth_start.1.after_ref.basis_ref = f32[128,1024]{1,0:T(8,128)S(1)} custom-call(f32[128,640]{1,0:T(8,128)S(1)} %get-tuple-element.19.after_ref.refs_0_, f32[1024,128]{1,0:T(8,128)S(1)} %copy-done.2), custom_call_target="tpu_custom_call" | custom-call | flops 1000000000 | bytes 1048576 | tf_op jit(solution)/shard_map/orth_start/pallas_call | solution.py:236
  13.3 1.9 %collective-permute-done.1.refs_1_ = f32[128,640]{1,0:T(8,128)S(1)} collective-permute-done((f32[128,640]{1,0:T(8,128)S(1)}, f32[128,640]{1,0:T(8,128)S(1)}, u32[]{:S(2)}, u32[]{:S(2)}) %collective-permute-start.1) | collective-permute-done | bytes 327712 | tf_op jit(solution)/shard_map/ppermute | solution.py:252
  15.1 8.0 %collective-permute-done.2.refs_2_ = f32[128,640]{1,0:T(8,128)S(1)} collective-permute-done((f32[128,640]{1,0:T(8,128)S(1)}, f32[128,640]{1,0:T(8,128)S(1)}, u32[]{:S(2)}, u32[]{:S(2)}) %collective-permute-start.2) | collective-permute-done | bytes 327712 | tf_op jit(solution)/shard_map/ppermute | solution.py:252
  23.1 0.6 sum_groups.1
  23.8 1.6 %collective-permute-start.4 = (f32[32,640]{1,0:T(8,128)S(1)}, f32[32,640]{1,0:T(8,128)S(1)}, u32[]{:S(2)}, u32[]{:S(2)}) collective-permute-start(f32[32,640]{1,0:T(8,128)S(1)} %get-tuple-element.24), channel_id=1, source_target_pairs={{0,8},{8,0},{16,24},{24,16},{1,9},{9,1},{17,25},{25,17},{2,10},{10... | collective-permute-start | bytes 245768 | tf_op jit(solution)/shard_map/ppermute | solution.py:252
  25.4 2.6 %collective-permute-start.5 = (f32[32,640]{1,0:T(8,128)S(1)}, f32[32,640]{1,0:T(8,128)S(1)}, u32[]{:S(2)}, u32[]{:S(2)}) collective-permute-start(f32[32,640]{1,0:T(8,128)S(1)} %get-tuple-element.25), channel_id=1, source_target_pairs={{0,16},{8,24},{16,0},{24,8},{1,17},{9,25},{17,1},{25,9},{2,18},{10... | collective-permute-start | bytes 245768 | tf_op jit(solution)/shard_map/ppermute | solution.py:252
  28.0 0.2 collective-permute-start.6
  28.2 0.9 collective-permute-done.4.refs_1_
  29.1 3.9 %collective-permute-done.5.refs_2_ = f32[32,640]{1,0:T(8,128)S(1)} collective-permute-done((f32[32,640]{1,0:T(8,128)S(1)}, f32[32,640]{1,0:T(8,128)S(1)}, u32[]{:S(2)}, u32[]{:S(2)}) %collective-permute-start.5) | collective-permute-done | bytes 81952 | tf_op jit(solution)/shard_map/ppermute | solution.py:252
  33.0 1.4 %collective-permute-done.6.refs_3_ = f32[32,640]{1,0:T(8,128)S(1)} collective-permute-done((f32[32,640]{1,0:T(8,128)S(1)}, f32[32,640]{1,0:T(8,128)S(1)}, u32[]{:S(2)}, u32[]{:S(2)}) %collective-permute-start.6) | collective-permute-done | bytes 81952 | tf_op jit(solution)/shard_map/ppermute | solution.py:252
  34.4 2.0 %collective-permute-start.9 = (f32[32,640]{1,0:T(8,128)S(1)}, f32[32,640]{1,0:T(8,128)S(1)}, u32[]{:S(2)}, u32[]{:S(2)}) collective-permute-start(f32[32,640]{1,0:T(8,128)S(1)} %sum_planes.1.refs_0_), channel_id=1, source_target_pairs={{0,24},{8,16},{16,8},{24,0},{1,25},{9,17},{17,9},{25,1},{2,26},{10... | collective-permute-start | bytes 245768 | tf_op jit(solution)/shard_map/ppermute | solution.py:252
  36.4 0.4 collective-permute-start.8
  36.8 2.0 %collective-permute-start.7 = (f32[32,640]{1,0:T(8,128)S(1)}, f32[32,640]{1,0:T(8,128)S(1)}, u32[]{:S(2)}, u32[]{:S(2)}) collective-permute-start(f32[32,640]{1,0:T(8,128)S(1)} %sum_planes.1.refs_0_), channel_id=1, source_target_pairs={{0,8},{8,0},{16,24},{24,16},{1,9},{9,1},{17,25},{25,17},{2,10},{10... | collective-permute-start | bytes 245768 | tf_op jit(solution)/shard_map/ppermute | solution.py:252
  38.8 2.0 %collective-permute-done.9.refs_3_ = f32[32,640]{1,0:T(8,128)S(1)} collective-permute-done((f32[32,640]{1,0:T(8,128)S(1)}, f32[32,640]{1,0:T(8,128)S(1)}, u32[]{:S(2)}, u32[]{:S(2)}) %collective-permute-start.9) | collective-permute-done | bytes 81952 | tf_op jit(solution)/shard_map/ppermute | solution.py:252
  40.8 1.8 %collective-permute-done.8.refs_2_ = f32[32,640]{1,0:T(8,128)S(1)} collective-permute-done((f32[32,640]{1,0:T(8,128)S(1)}, f32[32,640]{1,0:T(8,128)S(1)}, u32[]{:S(2)}, u32[]{:S(2)}) %collective-permute-start.8) | collective-permute-done | bytes 81952 | tf_op jit(solution)/shard_map/ppermute | solution.py:252
  42.6 0.6 join_planes.1.refs_0_
  43.2 1.5 %collective-permute-start.12 = (f32[128,640]{1,0:T(8,128)S(1)}, f32[128,640]{1,0:T(8,128)S(1)}, u32[]{:S(2)}, u32[]{:S(2)}) collective-permute-start(f32[128,640]{1,0:T(8,128)S(1)} %join_planes.1.refs_0_), channel_id=1, source_target_pairs={{0,6},{1,7},{2,4},{3,5},{4,2},{5,3},{6,0},{7,1},{8,14},{9,15},{10,... | collective-permute-start | bytes 983048 | tf_op jit(solution)/shard_map/ppermute | solution.py:252
  44.7 1.6 %collective-permute-start.11 = (f32[128,640]{1,0:T(8,128)S(1)}, f32[128,640]{1,0:T(8,128)S(1)}, u32[]{:S(2)}, u32[]{:S(2)}) collective-permute-start(f32[128,640]{1,0:T(8,128)S(1)} %join_planes.1.refs_0_), channel_id=1, source_target_pairs={{0,4},{1,5},{2,6},{3,7},{4,0},{5,1},{6,2},{7,3},{8,12},{9,13},{10,... | collective-permute-start | bytes 983048 | tf_op jit(solution)/shard_map/ppermute | solution.py:252
  46.3 0.4 collective-permute-start.10
  46.7 0.0 collective-permute-start.13
  46.7 7.2 %collective-permute-done.12.refs_3_ = f32[128,640]{1,0:T(8,128)S(1)} collective-permute-done((f32[128,640]{1,0:T(8,128)S(1)}, f32[128,640]{1,0:T(8,128)S(1)}, u32[]{:S(2)}, u32[]{:S(2)}) %collective-permute-start.12) | collective-permute-done | bytes 327712 | tf_op jit(solution)/shard_map/ppermute | solution.py:252
  53.9 3.4 %collective-permute-done.11.refs_2_ = f32[128,640]{1,0:T(8,128)S(1)} collective-permute-done((f32[128,640]{1,0:T(8,128)S(1)}, f32[128,640]{1,0:T(8,128)S(1)}, u32[]{:S(2)}, u32[]{:S(2)}) %collective-permute-start.11) | collective-permute-done | bytes 327712 | tf_op jit(solution)/shard_map/ppermute | solution.py:252
  57.3 0.5 collective-permute-done.10.refs_1_
  57.8 1.1 %collective-permute-done.15.refs_6_ = f32[128,640]{1,0:T(8,128)S(1)} collective-permute-done((f32[128,640]{1,0:T(8,128)S(1)}, f32[128,640]{1,0:T(8,128)S(1)}, u32[]{:S(2)}, u32[]{:S(2)}) %collective-permute-start.15) | collective-permute-done | bytes 327712 | tf_op jit(solution)/shard_map/ppermute | solution.py:252
  58.9 0.6 collective-permute-done.14.refs_5_
  59.4 17.4 %sweeps.1 = (f32[128,128]{1,0:T(8,128)S(1)}, f32[128,128]{1,0:T(8,128)S(1)}) custom-call(s32[3]{0:T(128)S(1)} %pad_add_fusion.where_ref, f32[128,1024]{1,0:T(8,128)S(1)} %orth_start.1.after_ref.basis_ref, f32[128,1024]{1,0:T(8,128)S(1)} %bitcast.6, f32[128,640]{1,0:T(8,128)S(1)} %join_planes.1.refs_0_, f32[128,640]{1,0:T(8,128)S(1)} %collective-permute-done.10.refs_1_, ...), custom_call_target="tpu_custom_call" | custom-call | bytes 3801100 | tf_op jit(solution)/shard_map/sweeps/pallas_call | solution.py:236
  76.8 4.0 %collective-permute-start.19 = (f32[128,128]{1,0:T(8,128)S(1)}, f32[128,128]{1,0:T(8,128)S(1)}, u32[]{:S(2)}, u32[]{:S(2)}) collective-permute-start(f32[128,128]{1,0:T(8,128)S(1)} %get-tuple-element.28.refs_0_), channel_id=1, source_target_pairs={{0,24},{8,16},{16,8},{24,0},{1,25},{9,17},{17,9},{25,1},{2,26},{10... | collective-permute-start | bytes 196616 | tf_op jit(solution)/shard_map/ppermute | solution.py:252
  80.8 0.6 collective-permute-start.17
  81.5 3.3 %last_factor.1.factor_ref = f32[128,128]{1,0:T(8,128)S(1)} custom-call(f32[128,128]{1,0:T(8,128)S(1)} %get-tuple-element.27.matrix_ref), custom_call_target="tpu_custom_call" | custom-call | flops 1000000000 | bytes 131072 | tf_op jit(solution)/shard_map/last_factor/pallas_call | solution.py:236
  84.7 1.4 %collective-permute-done.18.refs_2_ = f32[128,128]{1,0:T(8,128)S(1)} collective-permute-done((f32[128,128]{1,0:T(8,128)S(1)}, f32[128,128]{1,0:T(8,128)S(1)}, u32[]{:S(2)}, u32[]{:S(2)}) %collective-permute-start.18) | collective-permute-done | bytes 65568 | tf_op jit(solution)/shard_map/ppermute | solution.py:252
  86.1 0.3 collective-permute-done.17.refs_1_
  86.5 2.1 %pair_gram.1 = f32[8,128]{1,0:T(8,128)S(1)} custom-call(s32[3]{0:T(128)S(1)} %pad_add_fusion.where_ref, f32[128,128]{1,0:T(8,128)S(1)} %last_factor.1.factor_ref, f32[128,128]{1,0:T(8,128)S(1)} %get-tuple-element.28.refs_0_, f32[128,128]{1,0:T(8,128)S(1)} %collective-permute-done.17.refs_1_, f32[128,128]{1,0:T(8,128)S(1)} %collective-permute-done.18.refs_2_, ...), custom_call_target="tpu_custom_call" | custom-call | bytes 331788 | tf_op jit(solution)/shard_map/pair_gram/pallas_call | solution.py:236
  88.6 1.2 %collective-permute-done.20 = f32[8,128]{1,0:T(8,128)S(1)} collective-permute-done((f32[8,128]{1,0:T(8,128)S(1)}, f32[8,128]{1,0:T(8,128)S(1)}, u32[]{:S(2)}, u32[]{:S(2)}) %collective-permute-start.20) | collective-permute-done | bytes 4128 | tf_op jit(solution)/shard_map/ppermute | solution.py:252
  89.8 0.9 collective-permute-start.21
  90.6 2.7 %collective-permute-done.21 = f32[8,128]{1,0:T(8,128)S(1)} collective-permute-done((f32[8,128]{1,0:T(8,128)S(1)}, f32[8,128]{1,0:T(8,128)S(1)}, u32[]{:S(2)}, u32[]{:S(2)}) %collective-permute-start.21) | collective-permute-done | bytes 4128 | tf_op jit(solution)/shard_map/ppermute | solution.py:252
  93.4 1.2 %collective-permute-start.22 = (f32[8,128]{1,0:T(8,128)S(1)}, f32[8,128]{1,0:T(8,128)S(1)}, u32[]{:S(2)}, u32[]{:S(2)}) collective-permute-start(f32[8,128]{1,0:T(8,128)S(1)} %add.19), channel_id=1, source_target_pairs={{0,4},{1,5},{2,6},{3,7},{4,0},{5,1},{6,2},{7,3},{8,12},{9,13},{10,... | collective-permute-start | bytes 12296 | tf_op jit(solution)/shard_map/ppermute | solution.py:252
  94.6 2.4 %collective-permute-done.22 = f32[8,128]{1,0:T(8,128)S(1)} collective-permute-done((f32[8,128]{1,0:T(8,128)S(1)}, f32[8,128]{1,0:T(8,128)S(1)}, u32[]{:S(2)}, u32[]{:S(2)}) %collective-permute-start.22) | collective-permute-done | bytes 4128 | tf_op jit(solution)/shard_map/ppermute | solution.py:252
  97.0 0.1 dynamic-slice_multiply_fusion
  97.0 0.7 copy.3
  (19 shorter events, 0.1 us)
Async XLA Ops:
  0.0 2.2 %collective-permute-start = (f32[128,1024]{1,0:T(8,128)}, f32[128,1024]{1,0:T(8,128)S(1)}, u32[]{:S(2)}, u32[]{:S(2)}) collective-permute-start(f32[128,1024]{1,0:T(8,128)} %bitcast.4), channel_id=1, source_target_pairs={{0,1},{1,0},{2,3},{3,2},{4,5},{5,4},{6,7},{7,6},{8,9},{9,8},{10,11... | collective-permute-start | bytes 1572872 | tf_op jit(solution)/shard_map/ppermute | solution.py:252
  0.5 1.0 %copy-start = (f32[8,16,1024]{2,1,0:T(8,128)S(1)}, f32[8,16,1024]{2,1,0:T(8,128)}, u32[]{:S(2)}) copy-start(f32[8,16,1024]{2,1,0:T(8,128)} %param.2) | copy-start | bytes 1572868
  2.2 6.0 %copy-start.2 = (f32[1024,128]{1,0:T(8,128)S(1)}, f32[1024,128]{1,0:T(8,128)}, u32[]{:S(2)}) copy-start(f32[1024,128]{1,0:T(8,128)} %start_ref.1) | copy-start | bytes 1572868
  3.7 11.4 %collective-permute-start.1 = (f32[128,640]{1,0:T(8,128)S(1)}, f32[128,640]{1,0:T(8,128)S(1)}, u32[]{:S(2)}, u32[]{:S(2)}) collective-permute-start(f32[128,640]{1,0:T(8,128)S(1)} %get-tuple-element.20), channel_id=1, source_target_pairs={{0,2},{1,3},{2,0},{3,1},{4,6},{5,7},{6,4},{7,5},{8,10},{9,11},{10,... | collective-permute-start | bytes 983048 | tf_op jit(solution)/shard_map/ppermute | solution.py:252
  6.6 16.5 %collective-permute-start.2 = (f32[128,640]{1,0:T(8,128)S(1)}, f32[128,640]{1,0:T(8,128)S(1)}, u32[]{:S(2)}, u32[]{:S(2)}) collective-permute-start(f32[128,640]{1,0:T(8,128)S(1)} %get-tuple-element.21), channel_id=1, source_target_pairs={{0,4},{1,5},{2,6},{3,7},{4,0},{5,1},{6,2},{7,3},{8,12},{9,13},{10,... | collective-permute-start | bytes 983048 | tf_op jit(solution)/shard_map/ppermute | solution.py:252
  8.2 15.0 %collective-permute-start.3 = (f32[128,640]{1,0:T(8,128)S(1)}, f32[128,640]{1,0:T(8,128)S(1)}, u32[]{:S(2)}, u32[]{:S(2)}) collective-permute-start(f32[128,640]{1,0:T(8,128)S(1)} %get-tuple-element.22), channel_id=1, source_target_pairs={{0,6},{1,7},{2,4},{3,5},{4,2},{5,3},{6,0},{7,1},{8,14},{9,15},{10,... | collective-permute-start | bytes 983048 | tf_op jit(solution)/shard_map/ppermute | solution.py:252
  23.8 5.3 %collective-permute-start.4 = (f32[32,640]{1,0:T(8,128)S(1)}, f32[32,640]{1,0:T(8,128)S(1)}, u32[]{:S(2)}, u32[]{:S(2)}) collective-permute-start(f32[32,640]{1,0:T(8,128)S(1)} %get-tuple-element.24), channel_id=1, source_target_pairs={{0,8},{8,0},{16,24},{24,16},{1,9},{9,1},{17,25},{25,17},{2,10},{10... | collective-permute-start | bytes 245768 | tf_op jit(solution)/shard_map/ppermute | solution.py:252
  25.4 7.6 %collective-permute-start.5 = (f32[32,640]{1,0:T(8,128)S(1)}, f32[32,640]{1,0:T(8,128)S(1)}, u32[]{:S(2)}, u32[]{:S(2)}) collective-permute-start(f32[32,640]{1,0:T(8,128)S(1)} %get-tuple-element.25), channel_id=1, source_target_pairs={{0,16},{8,24},{16,0},{24,8},{1,17},{9,25},{17,1},{25,9},{2,18},{10... | collective-permute-start | bytes 245768 | tf_op jit(solution)/shard_map/ppermute | solution.py:252
  28.0 6.3 %collective-permute-start.6 = (f32[32,640]{1,0:T(8,128)S(1)}, f32[32,640]{1,0:T(8,128)S(1)}, u32[]{:S(2)}, u32[]{:S(2)}) collective-permute-start(f32[32,640]{1,0:T(8,128)S(1)} %get-tuple-element.26), channel_id=1, source_target_pairs={{0,24},{8,16},{16,8},{24,0},{1,25},{9,17},{17,9},{25,1},{2,26},{10... | collective-permute-start | bytes 245768 | tf_op jit(solution)/shard_map/ppermute | solution.py:252
  34.3 25.1 %copy-start.1 = (f32[8,16,1024]{2,1,0:T(8,128)S(1)}, f32[8,16,1024]{2,1,0:T(8,128)}, u32[]{:S(2)}) copy-start(f32[8,16,1024]{2,1,0:T(8,128)} %param.2) | copy-start | bytes 1572868
  34.4 6.4 %collective-permute-start.9 = (f32[32,640]{1,0:T(8,128)S(1)}, f32[32,640]{1,0:T(8,128)S(1)}, u32[]{:S(2)}, u32[]{:S(2)}) collective-permute-start(f32[32,640]{1,0:T(8,128)S(1)} %sum_planes.1.refs_0_), channel_id=1, source_target_pairs={{0,24},{8,16},{16,8},{24,0},{1,25},{9,17},{17,9},{25,1},{2,26},{10... | collective-permute-start | bytes 245768 | tf_op jit(solution)/shard_map/ppermute | solution.py:252
  36.4 6.2 %collective-permute-start.8 = (f32[32,640]{1,0:T(8,128)S(1)}, f32[32,640]{1,0:T(8,128)S(1)}, u32[]{:S(2)}, u32[]{:S(2)}) collective-permute-start(f32[32,640]{1,0:T(8,128)S(1)} %sum_planes.1.refs_0_), channel_id=1, source_target_pairs={{0,16},{8,24},{16,0},{24,8},{1,17},{9,25},{17,1},{25,9},{2,18},{10... | collective-permute-start | bytes 245768 | tf_op jit(solution)/shard_map/ppermute | solution.py:252
  36.8 5.8 %collective-permute-start.7 = (f32[32,640]{1,0:T(8,128)S(1)}, f32[32,640]{1,0:T(8,128)S(1)}, u32[]{:S(2)}, u32[]{:S(2)}) collective-permute-start(f32[32,640]{1,0:T(8,128)S(1)} %sum_planes.1.refs_0_), channel_id=1, source_target_pairs={{0,8},{8,0},{16,24},{24,16},{1,9},{9,1},{17,25},{25,17},{2,10},{10... | collective-permute-start | bytes 245768 | tf_op jit(solution)/shard_map/ppermute | solution.py:252
  43.2 10.7 %collective-permute-start.12 = (f32[128,640]{1,0:T(8,128)S(1)}, f32[128,640]{1,0:T(8,128)S(1)}, u32[]{:S(2)}, u32[]{:S(2)}) collective-permute-start(f32[128,640]{1,0:T(8,128)S(1)} %join_planes.1.refs_0_), channel_id=1, source_target_pairs={{0,6},{1,7},{2,4},{3,5},{4,2},{5,3},{6,0},{7,1},{8,14},{9,15},{10,... | collective-permute-start | bytes 983048 | tf_op jit(solution)/shard_map/ppermute | solution.py:252
  44.7 12.5 %collective-permute-start.11 = (f32[128,640]{1,0:T(8,128)S(1)}, f32[128,640]{1,0:T(8,128)S(1)}, u32[]{:S(2)}, u32[]{:S(2)}) collective-permute-start(f32[128,640]{1,0:T(8,128)S(1)} %join_planes.1.refs_0_), channel_id=1, source_target_pairs={{0,4},{1,5},{2,6},{3,7},{4,0},{5,1},{6,2},{7,3},{8,12},{9,13},{10,... | collective-permute-start | bytes 983048 | tf_op jit(solution)/shard_map/ppermute | solution.py:252
  46.3 11.5 %collective-permute-start.10 = (f32[128,640]{1,0:T(8,128)S(1)}, f32[128,640]{1,0:T(8,128)S(1)}, u32[]{:S(2)}, u32[]{:S(2)}) collective-permute-start(f32[128,640]{1,0:T(8,128)S(1)} %join_planes.1.refs_0_), channel_id=1, source_target_pairs={{0,2},{1,3},{2,0},{3,1},{4,6},{5,7},{6,4},{7,5},{8,10},{9,11},{10,... | collective-permute-start | bytes 983048 | tf_op jit(solution)/shard_map/ppermute | solution.py:252
  46.7 11.1 %collective-permute-start.13 = (f32[128,640]{1,0:T(8,128)S(1)}, f32[128,640]{1,0:T(8,128)S(1)}, u32[]{:S(2)}, u32[]{:S(2)}) collective-permute-start(f32[128,640]{1,0:T(8,128)S(1)} %join_planes.1.refs_0_), channel_id=1, source_target_pairs={{0,1},{1,0},{2,3},{3,2},{4,5},{5,4},{6,7},{7,6},{8,9},{9,8},{10,11... | collective-permute-start | bytes 983048 | tf_op jit(solution)/shard_map/ppermute | solution.py:252
  53.9 3.9 %collective-permute-start.16 = (f32[128,640]{1,0:T(8,128)S(1)}, f32[128,640]{1,0:T(8,128)S(1)}, u32[]{:S(2)}, u32[]{:S(2)}) collective-permute-start(f32[128,640]{1,0:T(8,128)S(1)} %collective-permute-done.12.refs_3_), channel_id=1, source_target_pairs={{0,1},{1,0},{2,3},{3,2},{4,5},{5,4},{6,7},{7,6},{8,9},{9,8},{10,11... | collective-permute-start | bytes 983048 | tf_op jit(solution)/shard_map/ppermute | solution.py:252
  57.3 1.6 %collective-permute-start.15 = (f32[128,640]{1,0:T(8,128)S(1)}, f32[128,640]{1,0:T(8,128)S(1)}, u32[]{:S(2)}, u32[]{:S(2)}) collective-permute-start(f32[128,640]{1,0:T(8,128)S(1)} %collective-permute-done.11.refs_2_), channel_id=1, source_target_pairs={{0,1},{1,0},{2,3},{3,2},{4,5},{5,4},{6,7},{7,6},{8,9},{9,8},{10,11... | collective-permute-start | bytes 983048 | tf_op jit(solution)/shard_map/ppermute | solution.py:252
  57.8 1.6 %collective-permute-start.14 = (f32[128,640]{1,0:T(8,128)S(1)}, f32[128,640]{1,0:T(8,128)S(1)}, u32[]{:S(2)}, u32[]{:S(2)}) collective-permute-start(f32[128,640]{1,0:T(8,128)S(1)} %collective-permute-done.10.refs_1_), channel_id=1, source_target_pairs={{0,1},{1,0},{2,3},{3,2},{4,5},{5,4},{6,7},{7,6},{8,9},{9,8},{10,11... | collective-permute-start | bytes 983048 | tf_op jit(solution)/shard_map/ppermute | solution.py:252
  76.8 7.9 %collective-permute-start.19 = (f32[128,128]{1,0:T(8,128)S(1)}, f32[128,128]{1,0:T(8,128)S(1)}, u32[]{:S(2)}, u32[]{:S(2)}) collective-permute-start(f32[128,128]{1,0:T(8,128)S(1)} %get-tuple-element.28.refs_0_), channel_id=1, source_target_pairs={{0,24},{8,16},{16,8},{24,0},{1,25},{9,17},{17,9},{25,1},{2,26},{10... | collective-permute-start | bytes 196616 | tf_op jit(solution)/shard_map/ppermute | solution.py:252
  80.8 5.3 %collective-permute-start.18 = (f32[128,128]{1,0:T(8,128)S(1)}, f32[128,128]{1,0:T(8,128)S(1)}, u32[]{:S(2)}, u32[]{:S(2)}) collective-permute-start(f32[128,128]{1,0:T(8,128)S(1)} %get-tuple-element.28.refs_0_), channel_id=1, source_target_pairs={{0,16},{8,24},{16,0},{24,8},{1,17},{9,25},{17,1},{25,9},{2,18},{10... | collective-permute-start | bytes 196616 | tf_op jit(solution)/shard_map/ppermute | solution.py:252
  80.8 5.7 %collective-permute-start.17 = (f32[128,128]{1,0:T(8,128)S(1)}, f32[128,128]{1,0:T(8,128)S(1)}, u32[]{:S(2)}, u32[]{:S(2)}) collective-permute-start(f32[128,128]{1,0:T(8,128)S(1)} %get-tuple-element.28.refs_0_), channel_id=1, source_target_pairs={{0,8},{8,0},{16,24},{24,16},{1,9},{9,1},{17,25},{25,17},{2,10},{10... | collective-permute-start | bytes 196616 | tf_op jit(solution)/shard_map/ppermute | solution.py:252
  88.6 1.2 %collective-permute-start.20 = (f32[8,128]{1,0:T(8,128)S(1)}, f32[8,128]{1,0:T(8,128)S(1)}, u32[]{:S(2)}, u32[]{:S(2)}) collective-permute-start(f32[8,128]{1,0:T(8,128)S(1)} %pair_gram.1), channel_id=1, source_target_pairs={{0,1},{1,0},{2,3},{3,2},{4,5},{5,4},{6,7},{7,6},{8,9},{9,8},{10,11... | collective-permute-start | bytes 12296 | tf_op jit(solution)/shard_map/ppermute | solution.py:252
  89.8 3.6 %collective-permute-start.21 = (f32[8,128]{1,0:T(8,128)S(1)}, f32[8,128]{1,0:T(8,128)S(1)}, u32[]{:S(2)}, u32[]{:S(2)}) collective-permute-start(f32[8,128]{1,0:T(8,128)S(1)} %add.18), channel_id=1, source_target_pairs={{0,2},{1,3},{2,0},{3,1},{4,6},{5,7},{6,4},{7,5},{8,10},{9,11},{10,... | collective-permute-start | bytes 12296 | tf_op jit(solution)/shard_map/ppermute | solution.py:252
  93.4 3.6 %collective-permute-start.22 = (f32[8,128]{1,0:T(8,128)S(1)}, f32[8,128]{1,0:T(8,128)S(1)}, u32[]{:S(2)}, u32[]{:S(2)}) collective-permute-start(f32[8,128]{1,0:T(8,128)S(1)} %add.19), channel_id=1, source_target_pairs={{0,4},{1,5},{2,6},{3,7},{4,0},{5,1},{6,2},{7,3},{8,12},{9,13},{10,... | collective-permute-start | bytes 12296 | tf_op jit(solution)/shard_map/ppermute | solution.py:252

commit v2 on v1

--- a/solution.py
+++ b/solution.py
@@ -161,7 +161,7 @@
         out[pl.ds(pl.multiple_of(jnp.bitwise_xor(plane, k) * rows, rows), rows), :] = piece[...]
 
 
-def sweeps_and_core(basis_ref, field_ref, core_ref, last_ref, high_ref, low_ref, factor_ref, spread_ref, image_ref):
+def sweeps(basis_ref, image_ref, last_ref, high_ref, low_ref, factor_ref, spread_ref):
     def times_gram(rows):
         return dot_split(split(rows), (high_ref[...], low_ref[...]), NN)
 
@@ -178,15 +178,14 @@
     lax.fori_loop(0, ITERS - 1, body, 0)
     image = image_ref[...]
     last_ref[...] = dot_full(image, image, NT)
-    core_ref[...] = dot_full(field_ref[...], image, NT)
 
 
 def last_kernel(matrix_ref, out_ref, spread_ref):
     inverse_factor(matrix_ref[...], out_ref, spread_ref)
 
 
-def banded_kernel(blocks, where_ref, basis_ref, field_ref, *refs):
-    bands, rest = refs[:-7], refs[-7:]
+def banded_kernel(blocks, where_ref, basis_ref, *refs):
+    bands, rest = refs[:-6], refs[-6:]
     high_ref, low_ref = rest[2:4]
     group, core = where_ref[0], where_ref[1]
     half = len(bands) // 2
@@ -201,33 +200,37 @@
             high_ref[rows, columns], low_ref[rows, columns] = split(part)
             if 0 < k < blocks // 2:
                 high_ref[columns, rows], low_ref[columns, rows] = split(part.T)
-    sweeps_and_core(basis_ref, field_ref, *rest)
-
-
-def whole_kernel(basis_ref, field_ref, gram_ref, *rest):
+    sweeps(basis_ref, *rest)
+
+
+def whole_kernel(basis_ref, gram_ref, *rest):
     rest[2][...], rest[3][...] = split(gram_ref[...])
-    sweeps_and_core(basis_ref, field_ref, *rest)
-
-
-def pair_kernel(cells_three, where_ref, factor_ref, *refs):
-    images, out_ref = refs[:-1], refs[-1]
-    size = images[0].shape[0]
+    sweeps(basis_ref, *rest)
+
+
+def tail_kernel(cells_three, where_ref, inner_ref, image_ref, *refs):
+    fields, (out_ref, factor_ref, spread_ref, own_ref, all_ref) = refs[:-5], refs[-5:]
+    size = fields[0].shape[0]
     cells_two = size // cells_three
-    cores = [dot_full(image[...], factor_ref[...], NT) for image in images]
-    row = lax.broadcasted_iota(jnp.int32, (size, size), 0)
-    column = lax.broadcasted_iota(jnp.int32, (size, size), 1)
-    same = lax.rem(row, cells_three) == lax.rem(column, cells_three)
-    width = out_ref.shape[1]
-    target = lax.broadcasted_iota(jnp.int32, (size, width), 1)
-    source = lax.broadcasted_iota(jnp.int32, (size, width), 0) // cells_three
+    image = split(image_ref[...])
+    raw = [dot_split(split(field[...]), image, NT) for field in fields]
+    inverse_factor(inner_ref[...], factor_ref, spread_ref)
+    factor = factor_ref[...]
     plane = where_ref[2]
-    total = jnp.zeros(out_ref.shape, jnp.float32)
-    for k, core in enumerate(cores):
-        product = jnp.where(same, dot_full(cores[0], core, NT), 0.0)
-        summed = jnp.sum(product.reshape(cells_two, cells_three, size), axis=1)
-        place = jnp.where(target == source + jnp.bitwise_xor(plane, k) * cells_two, 1.0, 0.0)
-        total = total + dot_full(summed, place, NN)
-    out_ref[...] = total
+    for k, part in enumerate(raw):
+        core = dot_full(part, factor, NT)
+        if k == 0:
+            own_ref[...] = core
+        place = pl.multiple_of(jnp.bitwise_xor(plane, k) * size, size)
+        all_ref[pl.ds(place, size), :] = core
+    own = [own_ref[pl.ds(k, cells_two, stride=cells_three), :] for k in range(cells_three)]
+    every = [
+        jnp.concatenate(
+            [all_ref[pl.ds(size * q + k, cells_two, stride=cells_three), :] for q in range(len(fields))], axis=0
+        )
+        for k in range(cells_three)
+    ]
+    out_ref[...] = dot_full(jnp.concatenate(own, axis=1), jnp.concatenate(every, axis=1), NT)
 
 
 def call(kernel, outs, name, operands, scratch=(), scalars=0, order_only=(), flops=0, dtype=jnp.float32):
@@ -252,6 +255,15 @@
     return lax.ppermute(array, axis, [(i, i ^ mask) for i in range(lax.axis_size(axis))])
 
 
+def gather_planes(rows, planes):
+    mask = planes // 2
+    found = {0: rows}
+    while mask:
+        found.update({k | mask: swap(found[k], "narrow", mask) for k in list(found)})
+        mask //= 2
+    return [found[k] for k in range(1, planes)]
+
+
 def shards(field, start_block):
     cells_two, cells_three, order = field.shape
     rank = start_block.shape[1]
@@ -278,15 +290,15 @@
         pltpu.VMEM((order, order), jnp.bfloat16),
         pltpu.VMEM((rank, rank), jnp.float32),
         spread,
-        pltpu.VMEM((rank, order), jnp.float32),
     ]
-    results = [(cells, rank), (rank, rank)]
+    results = [(rank, order), (rank, rank)]
     blocks = order // BLOCK
     if wide == blocks and narrow & (narrow - 1) == 0 and BLOCK % (8 * narrow) == 0:
         groups = wide // 2
         band = BLOCK * (blocks // 2 + 1)
         extended = (cells, order + band - BLOCK)
         other = swap(unfolded, "wide", 1)
+        fields = [unfolded] + gather_planes(unfolded, narrow)
         own = call(split_kernel, [extended] * 2, "split_field", [unfolded], dtype=jnp.bfloat16)
         parts = call(
             gram_kernel,
@@ -316,24 +328,21 @@
             functools.partial(banded_kernel, blocks),
             results,
             "sweeps",
-            [where, basis, unfolded, *bands],
+            [where, basis, *bands],
             scratch,
             scalars=1,
         )
-    else:
-        basis = orthonormal_start(start_block)
-        gram = lax.dot_general(unfolded, unfolded, (((0,), (0,)), ((), ())), precision=HIGHEST)
-        gram = lax.psum(gram, ("narrow", "wide"))
-        image, inner = call(whole_kernel, results, "sweeps", [basis, unfolded, gram], scratch)
-    factor = call(last_kernel, [(rank, rank)], "last_factor", [inner], [spread], flops=10**9)
-    if narrow & (narrow - 1) == 0 and wide & (wide - 1) == 0:
-        images = [image] + [swap(image, "narrow", k) for k in range(1, narrow)]
-        width = -(-narrow * cells_two // BLOCK) * BLOCK
         total = call(
-            functools.partial(pair_kernel, cells_three),
-            [(cells_two, width)],
-            "pair_gram",
-            [where, factor, *images],
+            functools.partial(tail_kernel, cells_three),
+            [(cells_two, narrow * cells_two)],
+            "core_pairs",
+            [where, inner, image, *fields],
+            [
+                pltpu.VMEM((rank, rank), jnp.float32),
+                spread,
+                pltpu.VMEM((cells, rank), jnp.float32),
+                pltpu.VMEM((narrow * cells, rank), jnp.float32),
+            ],
             scalars=1,
         )
         mask = 1
@@ -343,7 +352,13 @@
         columns = narrow * cells_two // wide
         finished = lax.dynamic_slice_in_dim(total, place * columns, columns, 1)
     else:
-        core = lax.dot_general(image, factor, NT, precision=HIGHEST)
+        basis = orthonormal_start(start_block)
+        gram = lax.dot_general(unfolded, unfolded, (((0,), (0,)), ((), ())), precision=HIGHEST)
+        gram = lax.psum(gram, ("narrow", "wide"))
+        image, inner = call(whole_kernel, results, "sweeps", [basis, gram], scratch)
+        factor = call(last_kernel, [(rank, rank)], "last_factor", [inner], [spread])
+        core = lax.dot_general(unfolded, image, NT, precision=HIGHEST)
+        core = lax.dot_general(core, factor, NT, precision=HIGHEST)
         merged = core.reshape(cells_two, cells_three * rank)
         everyone = lax.all_gather(merged, "narrow", axis=0, tiled=True)
         part = lax.dot_general(merged, everyone, NT, precision=HIGHEST)

time: 97.9 us -> 103 us (1.052)
  starting transfers between devices: 24.1 us -> 27.8 us
  waiting for transfers between devices: 41 us -> 42.5 us
    ppermute x23, starting transfers between devices: 24.1 us -> 27.8 us  [swap(): lax.ppermute(array, axis, [(i, i ^ mask) for i in range(lax.axis_size(axi...]
    ppermute x23, waiting for transfers between devices: 41 us -> 42.5 us  [swap(): lax.ppermute(array, axis, [(i, i ^ mask) for i in range(lax.axis_size(axi...]
    pallas_call x9 -> x8, Pallas kernels: 30.6 us -> 30.2 us  [call(): pl.pallas_call(kernel, out_shape=shapes, in_specs=[SCALARS] * scalars + [...]
  transfers between devices with their start and end apart: 23 -> 23, of which waited for: 18 -> 14; matrix products, arithmetic and copies ran while one was open for 0% -> 0% of each run, Pallas kernels for 9% -> 23%
where the time goes in v2:
time: 103 us; the launch traced here: 102 us
  waiting for transfers between devices  42.5 us (41%)
  Pallas kernels  30.2 us (29%)
  starting transfers between devices  27.8 us (27%)
  local copies, waits for them, and re-layouts  1.7 us (2%)
    ppermute x23, waiting for transfers between devices, swap(): lax.ppermute(array, axis, [(i, i ^ mask) for i in range(lax.axis_size(axi...  42.5 us
    pallas_call x8, Pallas kernels, call(): pl.pallas_call(kernel, out_shape=shapes, in_specs=[SCALARS] * scalars + [...  30.2 us
    ppermute x23, starting transfers between devices, swap(): lax.ppermute(array, axis, [(i, i ^ mask) for i in range(lax.axis_size(axi...  27.8 us
  transfers between devices with their start and end apart: 23, of which 14 were waited for; matrix products, arithmetic and copies ran while one was open for 0% of the time, Pallas kernels for 23%

profile of v2, /device:TPU:0, one launch (start us, length us, event | category | flops | bytes accessed | tf_op | source)
XLA Modules:
  0.0 102.5 jit_solution(8328008386759450620)
XLA Ops:
  0.0 0.5 collective-permute-start
  0.5 1.0 %copy-done = f32[8,16,1024]{2,1,0:T(8,128)S(1)} copy-done((f32[8,16,1024]{2,1,0:T(8,128)S(1)}, f32[8,16,1024]{2,1,0:T(8,128)}, u32[]{:S(2)}) %copy-start) | copy-done | bytes 524312
  1.5 0.1 split_field.1
  1.6 0.1 pad_add_fusion.where_ref
  1.7 0.5 collective-permute-done.other_ref
  2.2 1.5 %gram_band.1 = (f32[128,640]{1,0:T(8,128)S(1)}, f32[128,640]{1,0:T(8,128)S(1)}, f32[128,640]{1,0:T(8,128)S(1)}, f32[128,640]{1,0:T(8,128)S(1)}) custom-call(s32[3]{0:T(128)S(1)} %pad_add_fusion.where_ref, bf16[128,1536]{1,0:T(8,128)(2,1)S(1)} %get-tuple-element.17.own_high, bf16[128,1536]{1,0:T(8,128)(2,1)S(1)} %get-tuple-element.18.own_low, ...), custom_call_target="tpu_custom_call" | custom-call | bytes 3407884 | tf_op jit(solution)/shard_map/gram_band/pallas_call | solution.py:239
  3.7 2.9 %collective-permute-start.1 = (f32[128,640]{1,0:T(8,128)S(1)}, f32[128,640]{1,0:T(8,128)S(1)}, u32[]{:S(2)}, u32[]{:S(2)}) collective-permute-start(f32[128,640]{1,0:T(8,128)S(1)} %get-tuple-element.20), channel_id=1, source_target_pairs={{0,2},{1,3},{2,0},{3,1},{4,6},{5,7},{6,4},{7,5},{8,10},{9,11},{10,... | collective-permute-start | bytes 983048 | tf_op jit(solution)/shard_map/ppermute | solution.py:255
  6.6 1.5 %collective-permute-start.2 = (f32[128,640]{1,0:T(8,128)S(1)}, f32[128,640]{1,0:T(8,128)S(1)}, u32[]{:S(2)}, u32[]{:S(2)}) collective-permute-start(f32[128,640]{1,0:T(8,128)S(1)} %get-tuple-element.21), channel_id=1, source_target_pairs={{0,4},{1,5},{2,6},{3,7},{4,0},{5,1},{6,2},{7,3},{8,12},{9,13},{10,... | collective-permute-start | bytes 983048 | tf_op jit(solution)/shard_map/ppermute | solution.py:255
  8.2 0.0 collective-permute-start.3
  8.2 3.0 %collective-permute-start.18 = (f32[128,1024]{1,0:T(8,128)S(1)}, f32[128,1024]{1,0:T(8,128)S(1)}, u32[]{:S(2)}, u32[]{:S(2)}) collective-permute-start(f32[128,1024]{1,0:T(8,128)S(1)} %bitcast.6), channel_id=1, source_target_pairs={{0,16},{8,24},{16,0},{24,8},{1,17},{9,25},{17,1},{25,9},{2,18},{10... | collective-permute-start | bytes 1572872 | tf_op jit(solution)/shard_map/ppermute | solution.py:255
  11.2 5.1 %orth_start.1.after_ref.basis_ref = f32[128,1024]{1,0:T(8,128)S(1)} custom-call(f32[128,640]{1,0:T(8,128)S(1)} %get-tuple-element.19.after_ref.refs_0_, f32[1024,128]{1,0:T(8,128)S(1)} %copy-done.2), custom_call_target="tpu_custom_call" | custom-call | flops 1000000000 | bytes 1048576 | tf_op jit(solution)/shard_map/orth_start/pallas_call | solution.py:239
  16.3 6.8 %collective-permute-done.2.refs_2_ = f32[128,640]{1,0:T(8,128)S(1)} collective-permute-done((f32[128,640]{1,0:T(8,128)S(1)}, f32[128,640]{1,0:T(8,128)S(1)}, u32[]{:S(2)}, u32[]{:S(2)}) %collective-permute-start.2) | collective-permute-done | bytes 327712 | tf_op jit(solution)/shard_map/ppermute | solution.py:255
  23.1 0.0 collective-permute-done.3.refs_3_
  23.1 0.6 sum_groups.1
  23.8 1.6 %collective-permute-start.4 = (f32[32,640]{1,0:T(8,128)S(1)}, f32[32,640]{1,0:T(8,128)S(1)}, u32[]{:S(2)}, u32[]{:S(2)}) collective-permute-start(f32[32,640]{1,0:T(8,128)S(1)} %get-tuple-element.24), channel_id=1, source_target_pairs={{0,8},{8,0},{16,24},{24,16},{1,9},{9,1},{17,25},{25,17},{2,10},{10... | collective-permute-start | bytes 245768 | tf_op jit(solution)/shard_map/ppermute | solution.py:255
  25.4 2.6 %collective-permute-start.5 = (f32[32,640]{1,0:T(8,128)S(1)}, f32[32,640]{1,0:T(8,128)S(1)}, u32[]{:S(2)}, u32[]{:S(2)}) collective-permute-start(f32[32,640]{1,0:T(8,128)S(1)} %get-tuple-element.25), channel_id=1, source_target_pairs={{0,16},{8,24},{16,0},{24,8},{1,17},{9,25},{17,1},{25,9},{2,18},{10... | collective-permute-start | bytes 245768 | tf_op jit(solution)/shard_map/ppermute | solution.py:255
  28.0 0.2 collective-permute-start.6
  28.2 3.2 %collective-permute-done.4.refs_1_ = f32[32,640]{1,0:T(8,128)S(1)} collective-permute-done((f32[32,640]{1,0:T(8,128)S(1)}, f32[32,640]{1,0:T(8,128)S(1)}, u32[]{:S(2)}, u32[]{:S(2)}) %collective-permute-start.4) | collective-permute-done | bytes 81952 | tf_op jit(solution)/shard_map/ppermute | solution.py:255
  31.4 8.7 %collective-permute-done.5.refs_2_ = f32[32,640]{1,0:T(8,128)S(1)} collective-permute-done((f32[32,640]{1,0:T(8,128)S(1)}, f32[32,640]{1,0:T(8,128)S(1)}, u32[]{:S(2)}, u32[]{:S(2)}) %collective-permute-start.5) | collective-permute-done | bytes 81952 | tf_op jit(solution)/shard_map/ppermute | solution.py:255
  40.0 0.0 collective-permute-done.6.refs_3_
  40.1 1.7 %collective-permute-start.7 = (f32[32,640]{1,0:T(8,128)S(1)}, f32[32,640]{1,0:T(8,128)S(1)}, u32[]{:S(2)}, u32[]{:S(2)}) collective-permute-start(f32[32,640]{1,0:T(8,128)S(1)} %sum_planes.1.refs_0_), channel_id=1, source_target_pairs={{0,8},{8,0},{16,24},{24,16},{1,9},{9,1},{17,25},{25,17},{2,10},{10... | collective-permute-start | bytes 245768 | tf_op jit(solution)/shard_map/ppermute | solution.py:255
  41.7 2.0 %collective-permute-start.8 = (f32[32,640]{1,0:T(8,128)S(1)}, f32[32,640]{1,0:T(8,128)S(1)}, u32[]{:S(2)}, u32[]{:S(2)}) collective-permute-start(f32[32,640]{1,0:T(8,128)S(1)} %sum_planes.1.refs_0_), channel_id=1, source_target_pairs={{0,16},{8,24},{16,0},{24,8},{1,17},{9,25},{17,1},{25,9},{2,18},{10... | collective-permute-start | bytes 245768 | tf_op jit(solution)/shard_map/ppermute | solution.py:255
  43.7 1.4 %collective-permute-start.9 = (f32[32,640]{1,0:T(8,128)S(1)}, f32[32,640]{1,0:T(8,128)S(1)}, u32[]{:S(2)}, u32[]{:S(2)}) collective-permute-start(f32[32,640]{1,0:T(8,128)S(1)} %sum_planes.1.refs_0_), channel_id=1, source_target_pairs={{0,24},{8,16},{16,8},{24,0},{1,25},{9,17},{17,9},{25,1},{2,26},{10... | collective-permute-start | bytes 245768 | tf_op jit(solution)/shard_map/ppermute | solution.py:255
  45.1 3.0 %collective-permute-done.8.refs_2_ = f32[32,640]{1,0:T(8,128)S(1)} collective-permute-done((f32[32,640]{1,0:T(8,128)S(1)}, f32[32,640]{1,0:T(8,128)S(1)}, u32[]{:S(2)}, u32[]{:S(2)}) %collective-permute-start.8) | collective-permute-done | bytes 81952 | tf_op jit(solution)/shard_map/ppermute | solution.py:255
  48.1 2.9 %collective-permute-done.9.refs_3_ = f32[32,640]{1,0:T(8,128)S(1)} collective-permute-done((f32[32,640]{1,0:T(8,128)S(1)}, f32[32,640]{1,0:T(8,128)S(1)}, u32[]{:S(2)}, u32[]{:S(2)}) %collective-permute-start.9) | collective-permute-done | bytes 81952 | tf_op jit(solution)/shard_map/ppermute | solution.py:255
  51.0 0.6 join_planes.1.refs_0_
  51.6 1.6 %collective-permute-start.10 = (f32[128,640]{1,0:T(8,128)S(1)}, f32[128,640]{1,0:T(8,128)S(1)}, u32[]{:S(2)}, u32[]{:S(2)}) collective-permute-start(f32[128,640]{1,0:T(8,128)S(1)} %join_planes.1.refs_0_), channel_id=1, source_target_pairs={{0,2},{1,3},{2,0},{3,1},{4,6},{5,7},{6,4},{7,5},{8,10},{9,11},{10,... | collective-permute-start | bytes 983048 | tf_op jit(solution)/shard_map/ppermute | solution.py:255
  53.1 1.5 %collective-permute-start.11 = (f32[128,640]{1,0:T(8,128)S(1)}, f32[128,640]{1,0:T(8,128)S(1)}, u32[]{:S(2)}, u32[]{:S(2)}) collective-permute-start(f32[128,640]{1,0:T(8,128)S(1)} %join_planes.1.refs_0_), channel_id=1, source_target_pairs={{0,4},{1,5},{2,6},{3,7},{4,0},{5,1},{6,2},{7,3},{8,12},{9,13},{10,... | collective-permute-start | bytes 983048 | tf_op jit(solution)/shard_map/ppermute | solution.py:255
  54.7 0.5 collective-permute-start.12
  55.1 1.9 %collective-permute-start.17 = (f32[128,1024]{1,0:T(8,128)S(1)}, f32[128,1024]{1,0:T(8,128)S(1)}, u32[]{:S(2)}, u32[]{:S(2)}) collective-permute-start(f32[128,1024]{1,0:T(8,128)S(1)} %bitcast.7), channel_id=1, source_target_pairs={{0,8},{8,0},{16,24},{24,16},{1,9},{9,1},{17,25},{25,17},{2,10},{10... | collective-permute-start | bytes 1572872 | tf_op jit(solution)/shard_map/ppermute | solution.py:255
  57.0 5.3 %collective-permute-done.10.refs_1_ = f32[128,640]{1,0:T(8,128)S(1)} collective-permute-done((f32[128,640]{1,0:T(8,128)S(1)}, f32[128,640]{1,0:T(8,128)S(1)}, u32[]{:S(2)}, u32[]{:S(2)}) %collective-permute-start.10) | collective-permute-done | bytes 327712 | tf_op jit(solution)/shard_map/ppermute | solution.py:255
  62.3 1.9 %collective-permute-start.19 = (f32[128,1024]{1,0:T(8,128)S(1)}, f32[128,1024]{1,0:T(8,128)S(1)}, u32[]{:S(2)}, u32[]{:S(2)}) collective-permute-start(f32[128,1024]{1,0:T(8,128)S(1)} %collective-permute-done.18.refs_2_), channel_id=1, source_target_pairs={{0,8},{8,0},{16,24},{24,16},{1,9},{9,1},{17,25},{25,17},{2,10},{10... | collective-permute-start | bytes 1572872 | tf_op jit(solution)/shard_map/ppermute | solution.py:255
  64.2 4.2 %collective-permute-done.11.refs_2_ = f32[128,640]{1,0:T(8,128)S(1)} collective-permute-done((f32[128,640]{1,0:T(8,128)S(1)}, f32[128,640]{1,0:T(8,128)S(1)}, u32[]{:S(2)}, u32[]{:S(2)}) %collective-permute-start.11) | collective-permute-done | bytes 327712 | tf_op jit(solution)/shard_map/ppermute | solution.py:255
  68.4 0.5 collective-permute-start.15
  68.9 0.1 collective-permute-start.16
  69.0 1.0 %collective-permute-done.14.refs_5_ = f32[128,640]{1,0:T(8,128)S(1)} collective-permute-done((f32[128,640]{1,0:T(8,128)S(1)}, f32[128,640]{1,0:T(8,128)S(1)}, u32[]{:S(2)}, u32[]{:S(2)}) %collective-permute-start.14) | collective-permute-done | bytes 327712 | tf_op jit(solution)/shard_map/ppermute | solution.py:255
  70.0 0.5 collective-permute-done.15.refs_6_
  70.5 0.5 collective-permute-done.16.refs_7_
  70.9 17.0 %sweeps.1 = (f32[128,1024]{1,0:T(8,128)S(1)}, f32[128,128]{1,0:T(8,128)S(1)}) custom-call(s32[3]{0:T(128)S(1)} %pad_add_fusion.where_ref, f32[128,1024]{1,0:T(8,128)S(1)} %orth_start.1.after_ref.basis_ref, f32[128,640]{1,0:T(8,128)S(1)} %join_planes.1.refs_0_, f32[128,640]{1,0:T(8,128)S(1)} %collective-permute-done.10.refs_1_, ...), custom_call_target="tpu_custom_call" | custom-call | bytes 3735564 | tf_op jit(solution)/shard_map/sweeps/pallas_call | solution.py:239
  88.0 5.3 %core_pairs.1 = f32[8,32]{1,0:T(8,128)S(1)} custom-call(s32[3]{0:T(128)S(1)} %pad_add_fusion.where_ref, f32[128,128]{1,0:T(8,128)S(1)} %get-tuple-element.27.inner_ref, f32[128,1024]{1,0:T(8,128)S(1)} %get-tuple-element.28.image_ref, f32[128,1024]{1,0:T(8,128)S(1)} %bitcast.8, f32[128,1024]{1,0:T(8,128)S(1)} %collective-permute-done.17.refs_1_, ...), custom_call_target="tpu_custom_call" | custom-call | bytes 2688012 | tf_op jit(solution)/shard_map/core_pairs/pallas_call | solution.py:239
  93.3 0.2 collective-permute-start.20
  93.5 1.0 collective-permute-done.20
  94.5 0.8 collective-permute-start.21
  95.3 2.8 %collective-permute-done.21 = f32[8,32]{1,0:T(8,128)S(1)} collective-permute-done((f32[8,32]{1,0:T(8,128)S(1)}, f32[8,32]{1,0:T(8,128)S(1)}, u32[]{:S(2)}, u32[]{:S(2)}) %collective-permute-start.21) | collective-permute-done | bytes 1056 | tf_op jit(solution)/shard_map/ppermute | solution.py:255
  98.1 1.5 %collective-permute-start.22 = (f32[8,32]{1,0:T(8,128)S(1)}, f32[8,32]{1,0:T(8,128)S(1)}, u32[]{:S(2)}, u32[]{:S(2)}) collective-permute-start(f32[8,32]{1,0:T(8,128)S(1)} %add.19), channel_id=1, source_target_pairs={{0,4},{1,5},{2,6},{3,7},{4,0},{5,1},{6,2},{7,3},{8,12},{9,13},{10,... | collective-permute-start | bytes 3080 | tf_op jit(solution)/shard_map/ppermute | solution.py:255
  99.7 2.1 %collective-permute-done.22 = f32[8,32]{1,0:T(8,128)S(1)} collective-permute-done((f32[8,32]{1,0:T(8,128)S(1)}, f32[8,32]{1,0:T(8,128)S(1)}, u32[]{:S(2)}, u32[]{:S(2)}) %collective-permute-start.22) | collective-permute-done | bytes 1056 | tf_op jit(solution)/shard_map/ppermute | solution.py:255
  101.8 0.1 dynamic-slice_multiply_fusion
  101.8 0.7 copy.3
  (18 shorter events, 0.1 us)
Async XLA Ops:
  0.0 2.2 %collective-permute-start = (f32[128,1024]{1,0:T(8,128)}, f32[128,1024]{1,0:T(8,128)S(1)}, u32[]{:S(2)}, u32[]{:S(2)}) collective-permute-start(f32[128,1024]{1,0:T(8,128)} %bitcast.4), channel_id=1, source_target_pairs={{0,1},{1,0},{2,3},{3,2},{4,5},{5,4},{6,7},{7,6},{8,9},{9,8},{10,11... | collective-permute-start | bytes 1572872 | tf_op jit(solution)/shard_map/ppermute | solution.py:255
  0.5 1.0 %copy-start = (f32[8,16,1024]{2,1,0:T(8,128)S(1)}, f32[8,16,1024]{2,1,0:T(8,128)}, u32[]{:S(2)}) copy-start(f32[8,16,1024]{2,1,0:T(8,128)} %param.2) | copy-start | bytes 1572868
  2.2 6.0 %copy-start.1 = (f32[8,16,1024]{2,1,0:T(8,128)S(1)}, f32[8,16,1024]{2,1,0:T(8,128)}, u32[]{:S(2)}) copy-start(f32[8,16,1024]{2,1,0:T(8,128)} %param.2) | copy-start | bytes 1572868
  2.2 9.0 %copy-start.2 = (f32[1024,128]{1,0:T(8,128)S(1)}, f32[1024,128]{1,0:T(8,128)}, u32[]{:S(2)}) copy-start(f32[1024,128]{1,0:T(8,128)} %start_ref.1) | copy-start | bytes 1572868
  3.7 12.6 %collective-permute-start.1 = (f32[128,640]{1,0:T(8,128)S(1)}, f32[128,640]{1,0:T(8,128)S(1)}, u32[]{:S(2)}, u32[]{:S(2)}) collective-permute-start(f32[128,640]{1,0:T(8,128)S(1)} %get-tuple-element.20), channel_id=1, source_target_pairs={{0,2},{1,3},{2,0},{3,1},{4,6},{5,7},{6,4},{7,5},{8,10},{9,11},{10,... | collective-permute-start | bytes 983048 | tf_op jit(solution)/shard_map/ppermute | solution.py:255
  6.6 16.5 %collective-permute-start.2 = (f32[128,640]{1,0:T(8,128)S(1)}, f32[128,640]{1,0:T(8,128)S(1)}, u32[]{:S(2)}, u32[]{:S(2)}) collective-permute-start(f32[128,640]{1,0:T(8,128)S(1)} %get-tuple-element.21), channel_id=1, source_target_pairs={{0,4},{1,5},{2,6},{3,7},{4,0},{5,1},{6,2},{7,3},{8,12},{9,13},{10,... | collective-permute-start | bytes 983048 | tf_op jit(solution)/shard_map/ppermute | solution.py:255
  8.2 15.0 %collective-permute-start.3 = (f32[128,640]{1,0:T(8,128)S(1)}, f32[128,640]{1,0:T(8,128)S(1)}, u32[]{:S(2)}, u32[]{:S(2)}) collective-permute-start(f32[128,640]{1,0:T(8,128)S(1)} %get-tuple-element.22), channel_id=1, source_target_pairs={{0,6},{1,7},{2,4},{3,5},{4,2},{5,3},{6,0},{7,1},{8,14},{9,15},{10,... | collective-permute-start | bytes 983048 | tf_op jit(solution)/shard_map/ppermute | solution.py:255
  8.2 47.0 %collective-permute-start.18 = (f32[128,1024]{1,0:T(8,128)S(1)}, f32[128,1024]{1,0:T(8,128)S(1)}, u32[]{:S(2)}, u32[]{:S(2)}) collective-permute-start(f32[128,1024]{1,0:T(8,128)S(1)} %bitcast.6), channel_id=1, source_target_pairs={{0,16},{8,24},{16,0},{24,8},{1,17},{9,25},{17,1},{25,9},{2,18},{10... | collective-permute-start | bytes 1572872 | tf_op jit(solution)/shard_map/ppermute | solution.py:255
  23.8 7.6 %collective-permute-start.4 = (f32[32,640]{1,0:T(8,128)S(1)}, f32[32,640]{1,0:T(8,128)S(1)}, u32[]{:S(2)}, u32[]{:S(2)}) collective-permute-start(f32[32,640]{1,0:T(8,128)S(1)} %get-tuple-element.24), channel_id=1, source_target_pairs={{0,8},{8,0},{16,24},{24,16},{1,9},{9,1},{17,25},{25,17},{2,10},{10... | collective-permute-start | bytes 245768 | tf_op jit(solution)/shard_map/ppermute | solution.py:255
  25.4 14.6 %collective-permute-start.5 = (f32[32,640]{1,0:T(8,128)S(1)}, f32[32,640]{1,0:T(8,128)S(1)}, u32[]{:S(2)}, u32[]{:S(2)}) collective-permute-start(f32[32,640]{1,0:T(8,128)S(1)} %get-tuple-element.25), channel_id=1, source_target_pairs={{0,16},{8,24},{16,0},{24,8},{1,17},{9,25},{17,1},{25,9},{2,18},{10... | collective-permute-start | bytes 245768 | tf_op jit(solution)/shard_map/ppermute | solution.py:255
  28.0 12.0 %collective-permute-start.6 = (f32[32,640]{1,0:T(8,128)S(1)}, f32[32,640]{1,0:T(8,128)S(1)}, u32[]{:S(2)}, u32[]{:S(2)}) collective-permute-start(f32[32,640]{1,0:T(8,128)S(1)} %get-tuple-element.26), channel_id=1, source_target_pairs={{0,24},{8,16},{16,8},{24,0},{1,25},{9,17},{17,9},{25,1},{2,26},{10... | collective-permute-start | bytes 245768 | tf_op jit(solution)/shard_map/ppermute | solution.py:255
  40.1 5.0 %collective-permute-start.7 = (f32[32,640]{1,0:T(8,128)S(1)}, f32[32,640]{1,0:T(8,128)S(1)}, u32[]{:S(2)}, u32[]{:S(2)}) collective-permute-start(f32[32,640]{1,0:T(8,128)S(1)} %sum_planes.1.refs_0_), channel_id=1, source_target_pairs={{0,8},{8,0},{16,24},{24,16},{1,9},{9,1},{17,25},{25,17},{2,10},{10... | collective-permute-start | bytes 245768 | tf_op jit(solution)/shard_map/ppermute | solution.py:255
  41.7 6.4 %collective-permute-start.8 = (f32[32,640]{1,0:T(8,128)S(1)}, f32[32,640]{1,0:T(8,128)S(1)}, u32[]{:S(2)}, u32[]{:S(2)}) collective-permute-start(f32[32,640]{1,0:T(8,128)S(1)} %sum_planes.1.refs_0_), channel_id=1, source_target_pairs={{0,16},{8,24},{16,0},{24,8},{1,17},{9,25},{17,1},{25,9},{2,18},{10... | collective-permute-start | bytes 245768 | tf_op jit(solution)/shard_map/ppermute | solution.py:255
  43.7 7.3 %collective-permute-start.9 = (f32[32,640]{1,0:T(8,128)S(1)}, f32[32,640]{1,0:T(8,128)S(1)}, u32[]{:S(2)}, u32[]{:S(2)}) collective-permute-start(f32[32,640]{1,0:T(8,128)S(1)} %sum_planes.1.refs_0_), channel_id=1, source_target_pairs={{0,24},{8,16},{16,8},{24,0},{1,25},{9,17},{17,9},{25,1},{2,26},{10... | collective-permute-start | bytes 245768 | tf_op jit(solution)/shard_map/ppermute | solution.py:255
  51.6 10.7 %collective-permute-start.10 = (f32[128,640]{1,0:T(8,128)S(1)}, f32[128,640]{1,0:T(8,128)S(1)}, u32[]{:S(2)}, u32[]{:S(2)}) collective-permute-start(f32[128,640]{1,0:T(8,128)S(1)} %join_planes.1.refs_0_), channel_id=1, source_target_pairs={{0,2},{1,3},{2,0},{3,1},{4,6},{5,7},{6,4},{7,5},{8,10},{9,11},{10,... | collective-permute-start | bytes 983048 | tf_op jit(solution)/shard_map/ppermute | solution.py:255
  53.1 15.2 %collective-permute-start.11 = (f32[128,640]{1,0:T(8,128)S(1)}, f32[128,640]{1,0:T(8,128)S(1)}, u32[]{:S(2)}, u32[]{:S(2)}) collective-permute-start(f32[128,640]{1,0:T(8,128)S(1)} %join_planes.1.refs_0_), channel_id=1, source_target_pairs={{0,4},{1,5},{2,6},{3,7},{4,0},{5,1},{6,2},{7,3},{8,12},{9,13},{10,... | collective-permute-start | bytes 983048 | tf_op jit(solution)/shard_map/ppermute | solution.py:255
  54.7 13.7 %collective-permute-start.12 = (f32[128,640]{1,0:T(8,128)S(1)}, f32[128,640]{1,0:T(8,128)S(1)}, u32[]{:S(2)}, u32[]{:S(2)}) collective-permute-start(f32[128,640]{1,0:T(8,128)S(1)} %join_planes.1.refs_0_), channel_id=1, source_target_pairs={{0,6},{1,7},{2,4},{3,5},{4,2},{5,3},{6,0},{7,1},{8,14},{9,15},{10,... | collective-permute-start | bytes 983048 | tf_op jit(solution)/shard_map/ppermute | solution.py:255
  55.1 13.8 %collective-permute-start.13 = (f32[128,640]{1,0:T(8,128)S(1)}, f32[128,640]{1,0:T(8,128)S(1)}, u32[]{:S(2)}, u32[]{:S(2)}) collective-permute-start(f32[128,640]{1,0:T(8,128)S(1)} %join_planes.1.refs_0_), channel_id=1, source_target_pairs={{0,1},{1,0},{2,3},{3,2},{4,5},{5,4},{6,7},{7,6},{8,9},{9,8},{10,11... | collective-permute-start | bytes 983048 | tf_op jit(solution)/shard_map/ppermute | solution.py:255
  55.1 32.8 %collective-permute-start.17 = (f32[128,1024]{1,0:T(8,128)S(1)}, f32[128,1024]{1,0:T(8,128)S(1)}, u32[]{:S(2)}, u32[]{:S(2)}) collective-permute-start(f32[128,1024]{1,0:T(8,128)S(1)} %bitcast.7), channel_id=1, source_target_pairs={{0,8},{8,0},{16,24},{24,16},{1,9},{9,1},{17,25},{25,17},{2,10},{10... | collective-permute-start | bytes 1572872 | tf_op jit(solution)/shard_map/ppermute | solution.py:255
  62.3 25.7 %collective-permute-start.19 = (f32[128,1024]{1,0:T(8,128)S(1)}, f32[128,1024]{1,0:T(8,128)S(1)}, u32[]{:S(2)}, u32[]{:S(2)}) collective-permute-start(f32[128,1024]{1,0:T(8,128)S(1)} %collective-permute-done.18.refs_2_), channel_id=1, source_target_pairs={{0,8},{8,0},{16,24},{24,16},{1,9},{9,1},{17,25},{25,17},{2,10},{10... | collective-permute-start | bytes 1572872 | tf_op jit(solution)/shard_map/ppermute | solution.py:255
  68.4 1.6 %collective-permute-start.14 = (f32[128,640]{1,0:T(8,128)S(1)}, f32[128,640]{1,0:T(8,128)S(1)}, u32[]{:S(2)}, u32[]{:S(2)}) collective-permute-start(f32[128,640]{1,0:T(8,128)S(1)} %collective-permute-done.10.refs_1_), channel_id=1, source_target_pairs={{0,1},{1,0},{2,3},{3,2},{4,5},{5,4},{6,7},{7,6},{8,9},{9,8},{10,11... | collective-permute-start | bytes 983048 | tf_op jit(solution)/shard_map/ppermute | solution.py:255
  68.4 2.1 %collective-permute-start.15 = (f32[128,640]{1,0:T(8,128)S(1)}, f32[128,640]{1,0:T(8,128)S(1)}, u32[]{:S(2)}, u32[]{:S(2)}) collective-permute-start(f32[128,640]{1,0:T(8,128)S(1)} %collective-permute-done.11.refs_2_), channel_id=1, source_target_pairs={{0,1},{1,0},{2,3},{3,2},{4,5},{5,4},{6,7},{7,6},{8,9},{9,8},{10,11... | collective-permute-start | bytes 983048 | tf_op jit(solution)/shard_map/ppermute | solution.py:255
  68.9 2.0 %collective-permute-start.16 = (f32[128,640]{1,0:T(8,128)S(1)}, f32[128,640]{1,0:T(8,128)S(1)}, u32[]{:S(2)}, u32[]{:S(2)}) collective-permute-start(f32[128,640]{1,0:T(8,128)S(1)} %collective-permute-done.12.refs_3_), channel_id=1, source_target_pairs={{0,1},{1,0},{2,3},{3,2},{4,5},{5,4},{6,7},{7,6},{8,9},{9,8},{10,11... | collective-permute-start | bytes 983048 | tf_op jit(solution)/shard_map/ppermute | solution.py:255
  93.3 1.2 %collective-permute-start.20 = (f32[8,32]{1,0:T(8,128)S(1)}, f32[8,32]{1,0:T(8,128)S(1)}, u32[]{:S(2)}, u32[]{:S(2)}) collective-permute-start(f32[8,32]{1,0:T(8,128)S(1)} %core_pairs.1), channel_id=1, source_target_pairs={{0,1},{1,0},{2,3},{3,2},{4,5},{5,4},{6,7},{7,6},{8,9},{9,8},{10,11... | collective-permute-start | bytes 3080 | tf_op jit(solution)/shard_map/ppermute | solution.py:255
  94.5 3.6 %collective-permute-start.21 = (f32[8,32]{1,0:T(8,128)S(1)}, f32[8,32]{1,0:T(8,128)S(1)}, u32[]{:S(2)}, u32[]{:S(2)}) collective-permute-start(f32[8,32]{1,0:T(8,128)S(1)} %add.18), channel_id=1, source_target_pairs={{0,2},{1,3},{2,0},{3,1},{4,6},{5,7},{6,4},{7,5},{8,10},{9,11},{10,... | collective-permute-start | bytes 3080 | tf_op jit(solution)/shard_map/ppermute | solution.py:255
  98.1 3.6 %collective-permute-start.22 = (f32[8,32]{1,0:T(8,128)S(1)}, f32[8,32]{1,0:T(8,128)S(1)}, u32[]{:S(2)}, u32[]{:S(2)}) collective-permute-start(f32[8,32]{1,0:T(8,128)S(1)} %add.19), channel_id=1, source_target_pairs={{0,4},{1,5},{2,6},{3,7},{4,0},{5,1},{6,2},{7,3},{8,12},{9,13},{10,... | collective-permute-start | bytes 3080 | tf_op jit(solution)/shard_map/ppermute | solution.py:255

commit v3 on v2

v3 whole, which is shorter than its diff:
```python
import functools
import jax
import jax.numpy as jnp
from jax import lax
from jax.experimental import pallas as pl
from jax.experimental.pallas import tpu as pltpu
from jax.sharding import PartitionSpec as P

ITERS = 4
BLOCK = 128
PANEL = 8
HIGHEST = lax.Precision.HIGHEST
NN = (((1,), (0,)), ((), ()))
NT = (((1,), (1,)), ((), ()))
VMEM = pl.BlockSpec(memory_space=pltpu.VMEM)


def split(values):
    high = values.astype(jnp.bfloat16)
    return high, (values - high.astype(jnp.float32)).astype(jnp.bfloat16)


def dot_bf16(left, right, dims):
    return lax.dot_general(left, right, dims, preferred_element_type=jnp.float32)


def dot_split(left, right, dims):
    (left_high, left_low), (right_high, right_low) = left, right
    return (
        dot_bf16(left_high, right_high, dims)
        + (dot_bf16(left_low, right_high, dims) + dot_bf16(left_high, right_low, dims))
    )


def dot_full(left, right, dims):
    return lax.dot_general(left, right, dims, precision=HIGHEST, preferred_element_type=jnp.float32)


def add_pairs(terms):
    terms = list(terms)
    while len(terms) > 1:
        pairs = [terms[i] + terms[i + 1] for i in range(0, len(terms) - 1, 2)]
        terms = pairs + terms[2 * len(pairs) :]
    return terms[0]


def inverse_factor(matrix, out_ref, scratch):
    order = matrix.shape[0]
    panels = order // PANEL
    tiles = [matrix[PANEL * i : PANEL * (i + 1), :] for i in range(panels)]
    lane = lax.broadcasted_iota(jnp.int32, (PANEL, order), 1)

    def full(part):
        return jnp.broadcast_to(part, (PANEL, order))

    for p in range(panels):
        tile, start = tiles[p], PANEL * p
        base = PANEL * PANEL * (p % 2)
        inside = (lane >= start) & (lane < start + PANEL)
        for c in range(PANEL):
            scratch[base + PANEL * c : base + PANEL * (c + 1), :] = full(tile[:, start + c : start + c + 1])
        pivot = {
            (r, c): full(scratch[base + PANEL * c + r : base + PANEL * c + r + 1, :])
            for c in range(PANEL)
            for r in range(c, PANEL)
        }
        rows = [
            jnp.where(inside, jnp.where(lane == start + c, 1.0, 0.0), full(tile[c : c + 1, :]))
            for c in range(PANEL)
        ]
        reciprocal, inverse = {}, {}
        for c in range(PANEL):
            reciprocal[c] = 1.0 / pivot[c, c]
            lower = {r: pivot[r, c] * reciprocal[c] for r in range(c + 1, PANEL)}
            for d in range(c + 1, PANEL):
                for r in range(d, PANEL):
                    if r == c + 1:
                        pivot[r, d] = pivot[r, d] - (pivot[r, c] * pivot[d, c]) * reciprocal[c]
                    else:
                        pivot[r, d] = pivot[r, d] - lower[r] * pivot[d, c]
            for r in range(c + 1, PANEL):
                rows[r] = rows[r] - lower[r] * rows[c]
                for k in range(c):
                    inverse[r, k] = inverse[r, k] - lower[r] * inverse[c, k]
                inverse[r, c] = -lower[r]
        for r in range(PANEL):
            done = jnp.where(lane < start + PANEL, rows[r], 0.0) * lax.rsqrt(pivot[r, r])
            out_ref[start + r : start + r + 1, :] = done[0:1, :]
        if p == panels - 1:
            break
        scaled = [rows[r] * reciprocal[r] for r in range(PANEL)]
        eliminate = []
        for c in range(PANEL):
            total = scaled[c]
            for r in range(c + 1, PANEL):
                total = total + inverse[r, c] * scaled[r]
            eliminate.append(total)
        for i in range(p + 1, panels):
            steps = [full(tiles[i][:, start + c : start + c + 1]) * eliminate[c] for c in range(PANEL)]
            tiles[i] = jnp.where(inside, 0.0, tiles[i]) - add_pairs(steps)


def start_kernel(after_ref, start_ref, out_ref, factor_ref, spread_ref):
    del after_ref
    rows = start_ref[...].T
    inverse_factor(dot_full(rows, rows, NT), factor_ref, spread_ref)
    out_ref[...] = dot_full(factor_ref[...], rows, NN)


def split_kernel(rows_ref, high_ref, low_ref):
    order = rows_ref.shape[1]
    extra = high_ref.shape[1] - order
    for target, values in zip((high_ref, low_ref), split(rows_ref[...])):
        target[:, 0:order] = values
        target[:, order : order + extra] = values[:, :extra]


def chip_and_core():
    place = lax.axis_index("wide")
    return place // 2, lax.rem(place, 2)


def gram_kernel(own_high, own_low, other_ref, *refs):
    outs, (high_ref, low_ref) = refs[:-2], refs[-2:]
    band = outs[0].shape[1]
    rows, order = other_ref.shape
    extra = high_ref.shape[1] - order
    for own, target, values in zip((own_high, own_low), (high_ref, low_ref), split(other_ref[...])):
        target[0:rows, :] = own[...]
        target[rows : 2 * rows, 0:order] = values
        target[rows : 2 * rows, order : order + extra] = values[:, :extra]
    group, core = chip_and_core()
    half = BLOCK // 2
    first_keep, first_send, second_keep, second_send = outs
    upper = [first_keep, first_send, first_keep, first_send]
    lower = [second_keep, second_keep, second_send, second_send]
    for k in range(len(outs)):
        first = pl.multiple_of((2 * jnp.bitwise_xor(group, k) + core) * BLOCK, BLOCK)
        left = [ref[:, pl.ds(first, BLOCK)].astype(jnp.float32).T.astype(jnp.bfloat16) for ref in (high_ref, low_ref)]
        right = [ref[:, pl.ds(first, band)] for ref in (high_ref, low_ref)]
        rows = dot_split(left, right, NN)
        upper[k][half * (k // 2) : half * (k // 2 + 1), :] = rows[:half]
        lower[k][half * (k % 2) : half * (k % 2 + 1), :] = rows[half:]


def halve_kernel(after_ref, kept_first, got_first, kept_second, got_second, *outs):
    del after_ref
    half = kept_first.shape[0] // 2
    for kept, got, (own, send) in ((kept_first, got_first, outs[:2]), (kept_second, got_second, outs[2:])):
        own[...] = kept[:half, :] + got[:half, :]
        send[...] = kept[half:, :] + got[half:, :]


def cut_kernel(first, got_first, second, got_second, *outs):
    rows = outs[0].shape[0] // 2
    plane = lax.axis_index("narrow")
    for k, out in enumerate(outs):
        piece = pl.ds(pl.multiple_of(jnp.bitwise_xor(plane, k) * rows, rows), rows)
        out[:rows, :] = first[piece, :] + got_first[piece, :]
        out[rows:, :] = second[piece, :] + got_second[piece, :]


def add_kernel(*refs):
    total = refs[0][...]
    for term in refs[1:-1]:
        total = total + term[...]
    refs[-1][...] = total


def join_kernel(*refs):
    pieces, (first, second) = refs[:-2], refs[-2:]
    rows = pieces[0].shape[0] // 2
    plane = lax.axis_index("narrow")
    for k, piece in enumerate(pieces):
        place = pl.ds(pl.multiple_of(jnp.bitwise_xor(plane, k) * rows, rows), rows)
        first[place, :] = piece[:rows, :]
        second[place, :] = piece[rows:, :]


def stack_kernel(first, got_first, second, got_second, first_out, second_out):
    half = first.shape[0]
    for own, got, out in ((first, got_first, first_out), (second, got_second, second_out)):
        out[:half, :] = own[...]
        out[half:, :] = got[...]


def sweeps(basis_ref, field_ref, image_ref, inner_ref, raw_ref, high_ref, low_ref, factor_ref, spread_ref, basis_scratch):
    def times_gram(rows):
        return dot_split(split(rows), (high_ref[...], low_ref[...]), NN)

    def body(step, carry):
        image = basis_scratch[...]
        halves = split(image)
        inner = dot_split(halves, halves, NT)
        following = times_gram(image)
        inverse_factor(inner, factor_ref, spread_ref)
        basis_scratch[...] = dot_split(split(factor_ref[...]), split(following), NN)
        return carry

    basis_scratch[...] = times_gram(basis_ref[...])
    lax.fori_loop(0, ITERS - 2, body, 0)
    image = basis_scratch[...]
    following = times_gram(image)
    image_ref[...] = following
    inner_ref[...] = dot_full(image, image, NT)
    raw_ref[...] = dot_full(field_ref[...], following, NT)


def last_kernel(image_ref, inner_ref, out_ref, factor_ref, spread_ref):
    inverse_factor(inner_ref[...], factor_ref, spread_ref)
    before = factor_ref[...]
    image = dot_full(before, image_ref[...], NN)
    inverse_factor(dot_full(image, image, NT), factor_ref, spread_ref)
    out_ref[...] = dot_full(factor_ref[...], before, NN)


def banded_kernel(blocks, basis_ref, field_ref, *refs):
    bands, rest = refs[:-8], refs[-8:]
    high_ref, low_ref = rest[3:5]
    group, core = chip_and_core()
    half = BLOCK // 2
    halves = {0: ((0, 0), (1, 0)), 1: ((2, 0), (1, 1)), 2: ((0, 1), (3, 0)), 3: ((2, 1), (3, 1))}
    for place in range(2 * len(halves)):
        side = core if place < len(halves) else 1 - core
        row = 2 * jnp.bitwise_xor(group, place % len(halves)) + side
        upper, lower = [
            bands[number + 4 * (place // len(halves))].at[half * part : half * (part + 1)]
            for number, part in halves[place % len(halves)]
        ]
        rows = pl.ds(pl.multiple_of(row * BLOCK, BLOCK), BLOCK)
        for k in range(blocks // 2 + 1):
            column = lax.rem(row + k, blocks)
            columns = pl.ds(pl.multiple_of(column * BLOCK, BLOCK), BLOCK)
            inside = slice(BLOCK * k, BLOCK * (k + 1))
            part = jnp.concatenate([upper[:, inside], lower[:, inside]], axis=0)
            high_ref[rows, columns], low_ref[rows, columns] = split(part)
            if 0 < k < blocks // 2:
                high_ref[columns, rows], low_ref[columns, rows] = split(part.T)
    sweeps(basis_ref, field_ref, *rest)


def whole_kernel(basis_ref, field_ref, gram_ref, *rest):
    rest[3][...], rest[4][...] = split(gram_ref[...])
    sweeps(basis_ref, field_ref, *rest)


def tail_kernel(cells_three, factor_ref, *refs):
    raw, (out_ref, own_ref, all_ref) = refs[:-3], refs[-3:]
    size = raw[0].shape[0]
    cells_two = size // cells_three
    planes = len(raw)
    factor = factor_ref[...]
    plane = lax.axis_index("narrow")
    for k, part in enumerate(raw):
        core = dot_full(part[...], factor, NT)
        if k == 0:
            own_ref[...] = core
        place = pl.multiple_of(jnp.bitwise_xor(plane, k) * size, size)
        all_ref[pl.ds(place, size), :] = core
    own = [own_ref[pl.ds(k, cells_two, stride=cells_three), :] for k in range(cells_three)]
    every = [
        jnp.concatenate(
            [all_ref[pl.ds(size * q + k, cells_two, stride=cells_three), :] for q in range(planes)], axis=0
        )
        for k in range(cells_three)
    ]
    out_ref[...] = dot_full(jnp.concatenate(own, axis=1), jnp.concatenate(every, axis=1), NT)


def call(kernel, outs, name, operands, scratch=(), order_only=(), flops=0, dtype=jnp.float32):
    shapes = [jax.ShapeDtypeStruct(shape, dtype) for shape in outs]
    touched = sum(operand.size for operand in operands) + sum(shape.size for shape in shapes)
    result = pl.pallas_call(
        kernel,
        out_shape=shapes,
        in_specs=[pl.BlockSpec(memory_space=pl.ANY)] * len(order_only) + [VMEM] * len(operands),
        out_specs=[VMEM] * len(shapes),
        scratch_shapes=list(scratch),
        compiler_params=pltpu.CompilerParams(vmem_limit_bytes=32 * 2**20),
        cost_estimate=pl.CostEstimate(flops=flops, bytes_accessed=4 * touched, transcendentals=0),
        name=name,
    )(*order_only, *operands)
    return result if len(outs) > 1 else result[0]


def swap(array, axis, mask):
    return lax.ppermute(array, axis, [(i, i ^ mask) for i in range(lax.axis_size(axis))])


def shards(field, start_block):
    cells_two, cells_three, order = field.shape
    rank = start_block.shape[1]
    narrow, wide = lax.axis_size("narrow"), lax.axis_size("wide")
    unfolded = field.reshape(cells_two * cells_three, order)
    cells = unfolded.shape[0]
    place = lax.axis_index("wide")
    spread = pltpu.VMEM((2 * PANEL * PANEL, rank), jnp.float32)

    def orthonormal_start(after):
        return call(
            start_kernel,
            [(rank, order)],
            "orth_start",
            [start_block],
            [pltpu.VMEM((rank, rank), jnp.float32), spread],
            order_only=[after],
            flops=10**9,
        )

    def last_factors(image, inner):
        return call(
            last_kernel,
            [(rank, rank)],
            "last_factors",
            [image, inner],
            [pltpu.VMEM((rank, rank), jnp.float32), spread],
            flops=10**9,
        )

    scratch = [
        pltpu.VMEM((order, order), jnp.bfloat16),
        pltpu.VMEM((order, order), jnp.bfloat16),
        pltpu.VMEM((rank, rank), jnp.float32),
        spread,
        pltpu.VMEM((rank, order), jnp.float32),
    ]
    results = [(rank, order), (rank, rank), (cells, rank)]
    blocks = order // BLOCK
    if wide == blocks and narrow & (narrow - 1) == 0 and BLOCK % (8 * narrow) == 0:
        groups = wide // 2
        band = BLOCK * (blocks // 2 + 1)
        extended = (cells, order + band - BLOCK)
        other = swap(unfolded, "wide", 1)
        own = call(split_kernel, [extended] * 2, "split_field", [unfolded], dtype=jnp.bfloat16)
        first_kept, first_sent, second_kept, second_sent = call(
            gram_kernel,
            [(BLOCK, band)] * groups,
            "gram_band",
            [*own, other],
            [pltpu.VMEM((2 * cells, extended[1]), jnp.bfloat16)] * 2,
            flops=10**9,
        )
        first_got, second_got = swap(first_sent, "wide", 2), swap(second_sent, "wide", 4)
        basis = orthonormal_start(first_kept)
        first, first_sent, second, second_sent = call(
            halve_kernel,
            [(BLOCK // 2, band)] * 4,
            "sum_pairs",
            [first_kept, first_got, second_kept, second_got],
            order_only=[basis],
        )
        cuts = call(
            cut_kernel,
            [(BLOCK // narrow, band)] * narrow,
            "sum_groups",
            [first, swap(first_sent, "wide", 4), second, swap(second_sent, "wide", 2)],
        )
        arrived = [swap(cuts[k], "narrow", k) for k in range(1, narrow)]
        piece = call(add_kernel, [(BLOCK // narrow, band)], "sum_planes", [cuts[0], *arrived])
        arrived = [swap(piece, "narrow", k) for k in range(1, narrow)]
        first, second = call(
            join_kernel,
            [(BLOCK // 2, band)] * 2,
            "join_planes",
            [piece, *arrived],
        )
        stacks = call(
            stack_kernel,
            [(BLOCK, band)] * 2,
            "stack_pairs",
            [first, swap(first, "wide", 4), second, swap(second, "wide", 2)],
        )
        stacks = [*stacks, swap(stacks[0], "wide", 2), swap(stacks[1], "wide", 4)]
        bands = stacks + [swap(stack, "wide", 1) for stack in stacks]
        image, inner, raw = call(
            functools.partial(banded_kernel, blocks),
            results,
            "sweeps",
            [basis, unfolded, *bands],
            scratch,
        )
        raws = [raw] + [swap(raw, "narrow", k) for k in range(1, narrow)]
        factor = last_factors(image, inner)
        total = call(
            functools.partial(tail_kernel, cells_three),
            [(cells_two, narrow * cells_two)],
            "core_pairs",
            [factor, *raws],
            [pltpu.VMEM((cells, rank), jnp.float32), pltpu.VMEM((narrow * cells, rank), jnp.float32)],
        )
        total = add_pairs([total] + [swap(total, "wide", k) for k in range(1, 4)])
        total = total + swap(total, "wide", 4)
        columns = narrow * cells_two // wide
        finished = lax.dynamic_slice_in_dim(total, place * columns, columns, 1)
    else:
        basis = orthonormal_start(start_block)
        gram = lax.dot_general(unfolded, unfolded, (((0,), (0,)), ((), ())), precision=HIGHEST)
        gram = lax.psum(gram, ("narrow", "wide"))
        image, inner, raw = call(whole_kernel, results, "sweeps", [basis, unfolded, gram], scratch)
        core = lax.dot_general(raw, last_factors(image, inner), NT, precision=HIGHEST)
        merged = core.reshape(cells_two, cells_three * rank)
        everyone = lax.all_gather(merged, "narrow", axis=0, tiled=True)
        part = lax.dot_general(merged, everyone, NT, precision=HIGHEST)
        finished = lax.psum_scatter(part, "wide", scatter_dimension=1, tiled=True)
    return finished / (rank * cells_three * wide)


def solution(mesh):
    return jax.shard_map(
        shards,
        mesh=mesh,
        in_specs=(P("narrow", "wide", None), P()),
        out_specs=P("narrow", "wide"),
        check_vma=False,
    )
```

time: 103 us -> 94.8 us (0.920)
  waiting for transfers between devices: 42.5 us -> 35.9 us
    ppermute x23 -> x26, waiting for transfers between devices: 42.5 us -> 35.9 us  [swap(): lax.ppermute(array, axis, [(i, i ^ mask) for i in range(lax.axis_size(axi...]
    pallas_call x8 -> x11, Pallas kernels: 30.2 us -> 29.3 us  [call(): pl.pallas_call(kernel, out_shape=shapes, in_specs=[pl.BlockSpec(memory_sp...]
    ppermute x23 -> x26, starting transfers between devices: 27.8 us -> 27.5 us  [swap(): lax.ppermute(array, axis, [(i, i ^ mask) for i in range(lax.axis_size(axi...]
  transfers between devices with their start and end apart: 23 -> 26, of which waited for: 14 -> 18; matrix products, arithmetic and copies ran while one was open for 0% -> 0% of each run, Pallas kernels for 23% -> 14%
where the time goes in v3:
time: 94.8 us; the launch traced here: 94.6 us
  waiting for transfers between devices  35.9 us (38%)
  Pallas kernels  29.3 us (31%)
  starting transfers between devices  27.5 us (29%)
  local copies, waits for them, and re-layouts  1.71 us (2%)
    ppermute x26, waiting for transfers between devices, swap(): lax.ppermute(array, axis, [(i, i ^ mask) for i in range(lax.axis_size(axi...  35.9 us
    pallas_call x11, Pallas kernels, call(): pl.pallas_call(kernel, out_shape=shapes, in_specs=[pl.BlockSpec(memory_sp...  29.3 us
    ppermute x26, starting transfers between devices, swap(): lax.ppermute(array, axis, [(i, i ^ mask) for i in range(lax.axis_size(axi...  27.5 us
  transfers between devices with their start and end apart: 26, of which 18 were waited for; matrix products, arithmetic and copies ran while one was open for 0% of the time, Pallas kernels for 14%

profile of v3, /device:TPU:0, one launch (start us, length us, event | category | flops | bytes accessed | tf_op | source)
XLA Modules:
  0.0 94.6 jit_solution(5892476071180102689)
XLA Ops:
  0.0 0.5 collective-permute-start
  0.5 1.0 %copy-done = f32[8,16,1024]{2,1,0:T(8,128)S(1)} copy-done((f32[8,16,1024]{2,1,0:T(8,128)S(1)}, f32[8,16,1024]{2,1,0:T(8,128)}, u32[]{:S(2)}) %copy-start) | copy-done | bytes 524312
  1.5 0.1 split_field.1
  1.6 0.6 collective-permute-done.other_ref
  2.2 1.0 %gram_band.1 = (f32[128,640]{1,0:T(8,128)S(1)}, f32[128,640]{1,0:T(8,128)S(1)}, f32[128,640]{1,0:T(8,128)S(1)}, f32[128,640]{1,0:T(8,128)S(1)}) custom-call(bf16[128,1536]{1,0:T(8,128)(2,1)S(1)} %get-tuple-element.26.own_high, bf16[128,1536]{1,0:T(8,128)(2,1)S(1)} %get-tuple-element.27.own_low, f32[128,1024]{1,0:T(8,128)S(1)} %collective-permute-done.other_ref), custom_call_target="tpu_custom_call" | custom-call | flops 1000000000 | bytes 3407872 | tf_op jit(solution)/shard_map/gram_band/pallas_call | solution.py:273
  3.2 2.9 %collective-permute-start.1 = (f32[128,640]{1,0:T(8,128)S(1)}, f32[128,640]{1,0:T(8,128)S(1)}, u32[]{:S(2)}, u32[]{:S(2)}) collective-permute-start(f32[128,640]{1,0:T(8,128)S(1)} %get-tuple-element.29), channel_id=1, source_target_pairs={{0,2},{1,3},{2,0},{3,1},{4,6},{5,7},{6,4},{7,5},{8,10},{9,11},{10,... | collective-permute-start | bytes 983048 | tf_op jit(solution)/shard_map/ppermute | solution.py:287
  6.1 1.5 %collective-permute-start.2 = (f32[128,640]{1,0:T(8,128)S(1)}, f32[128,640]{1,0:T(8,128)S(1)}, u32[]{:S(2)}, u32[]{:S(2)}) collective-permute-start(f32[128,640]{1,0:T(8,128)S(1)} %get-tuple-element.31), channel_id=1, source_target_pairs={{0,4},{1,5},{2,6},{3,7},{4,0},{5,1},{6,2},{7,3},{8,12},{9,13},{10,... | collective-permute-start | bytes 983048 | tf_op jit(solution)/shard_map/ppermute | solution.py:287
  7.6 5.1 %orth_start.1.after_ref.basis_ref = f32[128,1024]{1,0:T(8,128)S(1)} custom-call(f32[128,640]{1,0:T(8,128)S(1)} %get-tuple-element.28.after_ref.kept_first, f32[1024,128]{1,0:T(8,128)S(1)} %copy-done.2), custom_call_target="tpu_custom_call" | custom-call | flops 1000000000 | bytes 1048576 | tf_op jit(solution)/shard_map/orth_start/pallas_call | solution.py:273
  12.7 1.4 %collective-permute-done.1.got_first = f32[128,640]{1,0:T(8,128)S(1)} collective-permute-done((f32[128,640]{1,0:T(8,128)S(1)}, f32[128,640]{1,0:T(8,128)S(1)}, u32[]{:S(2)}, u32[]{:S(2)}) %collective-permute-start.1) | collective-permute-done | bytes 327712 | tf_op jit(solution)/shard_map/ppermute | solution.py:287
  14.1 1.5 %collective-permute-done.2.got_second = f32[128,640]{1,0:T(8,128)S(1)} collective-permute-done((f32[128,640]{1,0:T(8,128)S(1)}, f32[128,640]{1,0:T(8,128)S(1)}, u32[]{:S(2)}, u32[]{:S(2)}) %collective-permute-start.2) | collective-permute-done | bytes 327712 | tf_op jit(solution)/shard_map/ppermute | solution.py:287
  15.7 1.6 %collective-permute-start.3 = (f32[64,640]{1,0:T(8,128)S(1)}, f32[64,640]{1,0:T(8,128)S(1)}, u32[]{:S(2)}, u32[]{:S(2)}) collective-permute-start(f32[64,640]{1,0:T(8,128)S(1)} %get-tuple-element.33), channel_id=1, source_target_pairs={{0,4},{1,5},{2,6},{3,7},{4,0},{5,1},{6,2},{7,3},{8,12},{9,13},{10,... | collective-permute-start | bytes 491528 | tf_op jit(solution)/shard_map/ppermute | solution.py:287
  17.2 0.5 collective-permute-start.4
  17.8 3.3 %collective-permute-done.3.got_first = f32[64,640]{1,0:T(8,128)S(1)} collective-permute-done((f32[64,640]{1,0:T(8,128)S(1)}, f32[64,640]{1,0:T(8,128)S(1)}, u32[]{:S(2)}, u32[]{:S(2)}) %collective-permute-start.3) | collective-permute-done | bytes 163872 | tf_op jit(solution)/shard_map/ppermute | solution.py:287
  21.0 1.5 %collective-permute-done.4.got_second = f32[64,640]{1,0:T(8,128)S(1)} collective-permute-done((f32[64,640]{1,0:T(8,128)S(1)}, f32[64,640]{1,0:T(8,128)S(1)}, u32[]{:S(2)}, u32[]{:S(2)}) %collective-permute-start.4) | collective-permute-done | bytes 163872 | tf_op jit(solution)/shard_map/ppermute | solution.py:287
  22.6 1.6 %collective-permute-start.5 = (f32[32,640]{1,0:T(8,128)S(1)}, f32[32,640]{1,0:T(8,128)S(1)}, u32[]{:S(2)}, u32[]{:S(2)}) collective-permute-start(f32[32,640]{1,0:T(8,128)S(1)} %get-tuple-element.37), channel_id=1, source_target_pairs={{0,8},{8,0},{16,24},{24,16},{1,9},{9,1},{17,25},{25,17},{2,10},{10... | collective-permute-start | bytes 245768 | tf_op jit(solution)/shard_map/ppermute | solution.py:287
  24.2 2.6 %collective-permute-start.6 = (f32[32,640]{1,0:T(8,128)S(1)}, f32[32,640]{1,0:T(8,128)S(1)}, u32[]{:S(2)}, u32[]{:S(2)}) collective-permute-start(f32[32,640]{1,0:T(8,128)S(1)} %get-tuple-element.38), channel_id=1, source_target_pairs={{0,16},{8,24},{16,0},{24,8},{1,17},{9,25},{17,1},{25,9},{2,18},{10... | collective-permute-start | bytes 245768 | tf_op jit(solution)/shard_map/ppermute | solution.py:287
  26.8 0.2 collective-permute-start.7
  27.1 0.1 collective-permute-done.5.refs_1_
  27.2 4.1 %collective-permute-done.6.refs_2_ = f32[32,640]{1,0:T(8,128)S(1)} collective-permute-done((f32[32,640]{1,0:T(8,128)S(1)}, f32[32,640]{1,0:T(8,128)S(1)}, u32[]{:S(2)}, u32[]{:S(2)}) %collective-permute-start.6) | collective-permute-done | bytes 81952 | tf_op jit(solution)/shard_map/ppermute | solution.py:287
  31.2 1.9 %collective-permute-done.7.refs_3_ = f32[32,640]{1,0:T(8,128)S(1)} collective-permute-done((f32[32,640]{1,0:T(8,128)S(1)}, f32[32,640]{1,0:T(8,128)S(1)}, u32[]{:S(2)}, u32[]{:S(2)}) %collective-permute-start.7) | collective-permute-done | bytes 81952 | tf_op jit(solution)/shard_map/ppermute | solution.py:287
  33.2 0.9 collective-permute-start.10
  34.2 1.3 %collective-permute-start.8 = (f32[32,640]{1,0:T(8,128)S(1)}, f32[32,640]{1,0:T(8,128)S(1)}, u32[]{:S(2)}, u32[]{:S(2)}) collective-permute-start(f32[32,640]{1,0:T(8,128)S(1)} %sum_planes.1.refs_0_), channel_id=1, source_target_pairs={{0,8},{8,0},{16,24},{24,16},{1,9},{9,1},{17,25},{25,17},{2,10},{10... | collective-permute-start | bytes 245768 | tf_op jit(solution)/shard_map/ppermute | solution.py:287
  35.5 2.2 %collective-permute-start.9 = (f32[32,640]{1,0:T(8,128)S(1)}, f32[32,640]{1,0:T(8,128)S(1)}, u32[]{:S(2)}, u32[]{:S(2)}) collective-permute-start(f32[32,640]{1,0:T(8,128)S(1)} %sum_planes.1.refs_0_), channel_id=1, source_target_pairs={{0,16},{8,24},{16,0},{24,8},{1,17},{9,25},{17,1},{25,9},{2,18},{10... | collective-permute-start | bytes 245768 | tf_op jit(solution)/shard_map/ppermute | solution.py:287
  37.7 1.9 %collective-permute-done.10.refs_3_ = f32[32,640]{1,0:T(8,128)S(1)} collective-permute-done((f32[32,640]{1,0:T(8,128)S(1)}, f32[32,640]{1,0:T(8,128)S(1)}, u32[]{:S(2)}, u32[]{:S(2)}) %collective-permute-start.10) | collective-permute-done | bytes 81952 | tf_op jit(solution)/shard_map/ppermute | solution.py:287
  39.5 2.2 %collective-permute-done.9.refs_2_ = f32[32,640]{1,0:T(8,128)S(1)} collective-permute-done((f32[32,640]{1,0:T(8,128)S(1)}, f32[32,640]{1,0:T(8,128)S(1)}, u32[]{:S(2)}, u32[]{:S(2)}) %collective-permute-start.9) | collective-permute-done | bytes 81952 | tf_op jit(solution)/shard_map/ppermute | solution.py:287
  41.8 1.2 %collective-permute-start.12 = (f32[64,640]{1,0:T(8,128)S(1)}, f32[64,640]{1,0:T(8,128)S(1)}, u32[]{:S(2)}, u32[]{:S(2)}) collective-permute-start(f32[64,640]{1,0:T(8,128)S(1)} %get-tuple-element.41.second), channel_id=1, source_target_pairs={{0,2},{1,3},{2,0},{3,1},{4,6},{5,7},{6,4},{7,5},{8,10},{9,11},{10,... | collective-permute-start | bytes 491528 | tf_op jit(solution)/shard_map/ppermute | solution.py:287
  43.0 5.9 %collective-permute-done.11.got_first = f32[64,640]{1,0:T(8,128)S(1)} collective-permute-done((f32[64,640]{1,0:T(8,128)S(1)}, f32[64,640]{1,0:T(8,128)S(1)}, u32[]{:S(2)}, u32[]{:S(2)}) %collective-permute-start.11) | collective-permute-done | bytes 163872 | tf_op jit(solution)/shard_map/ppermute | solution.py:287
  48.9 0.8 collective-permute-start.13
  49.7 1.4 %collective-permute-start.14 = (f32[128,640]{1,0:T(8,128)S(1)}, f32[128,640]{1,0:T(8,128)S(1)}, u32[]{:S(2)}, u32[]{:S(2)}) collective-permute-start(f32[128,640]{1,0:T(8,128)S(1)} %get-tuple-element.43.refs_1_), channel_id=1, source_target_pairs={{0,4},{1,5},{2,6},{3,7},{4,0},{5,1},{6,2},{7,3},{8,12},{9,13},{10,... | collective-permute-start | bytes 983048 | tf_op jit(solution)/shard_map/ppermute | solution.py:287
  51.1 0.5 collective-permute-start.16
  51.6 4.5 %collective-permute-done.13.refs_2_ = f32[128,640]{1,0:T(8,128)S(1)} collective-permute-done((f32[128,640]{1,0:T(8,128)S(1)}, f32[128,640]{1,0:T(8,128)S(1)}, u32[]{:S(2)}, u32[]{:S(2)}) %collective-permute-start.13) | collective-permute-done | bytes 327712 | tf_op jit(solution)/shard_map/ppermute | solution.py:287
  56.1 0.7 collective-permute-done.14.refs_3_
  56.8 0.9 collective-permute-done.17.refs_6_
  57.7 0.7 collective-permute-done.18.refs_7_
  58.4 13.3 %sweeps.1 = (f32[128,1024]{1,0:T(8,128)S(1)}, f32[128,128]{1,0:T(8,128)S(1)}, f32[128,128]{1,0:T(8,128)S(1)}) custom-call(f32[128,1024]{1,0:T(8,128)S(1)} %orth_start.1.after_ref.basis_ref, f32[128,1024]{1,0:T(8,128)S(1)} %bitcast.3, f32[128,640]{1,0:T(8,128)S(1)} %get-tuple-element.42.refs_0_, f32[128,640]{1,0:T(8,128)S(1)} %get-tuple-element.43.refs_1_, ...), custom_call_target="tpu_custom_call" | custom-call | bytes 4325376 | tf_op jit(solution)/shard_map/sweeps/pallas_call | solution.py:273
  71.7 0.6 collective-permute-start.19
  72.3 1.5 %collective-permute-start.20 = (f32[128,128]{1,0:T(8,128)S(1)}, f32[128,128]{1,0:T(8,128)S(1)}, u32[]{:S(2)}, u32[]{:S(2)}) collective-permute-start(f32[128,128]{1,0:T(8,128)S(1)} %get-tuple-element.46.refs_0_), channel_id=1, source_target_pairs={{0,16},{8,24},{16,0},{24,8},{1,17},{9,25},{17,1},{25,9},{2,18},{10... | collective-permute-start | bytes 196616 | tf_op jit(solution)/shard_map/ppermute | solution.py:287
  73.8 2.3 %collective-permute-start.21 = (f32[128,128]{1,0:T(8,128)S(1)}, f32[128,128]{1,0:T(8,128)S(1)}, u32[]{:S(2)}, u32[]{:S(2)}) collective-permute-start(f32[128,128]{1,0:T(8,128)S(1)} %get-tuple-element.46.refs_0_), channel_id=1, source_target_pairs={{0,24},{8,16},{16,8},{24,0},{1,25},{9,17},{17,9},{25,1},{2,26},{10... | collective-permute-start | bytes 196616 | tf_op jit(solution)/shard_map/ppermute | solution.py:287
  76.2 8.4 %last_factors.1.factor_ref = f32[128,128]{1,0:T(8,128)S(1)} custom-call(f32[128,1024]{1,0:T(8,128)S(1)} %get-tuple-element.44.image_ref, f32[128,128]{1,0:T(8,128)S(1)} %get-tuple-element.45.inner_ref), custom_call_target="tpu_custom_call" | custom-call | flops 1000000000 | bytes 655360 | tf_op jit(solution)/shard_map/last_factors/pallas_call | solution.py:273
  84.6 1.3 %core_pairs.1 = f32[8,32]{1,0:T(8,128)S(1)} custom-call(f32[128,128]{1,0:T(8,128)S(1)} %last_factors.1.factor_ref, f32[128,128]{1,0:T(8,128)S(1)} %get-tuple-element.46.refs_0_, f32[128,128]{1,0:T(8,128)S(1)} %collective-permute-done.19.refs_1_, f32[128,128]{1,0:T(8,128)S(1)} %collective-permute-done.20.refs_2_, f32[128,128]{1,0:T(8,128)S(1)} %collective-permute-done.21.refs_3_), custom_call_target="tpu_custom_call" | custom-call | bytes 328704 | tf_op jit(solution)/shard_map/core_pairs/pallas_call | solution.py:273
  85.9 1.4 %collective-permute-start.23 = (f32[8,32]{1,0:T(8,128)S(1)}, f32[8,32]{1,0:T(8,128)S(1)}, u32[]{:S(2)}, u32[]{:S(2)}) collective-permute-start(f32[8,32]{1,0:T(8,128)S(1)} %core_pairs.1), channel_id=1, source_target_pairs={{0,2},{1,3},{2,0},{3,1},{4,6},{5,7},{6,4},{7,5},{8,10},{9,11},{10,... | collective-permute-start | bytes 3080 | tf_op jit(solution)/shard_map/ppermute | solution.py:287
  87.2 0.5 collective-permute-start.24
  87.8 1.8 %collective-permute-done.23 = f32[8,32]{1,0:T(8,128)S(1)} collective-permute-done((f32[8,32]{1,0:T(8,128)S(1)}, f32[8,32]{1,0:T(8,128)S(1)}, u32[]{:S(2)}, u32[]{:S(2)}) %collective-permute-start.23) | collective-permute-done | bytes 1056 | tf_op jit(solution)/shard_map/ppermute | solution.py:287
  89.5 0.7 collective-permute-done.24
  90.3 1.4 %collective-permute-start.25 = (f32[8,32]{1,0:T(8,128)S(1)}, f32[8,32]{1,0:T(8,128)S(1)}, u32[]{:S(2)}, u32[]{:S(2)}) collective-permute-start(f32[8,32]{1,0:T(8,128)S(1)} %add_add_fusion), channel_id=1, source_target_pairs={{0,4},{1,5},{2,6},{3,7},{4,0},{5,1},{6,2},{7,3},{8,12},{9,13},{10,... | collective-permute-start | bytes 3080 | tf_op jit(solution)/shard_map/ppermute | solution.py:287
  91.6 2.3 %collective-permute-done.25 = f32[8,32]{1,0:T(8,128)S(1)} collective-permute-done((f32[8,32]{1,0:T(8,128)S(1)}, f32[8,32]{1,0:T(8,128)S(1)}, u32[]{:S(2)}, u32[]{:S(2)}) %collective-permute-start.25) | collective-permute-done | bytes 1056 | tf_op jit(solution)/shard_map/ppermute | solution.py:287
  93.9 0.1 dynamic-slice_multiply_fusion
  94.0 0.7 copy.3
  (25 shorter events, 0.3 us)
Async XLA Ops:
  0.0 2.2 %collective-permute-start = (f32[128,1024]{1,0:T(8,128)}, f32[128,1024]{1,0:T(8,128)S(1)}, u32[]{:S(2)}, u32[]{:S(2)}) collective-permute-start(f32[128,1024]{1,0:T(8,128)} %bitcast.1), channel_id=1, source_target_pairs={{0,1},{1,0},{2,3},{3,2},{4,5},{5,4},{6,7},{7,6},{8,9},{9,8},{10,11... | collective-permute-start | bytes 1572872 | tf_op jit(solution)/shard_map/ppermute | solution.py:287
  0.5 1.0 %copy-start = (f32[8,16,1024]{2,1,0:T(8,128)S(1)}, f32[8,16,1024]{2,1,0:T(8,128)}, u32[]{:S(2)}) copy-start(f32[8,16,1024]{2,1,0:T(8,128)} %param.2) | copy-start | bytes 1572868
  2.2 5.4 %copy-start.2 = (f32[1024,128]{1,0:T(8,128)S(1)}, f32[1024,128]{1,0:T(8,128)}, u32[]{:S(2)}) copy-start(f32[1024,128]{1,0:T(8,128)} %start_ref.1) | copy-start | bytes 1572868
  3.2 10.9 %collective-permute-start.1 = (f32[128,640]{1,0:T(8,128)S(1)}, f32[128,640]{1,0:T(8,128)S(1)}, u32[]{:S(2)}, u32[]{:S(2)}) collective-permute-start(f32[128,640]{1,0:T(8,128)S(1)} %get-tuple-element.29), channel_id=1, source_target_pairs={{0,2},{1,3},{2,0},{3,1},{4,6},{5,7},{6,4},{7,5},{8,10},{9,11},{10,... | collective-permute-start | bytes 983048 | tf_op jit(solution)/shard_map/ppermute | solution.py:287
  6.1 9.5 %collective-permute-start.2 = (f32[128,640]{1,0:T(8,128)S(1)}, f32[128,640]{1,0:T(8,128)S(1)}, u32[]{:S(2)}, u32[]{:S(2)}) collective-permute-start(f32[128,640]{1,0:T(8,128)S(1)} %get-tuple-element.31), channel_id=1, source_target_pairs={{0,4},{1,5},{2,6},{3,7},{4,0},{5,1},{6,2},{7,3},{8,12},{9,13},{10,... | collective-permute-start | bytes 983048 | tf_op jit(solution)/shard_map/ppermute | solution.py:287
  15.7 5.4 %collective-permute-start.3 = (f32[64,640]{1,0:T(8,128)S(1)}, f32[64,640]{1,0:T(8,128)S(1)}, u32[]{:S(2)}, u32[]{:S(2)}) collective-permute-start(f32[64,640]{1,0:T(8,128)S(1)} %get-tuple-element.33), channel_id=1, source_target_pairs={{0,4},{1,5},{2,6},{3,7},{4,0},{5,1},{6,2},{7,3},{8,12},{9,13},{10,... | collective-permute-start | bytes 491528 | tf_op jit(solution)/shard_map/ppermute | solution.py:287
  17.2 5.3 %collective-permute-start.4 = (f32[64,640]{1,0:T(8,128)S(1)}, f32[64,640]{1,0:T(8,128)S(1)}, u32[]{:S(2)}, u32[]{:S(2)}) collective-permute-start(f32[64,640]{1,0:T(8,128)S(1)} %get-tuple-element.35), channel_id=1, source_target_pairs={{0,2},{1,3},{2,0},{3,1},{4,6},{5,7},{6,4},{7,5},{8,10},{9,11},{10,... | collective-permute-start | bytes 491528 | tf_op jit(solution)/shard_map/ppermute | solution.py:287
  22.6 4.6 %collective-permute-start.5 = (f32[32,640]{1,0:T(8,128)S(1)}, f32[32,640]{1,0:T(8,128)S(1)}, u32[]{:S(2)}, u32[]{:S(2)}) collective-permute-start(f32[32,640]{1,0:T(8,128)S(1)} %get-tuple-element.37), channel_id=1, source_target_pairs={{0,8},{8,0},{16,24},{24,16},{1,9},{9,1},{17,25},{25,17},{2,10},{10... | collective-permute-start | bytes 245768 | tf_op jit(solution)/shard_map/ppermute | solution.py:287
  24.2 7.0 %collective-permute-start.6 = (f32[32,640]{1,0:T(8,128)S(1)}, f32[32,640]{1,0:T(8,128)S(1)}, u32[]{:S(2)}, u32[]{:S(2)}) collective-permute-start(f32[32,640]{1,0:T(8,128)S(1)} %get-tuple-element.38), channel_id=1, source_target_pairs={{0,16},{8,24},{16,0},{24,8},{1,17},{9,25},{17,1},{25,9},{2,18},{10... | collective-permute-start | bytes 245768 | tf_op jit(solution)/shard_map/ppermute | solution.py:287
  26.8 6.3 %collective-permute-start.7 = (f32[32,640]{1,0:T(8,128)S(1)}, f32[32,640]{1,0:T(8,128)S(1)}, u32[]{:S(2)}, u32[]{:S(2)}) collective-permute-start(f32[32,640]{1,0:T(8,128)S(1)} %get-tuple-element.39), channel_id=1, source_target_pairs={{0,24},{8,16},{16,8},{24,0},{1,25},{9,17},{17,9},{25,1},{2,26},{10... | collective-permute-start | bytes 245768 | tf_op jit(solution)/shard_map/ppermute | solution.py:287
  33.2 25.2 %copy-start.1 = (f32[8,16,1024]{2,1,0:T(8,128)S(1)}, f32[8,16,1024]{2,1,0:T(8,128)}, u32[]{:S(2)}) copy-start(f32[8,16,1024]{2,1,0:T(8,128)} %param.2) | copy-start | bytes 1572868
  33.2 6.3 %collective-permute-start.10 = (f32[32,640]{1,0:T(8,128)S(1)}, f32[32,640]{1,0:T(8,128)S(1)}, u32[]{:S(2)}, u32[]{:S(2)}) collective-permute-start(f32[32,640]{1,0:T(8,128)S(1)} %sum_planes.1.refs_0_), channel_id=1, source_target_pairs={{0,24},{8,16},{16,8},{24,0},{1,25},{9,17},{17,9},{25,1},{2,26},{10... | collective-permute-start | bytes 245768 | tf_op jit(solution)/shard_map/ppermute | solution.py:287
  34.2 5.4 %collective-permute-start.8 = (f32[32,640]{1,0:T(8,128)S(1)}, f32[32,640]{1,0:T(8,128)S(1)}, u32[]{:S(2)}, u32[]{:S(2)}) collective-permute-start(f32[32,640]{1,0:T(8,128)S(1)} %sum_planes.1.refs_0_), channel_id=1, source_target_pairs={{0,8},{8,0},{16,24},{24,16},{1,9},{9,1},{17,25},{25,17},{2,10},{10... | collective-permute-start | bytes 245768 | tf_op jit(solution)/shard_map/ppermute | solution.py:287
  35.5 6.2 %collective-permute-start.9 = (f32[32,640]{1,0:T(8,128)S(1)}, f32[32,640]{1,0:T(8,128)S(1)}, u32[]{:S(2)}, u32[]{:S(2)}) collective-permute-start(f32[32,640]{1,0:T(8,128)S(1)} %sum_planes.1.refs_0_), channel_id=1, source_target_pairs={{0,16},{8,24},{16,0},{24,8},{1,17},{9,25},{17,1},{25,9},{2,18},{10... | collective-permute-start | bytes 245768 | tf_op jit(solution)/shard_map/ppermute | solution.py:287
  41.7 7.2 %collective-permute-start.11 = (f32[64,640]{1,0:T(8,128)S(1)}, f32[64,640]{1,0:T(8,128)S(1)}, u32[]{:S(2)}, u32[]{:S(2)}) collective-permute-start(f32[64,640]{1,0:T(8,128)S(1)} %get-tuple-element.40.first), channel_id=1, source_target_pairs={{0,4},{1,5},{2,6},{3,7},{4,0},{5,1},{6,2},{7,3},{8,12},{9,13},{10,... | collective-permute-start | bytes 491528 | tf_op jit(solution)/shard_map/ppermute | solution.py:287
  41.8 7.1 %collective-permute-start.12 = (f32[64,640]{1,0:T(8,128)S(1)}, f32[64,640]{1,0:T(8,128)S(1)}, u32[]{:S(2)}, u32[]{:S(2)}) collective-permute-start(f32[64,640]{1,0:T(8,128)S(1)} %get-tuple-element.41.second), channel_id=1, source_target_pairs={{0,2},{1,3},{2,0},{3,1},{4,6},{5,7},{6,4},{7,5},{8,10},{9,11},{10,... | collective-permute-start | bytes 491528 | tf_op jit(solution)/shard_map/ppermute | solution.py:287
  48.9 7.1 %collective-permute-start.13 = (f32[128,640]{1,0:T(8,128)S(1)}, f32[128,640]{1,0:T(8,128)S(1)}, u32[]{:S(2)}, u32[]{:S(2)}) collective-permute-start(f32[128,640]{1,0:T(8,128)S(1)} %get-tuple-element.42.refs_0_), channel_id=1, source_target_pairs={{0,2},{1,3},{2,0},{3,1},{4,6},{5,7},{6,4},{7,5},{8,10},{9,11},{10,... | collective-permute-start | bytes 983048 | tf_op jit(solution)/shard_map/ppermute | solution.py:287
  49.7 7.1 %collective-permute-start.14 = (f32[128,640]{1,0:T(8,128)S(1)}, f32[128,640]{1,0:T(8,128)S(1)}, u32[]{:S(2)}, u32[]{:S(2)}) collective-permute-start(f32[128,640]{1,0:T(8,128)S(1)} %get-tuple-element.43.refs_1_), channel_id=1, source_target_pairs={{0,4},{1,5},{2,6},{3,7},{4,0},{5,1},{6,2},{7,3},{8,12},{9,13},{10,... | collective-permute-start | bytes 983048 | tf_op jit(solution)/shard_map/ppermute | solution.py:287
  51.1 5.7 %collective-permute-start.15 = (f32[128,640]{1,0:T(8,128)S(1)}, f32[128,640]{1,0:T(8,128)S(1)}, u32[]{:S(2)}, u32[]{:S(2)}) collective-permute-start(f32[128,640]{1,0:T(8,128)S(1)} %get-tuple-element.42.refs_0_), channel_id=1, source_target_pairs={{0,1},{1,0},{2,3},{3,2},{4,5},{5,4},{6,7},{7,6},{8,9},{9,8},{10,11... | collective-permute-start | bytes 983048 | tf_op jit(solution)/shard_map/ppermute | solution.py:287
  51.1 5.7 %collective-permute-start.16 = (f32[128,640]{1,0:T(8,128)S(1)}, f32[128,640]{1,0:T(8,128)S(1)}, u32[]{:S(2)}, u32[]{:S(2)}) collective-permute-start(f32[128,640]{1,0:T(8,128)S(1)} %get-tuple-element.43.refs_1_), channel_id=1, source_target_pairs={{0,1},{1,0},{2,3},{3,2},{4,5},{5,4},{6,7},{7,6},{8,9},{9,8},{10,11... | collective-permute-start | bytes 983048 | tf_op jit(solution)/shard_map/ppermute | solution.py:287
  56.1 1.6 %collective-permute-start.17 = (f32[128,640]{1,0:T(8,128)S(1)}, f32[128,640]{1,0:T(8,128)S(1)}, u32[]{:S(2)}, u32[]{:S(2)}) collective-permute-start(f32[128,640]{1,0:T(8,128)S(1)} %collective-permute-done.13.refs_2_), channel_id=1, source_target_pairs={{0,1},{1,0},{2,3},{3,2},{4,5},{5,4},{6,7},{7,6},{8,9},{9,8},{10,11... | collective-permute-start | bytes 983048 | tf_op jit(solution)/shard_map/ppermute | solution.py:287
  56.8 1.6 %collective-permute-start.18 = (f32[128,640]{1,0:T(8,128)S(1)}, f32[128,640]{1,0:T(8,128)S(1)}, u32[]{:S(2)}, u32[]{:S(2)}) collective-permute-start(f32[128,640]{1,0:T(8,128)S(1)} %collective-permute-done.14.refs_3_), channel_id=1, source_target_pairs={{0,1},{1,0},{2,3},{3,2},{4,5},{5,4},{6,7},{7,6},{8,9},{9,8},{10,11... | collective-permute-start | bytes 983048 | tf_op jit(solution)/shard_map/ppermute | solution.py:287
  71.7 12.9 %collective-permute-start.19 = (f32[128,128]{1,0:T(8,128)S(1)}, f32[128,128]{1,0:T(8,128)S(1)}, u32[]{:S(2)}, u32[]{:S(2)}) collective-permute-start(f32[128,128]{1,0:T(8,128)S(1)} %get-tuple-element.46.refs_0_), channel_id=1, source_target_pairs={{0,8},{8,0},{16,24},{24,16},{1,9},{9,1},{17,25},{25,17},{2,10},{10... | collective-permute-start | bytes 196616 | tf_op jit(solution)/shard_map/ppermute | solution.py:287
  72.3 12.3 %collective-permute-start.20 = (f32[128,128]{1,0:T(8,128)S(1)}, f32[128,128]{1,0:T(8,128)S(1)}, u32[]{:S(2)}, u32[]{:S(2)}) collective-permute-start(f32[128,128]{1,0:T(8,128)S(1)} %get-tuple-element.46.refs_0_), channel_id=1, source_target_pairs={{0,16},{8,24},{16,0},{24,8},{1,17},{9,25},{17,1},{25,9},{2,18},{10... | collective-permute-start | bytes 196616 | tf_op jit(solution)/shard_map/ppermute | solution.py:287
  73.8 10.8 %collective-permute-start.21 = (f32[128,128]{1,0:T(8,128)S(1)}, f32[128,128]{1,0:T(8,128)S(1)}, u32[]{:S(2)}, u32[]{:S(2)}) collective-permute-start(f32[128,128]{1,0:T(8,128)S(1)} %get-tuple-element.46.refs_0_), channel_id=1, source_target_pairs={{0,24},{8,16},{16,8},{24,0},{1,25},{9,17},{17,9},{25,1},{2,26},{10... | collective-permute-start | bytes 196616 | tf_op jit(solution)/shard_map/ppermute | solution.py:287
  85.9 1.9 %collective-permute-start.22 = (f32[8,32]{1,0:T(8,128)S(1)}, f32[8,32]{1,0:T(8,128)S(1)}, u32[]{:S(2)}, u32[]{:S(2)}) collective-permute-start(f32[8,32]{1,0:T(8,128)S(1)} %core_pairs.1), channel_id=1, source_target_pairs={{0,1},{1,0},{2,3},{3,2},{4,5},{5,4},{6,7},{7,6},{8,9},{9,8},{10,11... | collective-permute-start | bytes 3080 | tf_op jit(solution)/shard_map/ppermute | solution.py:287
  85.9 3.6 %collective-permute-start.23 = (f32[8,32]{1,0:T(8,128)S(1)}, f32[8,32]{1,0:T(8,128)S(1)}, u32[]{:S(2)}, u32[]{:S(2)}) collective-permute-start(f32[8,32]{1,0:T(8,128)S(1)} %core_pairs.1), channel_id=1, source_target_pairs={{0,2},{1,3},{2,0},{3,1},{4,6},{5,7},{6,4},{7,5},{8,10},{9,11},{10,... | collective-permute-start | bytes 3080 | tf_op jit(solution)/shard_map/ppermute | solution.py:287
  87.2 3.0 %collective-permute-start.24 = (f32[8,32]{1,0:T(8,128)S(1)}, f32[8,32]{1,0:T(8,128)S(1)}, u32[]{:S(2)}, u32[]{:S(2)}) collective-permute-start(f32[8,32]{1,0:T(8,128)S(1)} %core_pairs.1), channel_id=1, source_target_pairs={{0,3},{1,2},{2,1},{3,0},{4,7},{5,6},{6,5},{7,4},{8,11},{9,10},{10,... | collective-permute-start | bytes 3080 | tf_op jit(solution)/shard_map/ppermute | solution.py:287
  90.3 3.6 %collective-permute-start.25 = (f32[8,32]{1,0:T(8,128)S(1)}, f32[8,32]{1,0:T(8,128)S(1)}, u32[]{:S(2)}, u32[]{:S(2)}) collective-permute-start(f32[8,32]{1,0:T(8,128)S(1)} %add_add_fusion), channel_id=1, source_target_pairs={{0,4},{1,5},{2,6},{3,7},{4,0},{5,1},{6,2},{7,3},{8,12},{9,13},{10,... | collective-permute-start | bytes 3080 | tf_op jit(solution)/shard_map/ppermute | solution.py:287

commit v4 on v3

--- a/solution.py
+++ b/solution.py
@@ -121,8 +121,8 @@
 
 
 def gram_kernel(own_high, own_low, other_ref, *refs):
-    outs, (high_ref, low_ref) = refs[:-2], refs[-2:]
-    band = outs[0].shape[1]
+    outs, (high_ref, low_ref, corner_ref) = refs[:-3], refs[-3:]
+    half, band = outs[0].shape[0] // 2, outs[0].shape[1]
     rows, order = other_ref.shape
     extra = high_ref.shape[1] - order
     for own, target, values in zip((own_high, own_low), (high_ref, low_ref), split(other_ref[...])):
@@ -130,17 +130,27 @@
         target[rows : 2 * rows, 0:order] = values
         target[rows : 2 * rows, order : order + extra] = values[:, :extra]
     group, core = chip_and_core()
-    half = BLOCK // 2
     first_keep, first_send, second_keep, second_send = outs
     upper = [first_keep, first_send, first_keep, first_send]
     lower = [second_keep, second_keep, second_send, second_send]
+    opposite = order // 2 // BLOCK
+
+    def product(left_block, right_block, width):
+        first = pl.multiple_of(left_block * BLOCK, BLOCK)
+        second = pl.multiple_of(right_block * BLOCK, BLOCK)
+        left = [ref[:, pl.ds(first, BLOCK)].astype(jnp.float32).T.astype(jnp.bfloat16) for ref in (high_ref, low_ref)]
+        return dot_split(left, [ref[:, pl.ds(second, width)] for ref in (high_ref, low_ref)], NN)
+
     for k in range(len(outs)):
-        first = pl.multiple_of((2 * jnp.bitwise_xor(group, k) + core) * BLOCK, BLOCK)
-        left = [ref[:, pl.ds(first, BLOCK)].astype(jnp.float32).T.astype(jnp.bfloat16) for ref in (high_ref, low_ref)]
-        right = [ref[:, pl.ds(first, band)] for ref in (high_ref, low_ref)]
-        rows = dot_split(left, right, NN)
-        upper[k][half * (k // 2) : half * (k // 2 + 1), :] = rows[:half]
-        lower[k][half * (k % 2) : half * (k % 2 + 1), :] = rows[half:]
+        block = 2 * jnp.bitwise_xor(group, k) + core
+        corner = lax.rem(block, opposite)
+        corner_ref[...] = product(corner, corner + opposite, BLOCK)
+        part = corner_ref[pl.ds(pl.multiple_of(block // opposite * (BLOCK // 2), BLOCK // 2), BLOCK // 2), :]
+        pieces = BLOCK * BLOCK // 2 // band
+        part = jnp.concatenate([part[pieces * i : pieces * (i + 1), :] for i in range(band // BLOCK)], axis=1)
+        whole = jnp.concatenate([product(block, block, band), part], axis=0)
+        upper[k][half * (k // 2) : half * (k // 2 + 1), :] = whole[:half]
+        lower[k][half * (k % 2) : half * (k % 2 + 1), :] = whole[half:]
 
 
 def halve_kernel(after_ref, kept_first, got_first, kept_second, got_second, *outs):
@@ -152,12 +162,12 @@
 
 
 def cut_kernel(first, got_first, second, got_second, *outs):
-    rows = outs[0].shape[0] // 2
+    rows, columns = first.shape[0], outs[0].shape[1]
     plane = lax.axis_index("narrow")
     for k, out in enumerate(outs):
-        piece = pl.ds(pl.multiple_of(jnp.bitwise_xor(plane, k) * rows, rows), rows)
-        out[:rows, :] = first[piece, :] + got_first[piece, :]
-        out[rows:, :] = second[piece, :] + got_second[piece, :]
+        piece = pl.ds(pl.multiple_of(jnp.bitwise_xor(plane, k) * columns, columns), columns)
+        out[:rows, :] = first[:, piece] + got_first[:, piece]
+        out[rows:, :] = second[:, piece] + got_second[:, piece]
 
 
 def add_kernel(*refs):
@@ -169,12 +179,12 @@
 
 def join_kernel(*refs):
     pieces, (first, second) = refs[:-2], refs[-2:]
-    rows = pieces[0].shape[0] // 2
+    rows, columns = first.shape[0], pieces[0].shape[1]
     plane = lax.axis_index("narrow")
     for k, piece in enumerate(pieces):
-        place = pl.ds(pl.multiple_of(jnp.bitwise_xor(plane, k) * rows, rows), rows)
-        first[place, :] = piece[:rows, :]
-        second[place, :] = piece[rows:, :]
+        place = pl.ds(pl.multiple_of(jnp.bitwise_xor(plane, k) * columns, columns), columns)
+        first[:, place] = piece[:rows, :]
+        second[:, place] = piece[rows:, :]
 
 
 def stack_kernel(first, got_first, second, got_second, first_out, second_out):
@@ -184,58 +194,73 @@
         out[half:, :] = got[...]
 
 
-def sweeps(basis_ref, field_ref, image_ref, inner_ref, raw_ref, high_ref, low_ref, factor_ref, spread_ref, basis_scratch):
+def sweeps(basis_ref, field_ref, image_ref, factor_ref, raw_ref, high_ref, low_ref, spread_ref, basis_scratch):
     def times_gram(rows):
         return dot_split(split(rows), (high_ref[...], low_ref[...]), NN)
 
-    def body(step, carry):
-        image = basis_scratch[...]
+    def step(image):
         halves = split(image)
         inner = dot_split(halves, halves, NT)
         following = times_gram(image)
         inverse_factor(inner, factor_ref, spread_ref)
+        return following
+
+    def body(number, carry):
+        following = step(basis_scratch[...])
         basis_scratch[...] = dot_split(split(factor_ref[...]), split(following), NN)
         return carry
 
     basis_scratch[...] = times_gram(basis_ref[...])
     lax.fori_loop(0, ITERS - 2, body, 0)
     image = basis_scratch[...]
+    inner = dot_full(image, image, NT)
     following = times_gram(image)
     image_ref[...] = following
-    inner_ref[...] = dot_full(image, image, NT)
     raw_ref[...] = dot_full(field_ref[...], following, NT)
-
-
-def last_kernel(image_ref, inner_ref, out_ref, factor_ref, spread_ref):
-    inverse_factor(inner_ref[...], factor_ref, spread_ref)
-    before = factor_ref[...]
+    inverse_factor(inner, factor_ref, spread_ref)
+
+
+def last_kernel(image_ref, before_ref, out_ref, factor_ref, spread_ref):
+    before = before_ref[...]
     image = dot_full(before, image_ref[...], NN)
     inverse_factor(dot_full(image, image, NT), factor_ref, spread_ref)
     out_ref[...] = dot_full(factor_ref[...], before, NN)
 
 
 def banded_kernel(blocks, basis_ref, field_ref, *refs):
-    bands, rest = refs[:-8], refs[-8:]
+    bands, rest = refs[:-7], refs[-7:]
     high_ref, low_ref = rest[3:5]
     group, core = chip_and_core()
-    half = BLOCK // 2
+    opposite = blocks // 2
+
+    def store(row, column, part, mirror):
+        rows = pl.ds(pl.multiple_of(row * BLOCK, BLOCK), BLOCK)
+        columns = pl.ds(pl.multiple_of(column * BLOCK, BLOCK), BLOCK)
+        high_ref[rows, columns], low_ref[rows, columns] = split(part)
+        if mirror:
+            high_ref[columns, rows], low_ref[columns, rows] = split(part.T)
+
     halves = {0: ((0, 0), (1, 0)), 1: ((2, 0), (1, 1)), 2: ((0, 1), (3, 0)), 3: ((2, 1), (3, 1))}
-    for place in range(2 * len(halves)):
-        side = core if place < len(halves) else 1 - core
-        row = 2 * jnp.bitwise_xor(group, place % len(halves)) + side
-        upper, lower = [
-            bands[number + 4 * (place // len(halves))].at[half * part : half * (part + 1)]
-            for number, part in halves[place % len(halves)]
-        ]
-        rows = pl.ds(pl.multiple_of(row * BLOCK, BLOCK), BLOCK)
-        for k in range(blocks // 2 + 1):
-            column = lax.rem(row + k, blocks)
-            columns = pl.ds(pl.multiple_of(column * BLOCK, BLOCK), BLOCK)
-            inside = slice(BLOCK * k, BLOCK * (k + 1))
-            part = jnp.concatenate([upper[:, inside], lower[:, inside]], axis=0)
-            high_ref[rows, columns], low_ref[rows, columns] = split(part)
-            if 0 < k < blocks // 2:
-                high_ref[columns, rows], low_ref[columns, rows] = split(part.T)
+    half, band = bands[0].shape[0] // 2, bands[0].shape[1]
+    for stacks, side in ((bands[:4], core), (bands[4:], 1 - core)):
+        corners = {}
+        for mask, places in halves.items():
+            upper, lower = [stacks[number].at[half * part : half * (part + 1)] for number, part in places]
+            row = 2 * jnp.bitwise_xor(group, mask) + side
+            for k in range(opposite):
+                inside = slice(BLOCK * k, BLOCK * (k + 1))
+                part = jnp.concatenate([upper[:, inside], lower[: BLOCK - half, inside]], axis=0)
+                store(row, lax.rem(row + k, blocks), part, k > 0)
+            corners[mask] = jnp.concatenate(
+                [lower[BLOCK - half :, BLOCK * i : BLOCK * (i + 1)] for i in range(band // BLOCK)], axis=0
+            )
+        for mask in (0, 1):
+            row = 2 * jnp.bitwise_xor(group, mask) + side
+            here, across = corners[mask], corners[mask ^ 2]
+            near = row < opposite
+            part = jnp.concatenate([jnp.where(near, here, across), jnp.where(near, across, here)], axis=0)
+            row = lax.rem(row, opposite)
+            store(row, row + opposite, part, True)
     sweeps(basis_ref, field_ref, *rest)
 
 
@@ -307,12 +332,12 @@
             flops=10**9,
         )
 
-    def last_factors(image, inner):
+    def last_factors(image, before):
         return call(
             last_kernel,
             [(rank, rank)],
             "last_factors",
-            [image, inner],
+            [image, before],
             [pltpu.VMEM((rank, rank), jnp.float32), spread],
             flops=10**9,
         )
@@ -320,59 +345,59 @@
     scratch = [
         pltpu.VMEM((order, order), jnp.bfloat16),
         pltpu.VMEM((order, order), jnp.bfloat16),
-        pltpu.VMEM((rank, rank), jnp.float32),
         spread,
         pltpu.VMEM((rank, order), jnp.float32),
     ]
     results = [(rank, order), (rank, rank), (cells, rank)]
     blocks = order // BLOCK
-    if wide == blocks and narrow & (narrow - 1) == 0 and BLOCK % (8 * narrow) == 0:
+    if wide == blocks and narrow & (narrow - 1) == 0 and blocks // 2 % narrow == 0:
         groups = wide // 2
-        band = BLOCK * (blocks // 2 + 1)
+        band = order // 2
+        half = (BLOCK + BLOCK // blocks) // 2
         extended = (cells, order + band - BLOCK)
         other = swap(unfolded, "wide", 1)
         own = call(split_kernel, [extended] * 2, "split_field", [unfolded], dtype=jnp.bfloat16)
         first_kept, first_sent, second_kept, second_sent = call(
             gram_kernel,
-            [(BLOCK, band)] * groups,
+            [(2 * half, band)] * groups,
             "gram_band",
             [*own, other],
-            [pltpu.VMEM((2 * cells, extended[1]), jnp.bfloat16)] * 2,
+            [pltpu.VMEM((2 * cells, extended[1]), jnp.bfloat16)] * 2 + [pltpu.VMEM((BLOCK, BLOCK), jnp.float32)],
             flops=10**9,
         )
         first_got, second_got = swap(first_sent, "wide", 2), swap(second_sent, "wide", 4)
         basis = orthonormal_start(first_kept)
         first, first_sent, second, second_sent = call(
             halve_kernel,
-            [(BLOCK // 2, band)] * 4,
+            [(half, band)] * 4,
             "sum_pairs",
             [first_kept, first_got, second_kept, second_got],
             order_only=[basis],
         )
         cuts = call(
             cut_kernel,
-            [(BLOCK // narrow, band)] * narrow,
+            [(2 * half, band // narrow)] * narrow,
             "sum_groups",
             [first, swap(first_sent, "wide", 4), second, swap(second_sent, "wide", 2)],
         )
         arrived = [swap(cuts[k], "narrow", k) for k in range(1, narrow)]
-        piece = call(add_kernel, [(BLOCK // narrow, band)], "sum_planes", [cuts[0], *arrived])
+        piece = call(add_kernel, [(2 * half, band // narrow)], "sum_planes", [cuts[0], *arrived])
         arrived = [swap(piece, "narrow", k) for k in range(1, narrow)]
         first, second = call(
             join_kernel,
-            [(BLOCK // 2, band)] * 2,
+            [(half, band)] * 2,
             "join_planes",
             [piece, *arrived],
         )
         stacks = call(
             stack_kernel,
-            [(BLOCK, band)] * 2,
+            [(2 * half, band)] * 2,
             "stack_pairs",
             [first, swap(first, "wide", 4), second, swap(second, "wide", 2)],
         )
         stacks = [*stacks, swap(stacks[0], "wide", 2), swap(stacks[1], "wide", 4)]
         bands = stacks + [swap(stack, "wide", 1) for stack in stacks]
-        image, inner, raw = call(
+        image, before, raw = call(
             functools.partial(banded_kernel, blocks),
             results,
             "sweeps",
@@ -380,7 +405,7 @@
             scratch,
         )
         raws = [raw] + [swap(raw, "narrow", k) for k in range(1, narrow)]
-        factor = last_factors(image, inner)
+        factor = last_factors(image, before)
         total = call(
             functools.partial(tail_kernel, cells_three),
             [(cells_two, narrow * cells_two)],
@@ -396,8 +421,8 @@
         basis = orthonormal_start(start_block)
         gram = lax.dot_general(unfolded, unfolded, (((0,), (0,)), ((), ())), precision=HIGHEST)
         gram = lax.psum(gram, ("narrow", "wide"))
-        image, inner, raw = call(whole_kernel, results, "sweeps", [basis, unfolded, gram], scratch)
-        core = lax.dot_general(raw, last_factors(image, inner), NT, precision=HIGHEST)
+        image, before, raw = call(whole_kernel, results, "sweeps", [basis, unfolded, gram], scratch)
+        core = lax.dot_general(raw, last_factors(image, before), NT, precision=HIGHEST)
         merged = core.reshape(cells_two, cells_three * rank)
         everyone = lax.all_gather(merged, "narrow", axis=0, tiled=True)
         part = lax.dot_general(merged, everyone, NT, precision=HIGHEST)

time: 94.8 us -> 91.4 us (0.964)
  waiting for transfers between devices: 35.9 us -> 33.6 us
  Pallas kernels: 29.3 us -> 28.3 us
    ppermute x26, waiting for transfers between devices: 35.9 us -> 33.6 us  [swap(): lax.ppermute(array, axis, [(i, i ^ mask) for i in range(lax.axis_size(axi...]
    pallas_call x11, Pallas kernels: 29.3 us -> 28.3 us  [call(): pl.pallas_call(kernel, out_shape=shapes, in_specs=[pl.BlockSpec(memory_sp...]
  transfers between devices with their start and end apart: 26 -> 26, of which waited for: 18 -> 19; matrix products, arithmetic and copies ran while one was open for 0% -> 0% of each run, Pallas kernels for 14% -> 11%
where the time goes in v4:
time: 91.4 us; the launch traced here: 91.3 us
  waiting for transfers between devices  33.6 us (37%)
  Pallas kernels  28.3 us (31%)
  starting transfers between devices  27.5 us (30%)
  local copies, waits for them, and re-layouts  1.71 us (2%)
    ppermute x26, waiting for transfers between devices, swap(): lax.ppermute(array, axis, [(i, i ^ mask) for i in range(lax.axis_size(axi...  33.6 us
    pallas_call x11, Pallas kernels, call(): pl.pallas_call(kernel, out_shape=shapes, in_specs=[pl.BlockSpec(memory_sp...  28.3 us
    ppermute x26, starting transfers between devices, swap(): lax.ppermute(array, axis, [(i, i ^ mask) for i in range(lax.axis_size(axi...  27.5 us
  transfers between devices with their start and end apart: 26, of which 19 were waited for; matrix products, arithmetic and copies ran while one was open for 0% of the time, Pallas kernels for 11%

profile of v4, /device:TPU:0, one launch (start us, length us, event | category | flops | bytes accessed | tf_op | source)
XLA Modules:
  0.0 91.3 jit_solution(14578262362995262115)
XLA Ops:
  0.0 0.5 collective-permute-start
  0.5 1.0 %copy-done = f32[8,16,1024]{2,1,0:T(8,128)S(1)} copy-done((f32[8,16,1024]{2,1,0:T(8,128)S(1)}, f32[8,16,1024]{2,1,0:T(8,128)}, u32[]{:S(2)}) %copy-start) | copy-done | bytes 524312
  1.6 0.6 collective-permute-done.other_ref
  2.2 1.0 %gram_band.1 = (f32[144,512]{1,0:T(8,128)S(1)}, f32[144,512]{1,0:T(8,128)S(1)}, f32[144,512]{1,0:T(8,128)S(1)}, f32[144,512]{1,0:T(8,128)S(1)}) custom-call(bf16[128,1408]{1,0:T(8,128)(2,1)S(1)} %get-tuple-element.26.own_high, bf16[128,1408]{1,0:T(8,128)(2,1)S(1)} %get-tuple-element.27.own_low, f32[128,1024]{1,0:T(8,128)S(1)} %collective-permute-done.other_ref), custom_call_target="tpu_custom_call" | custom-call | flops 1000000000 | bytes 3145728 | tf_op jit(solution)/shard_map/gram_band/pallas_call | solution.py:298
  3.2 2.9 %collective-permute-start.1 = (f32[144,512]{1,0:T(8,128)S(1)}, f32[144,512]{1,0:T(8,128)S(1)}, u32[]{:S(2)}, u32[]{:S(2)}) collective-permute-start(f32[144,512]{1,0:T(8,128)S(1)} %get-tuple-element.29), channel_id=1, source_target_pairs={{0,2},{1,3},{2,0},{3,1},{4,6},{5,7},{6,4},{7,5},{8,10},{9,11},{10,... | collective-permute-start | bytes 884744 | tf_op jit(solution)/shard_map/ppermute | solution.py:312
  6.1 1.5 %collective-permute-start.2 = (f32[144,512]{1,0:T(8,128)S(1)}, f32[144,512]{1,0:T(8,128)S(1)}, u32[]{:S(2)}, u32[]{:S(2)}) collective-permute-start(f32[144,512]{1,0:T(8,128)S(1)} %get-tuple-element.31), channel_id=1, source_target_pairs={{0,4},{1,5},{2,6},{3,7},{4,0},{5,1},{6,2},{7,3},{8,12},{9,13},{10,... | collective-permute-start | bytes 884744 | tf_op jit(solution)/shard_map/ppermute | solution.py:312
  7.6 5.1 %orth_start.1.after_ref.basis_ref = f32[128,1024]{1,0:T(8,128)S(1)} custom-call(f32[144,512]{1,0:T(8,128)S(1)} %get-tuple-element.28.after_ref.kept_first, f32[1024,128]{1,0:T(8,128)S(1)} %copy-done.2), custom_call_target="tpu_custom_call" | custom-call | flops 1000000000 | bytes 1048576 | tf_op jit(solution)/shard_map/orth_start/pallas_call | solution.py:298
  12.7 0.7 collective-permute-done.1.got_first
  13.4 1.5 %collective-permute-done.2.got_second = f32[144,512]{1,0:T(8,128)S(1)} collective-permute-done((f32[144,512]{1,0:T(8,128)S(1)}, f32[144,512]{1,0:T(8,128)S(1)}, u32[]{:S(2)}, u32[]{:S(2)}) %collective-permute-start.2) | collective-permute-done | bytes 294944 | tf_op jit(solution)/shard_map/ppermute | solution.py:312
  14.9 1.6 %collective-permute-start.3 = (f32[72,512]{1,0:T(8,128)S(1)}, f32[72,512]{1,0:T(8,128)S(1)}, u32[]{:S(2)}, u32[]{:S(2)}) collective-permute-start(f32[72,512]{1,0:T(8,128)S(1)} %get-tuple-element.33), channel_id=1, source_target_pairs={{0,4},{1,5},{2,6},{3,7},{4,0},{5,1},{6,2},{7,3},{8,12},{9,13},{10,... | collective-permute-start | bytes 442376 | tf_op jit(solution)/shard_map/ppermute | solution.py:312
  16.5 0.5 collective-permute-start.4
  17.1 3.1 %collective-permute-done.3.got_first = f32[72,512]{1,0:T(8,128)S(1)} collective-permute-done((f32[72,512]{1,0:T(8,128)S(1)}, f32[72,512]{1,0:T(8,128)S(1)}, u32[]{:S(2)}, u32[]{:S(2)}) %collective-permute-start.3) | collective-permute-done | bytes 147488 | tf_op jit(solution)/shard_map/ppermute | solution.py:312
  20.2 1.5 %collective-permute-done.4.got_second = f32[72,512]{1,0:T(8,128)S(1)} collective-permute-done((f32[72,512]{1,0:T(8,128)S(1)}, f32[72,512]{1,0:T(8,128)S(1)}, u32[]{:S(2)}, u32[]{:S(2)}) %collective-permute-start.4) | collective-permute-done | bytes 147488 | tf_op jit(solution)/shard_map/ppermute | solution.py:312
  21.8 1.6 %collective-permute-start.5 = (f32[144,128]{1,0:T(8,128)S(1)}, f32[144,128]{1,0:T(8,128)S(1)}, u32[]{:S(2)}, u32[]{:S(2)}) collective-permute-start(f32[144,128]{1,0:T(8,128)S(1)} %get-tuple-element.37), channel_id=1, source_target_pairs={{0,8},{8,0},{16,24},{24,16},{1,9},{9,1},{17,25},{25,17},{2,10},{10... | collective-permute-start | bytes 221192 | tf_op jit(solution)/shard_map/ppermute | solution.py:312
  23.4 2.6 %collective-permute-start.6 = (f32[144,128]{1,0:T(8,128)S(1)}, f32[144,128]{1,0:T(8,128)S(1)}, u32[]{:S(2)}, u32[]{:S(2)}) collective-permute-start(f32[144,128]{1,0:T(8,128)S(1)} %get-tuple-element.38), channel_id=1, source_target_pairs={{0,16},{8,24},{16,0},{24,8},{1,17},{9,25},{17,1},{25,9},{2,18},{10... | collective-permute-start | bytes 221192 | tf_op jit(solution)/shard_map/ppermute | solution.py:312
  26.0 0.2 collective-permute-start.7
  26.2 4.0 %collective-permute-done.6.refs_2_ = f32[144,128]{1,0:T(8,128)S(1)} collective-permute-done((f32[144,128]{1,0:T(8,128)S(1)}, f32[144,128]{1,0:T(8,128)S(1)}, u32[]{:S(2)}, u32[]{:S(2)}) %collective-permute-start.6) | collective-permute-done | bytes 73760 | tf_op jit(solution)/shard_map/ppermute | solution.py:312
  30.2 2.1 %collective-permute-done.7.refs_3_ = f32[144,128]{1,0:T(8,128)S(1)} collective-permute-done((f32[144,128]{1,0:T(8,128)S(1)}, f32[144,128]{1,0:T(8,128)S(1)}, u32[]{:S(2)}, u32[]{:S(2)}) %collective-permute-start.7) | collective-permute-done | bytes 73760 | tf_op jit(solution)/shard_map/ppermute | solution.py:312
  32.3 0.9 collective-permute-start.10
  33.1 0.5 collective-permute-start.8
  33.7 3.1 %collective-permute-start.9 = (f32[144,128]{1,0:T(8,128)S(1)}, f32[144,128]{1,0:T(8,128)S(1)}, u32[]{:S(2)}, u32[]{:S(2)}) collective-permute-start(f32[144,128]{1,0:T(8,128)S(1)} %sum_planes.1.refs_0_), channel_id=1, source_target_pairs={{0,16},{8,24},{16,0},{24,8},{1,17},{9,25},{17,1},{25,9},{2,18},{10... | collective-permute-start | bytes 221192 | tf_op jit(solution)/shard_map/ppermute | solution.py:312
  36.7 1.8 %collective-permute-done.10.refs_3_ = f32[144,128]{1,0:T(8,128)S(1)} collective-permute-done((f32[144,128]{1,0:T(8,128)S(1)}, f32[144,128]{1,0:T(8,128)S(1)}, u32[]{:S(2)}, u32[]{:S(2)}) %collective-permute-start.10) | collective-permute-done | bytes 73760 | tf_op jit(solution)/shard_map/ppermute | solution.py:312
  38.5 0.8 collective-permute-done.9.refs_2_
  39.3 0.6 collective-permute-start.11
  39.9 0.5 collective-permute-start.12
  40.4 5.6 %collective-permute-done.11.got_first = f32[72,512]{1,0:T(8,128)S(1)} collective-permute-done((f32[72,512]{1,0:T(8,128)S(1)}, f32[72,512]{1,0:T(8,128)S(1)}, u32[]{:S(2)}, u32[]{:S(2)}) %collective-permute-start.11) | collective-permute-done | bytes 147488 | tf_op jit(solution)/shard_map/ppermute | solution.py:312
  46.1 0.6 collective-permute-done.12.got_second
  46.7 0.6 collective-permute-start.13
  47.3 1.5 %collective-permute-start.14 = (f32[144,512]{1,0:T(8,128)S(1)}, f32[144,512]{1,0:T(8,128)S(1)}, u32[]{:S(2)}, u32[]{:S(2)}) collective-permute-start(f32[144,512]{1,0:T(8,128)S(1)} %get-tuple-element.43.refs_1_), channel_id=1, source_target_pairs={{0,4},{1,5},{2,6},{3,7},{4,0},{5,1},{6,2},{7,3},{8,12},{9,13},{10,... | collective-permute-start | bytes 884744 | tf_op jit(solution)/shard_map/ppermute | solution.py:312
  48.8 0.5 collective-permute-start.16
  49.3 4.2 %collective-permute-done.13.refs_2_ = f32[144,512]{1,0:T(8,128)S(1)} collective-permute-done((f32[144,512]{1,0:T(8,128)S(1)}, f32[144,512]{1,0:T(8,128)S(1)}, u32[]{:S(2)}, u32[]{:S(2)}) %collective-permute-start.13) | collective-permute-done | bytes 294944 | tf_op jit(solution)/shard_map/ppermute | solution.py:312
  53.5 0.5 collective-permute-done.14.refs_3_
  54.0 1.1 %collective-permute-done.17.refs_6_ = f32[144,512]{1,0:T(8,128)S(1)} collective-permute-done((f32[144,512]{1,0:T(8,128)S(1)}, f32[144,512]{1,0:T(8,128)S(1)}, u32[]{:S(2)}, u32[]{:S(2)}) %collective-permute-start.17) | collective-permute-done | bytes 294944 | tf_op jit(solution)/shard_map/ppermute | solution.py:312
  55.1 0.5 collective-permute-done.18.refs_7_
  55.6 15.8 %sweeps.1 = (f32[128,1024]{1,0:T(8,128)S(1)}, f32[128,128]{1,0:T(8,128)S(1)}, f32[128,128]{1,0:T(8,128)S(1)}) custom-call(f32[128,1024]{1,0:T(8,128)S(1)} %orth_start.1.after_ref.basis_ref, f32[128,1024]{1,0:T(8,128)S(1)} %bitcast.3, f32[144,512]{1,0:T(8,128)S(1)} %get-tuple-element.42.refs_0_, f32[144,512]{1,0:T(8,128)S(1)} %get-tuple-element.43.refs_1_, ...), custom_call_target="tpu_custom_call" | custom-call | bytes 4063232 | tf_op jit(solution)/shard_map/sweeps/pallas_call | solution.py:298
  71.4 1.4 %collective-permute-start.19 = (f32[128,128]{1,0:T(8,128)S(1)}, f32[128,128]{1,0:T(8,128)S(1)}, u32[]{:S(2)}, u32[]{:S(2)}) collective-permute-start(f32[128,128]{1,0:T(8,128)S(1)} %get-tuple-element.46.refs_0_), channel_id=1, source_target_pairs={{0,8},{8,0},{16,24},{24,16},{1,9},{9,1},{17,25},{25,17},{2,10},{10... | collective-permute-start | bytes 196616 | tf_op jit(solution)/shard_map/ppermute | solution.py:312
  72.8 1.4 %collective-permute-start.20 = (f32[128,128]{1,0:T(8,128)S(1)}, f32[128,128]{1,0:T(8,128)S(1)}, u32[]{:S(2)}, u32[]{:S(2)}) collective-permute-start(f32[128,128]{1,0:T(8,128)S(1)} %get-tuple-element.46.refs_0_), channel_id=1, source_target_pairs={{0,16},{8,24},{16,0},{24,8},{1,17},{9,25},{17,1},{25,9},{2,18},{10... | collective-permute-start | bytes 196616 | tf_op jit(solution)/shard_map/ppermute | solution.py:312
  74.2 1.7 %collective-permute-start.21 = (f32[128,128]{1,0:T(8,128)S(1)}, f32[128,128]{1,0:T(8,128)S(1)}, u32[]{:S(2)}, u32[]{:S(2)}) collective-permute-start(f32[128,128]{1,0:T(8,128)S(1)} %get-tuple-element.46.refs_0_), channel_id=1, source_target_pairs={{0,24},{8,16},{16,8},{24,0},{1,25},{9,17},{17,9},{25,1},{2,26},{10... | collective-permute-start | bytes 196616 | tf_op jit(solution)/shard_map/ppermute | solution.py:312
  75.9 4.8 %last_factors.1.factor_ref = f32[128,128]{1,0:T(8,128)S(1)} custom-call(f32[128,1024]{1,0:T(8,128)S(1)} %get-tuple-element.44.image_ref, f32[128,128]{1,0:T(8,128)S(1)} %get-tuple-element.45.before_ref), custom_call_target="tpu_custom_call" | custom-call | flops 1000000000 | bytes 655360 | tf_op jit(solution)/shard_map/last_factors/pallas_call | solution.py:298
  80.7 0.3 collective-permute-done.20.refs_2_
  81.1 1.3 %core_pairs.1 = f32[8,32]{1,0:T(8,128)S(1)} custom-call(f32[128,128]{1,0:T(8,128)S(1)} %last_factors.1.factor_ref, f32[128,128]{1,0:T(8,128)S(1)} %get-tuple-element.46.refs_0_, f32[128,128]{1,0:T(8,128)S(1)} %collective-permute-done.19.refs_1_, f32[128,128]{1,0:T(8,128)S(1)} %collective-permute-done.20.refs_2_, f32[128,128]{1,0:T(8,128)S(1)} %collective-permute-done.21.refs_3_), custom_call_target="tpu_custom_call" | custom-call | bytes 328704 | tf_op jit(solution)/shard_map/core_pairs/pallas_call | solution.py:298
  82.3 1.6 %collective-permute-start.23 = (f32[8,32]{1,0:T(8,128)S(1)}, f32[8,32]{1,0:T(8,128)S(1)}, u32[]{:S(2)}, u32[]{:S(2)}) collective-permute-start(f32[8,32]{1,0:T(8,128)S(1)} %core_pairs.1), channel_id=1, source_target_pairs={{0,2},{1,3},{2,0},{3,1},{4,6},{5,7},{6,4},{7,5},{8,10},{9,11},{10,... | collective-permute-start | bytes 3080 | tf_op jit(solution)/shard_map/ppermute | solution.py:312
  83.9 0.3 collective-permute-start.24
  84.2 1.8 %collective-permute-done.23 = f32[8,32]{1,0:T(8,128)S(1)} collective-permute-done((f32[8,32]{1,0:T(8,128)S(1)}, f32[8,32]{1,0:T(8,128)S(1)}, u32[]{:S(2)}, u32[]{:S(2)}) %collective-permute-start.23) | collective-permute-done | bytes 1056 | tf_op jit(solution)/shard_map/ppermute | solution.py:312
  86.0 0.9 %collective-permute-done.24 = f32[8,32]{1,0:T(8,128)S(1)} collective-permute-done((f32[8,32]{1,0:T(8,128)S(1)}, f32[8,32]{1,0:T(8,128)S(1)}, u32[]{:S(2)}, u32[]{:S(2)}) %collective-permute-start.24) | collective-permute-done | bytes 1056 | tf_op jit(solution)/shard_map/ppermute | solution.py:312
  86.9 1.5 %collective-permute-start.25 = (f32[8,32]{1,0:T(8,128)S(1)}, f32[8,32]{1,0:T(8,128)S(1)}, u32[]{:S(2)}, u32[]{:S(2)}) collective-permute-start(f32[8,32]{1,0:T(8,128)S(1)} %add_add_fusion), channel_id=1, source_target_pairs={{0,4},{1,5},{2,6},{3,7},{4,0},{5,1},{6,2},{7,3},{8,12},{9,13},{10,... | collective-permute-start | bytes 3080 | tf_op jit(solution)/shard_map/ppermute | solution.py:312
  88.4 2.1 %collective-permute-done.25 = f32[8,32]{1,0:T(8,128)S(1)} collective-permute-done((f32[8,32]{1,0:T(8,128)S(1)}, f32[8,32]{1,0:T(8,128)S(1)}, u32[]{:S(2)}, u32[]{:S(2)}) %collective-permute-start.25) | collective-permute-done | bytes 1056 | tf_op jit(solution)/shard_map/ppermute | solution.py:312
  90.6 0.7 copy.3
  (25 shorter events, 0.5 us)
Async XLA Ops:
  0.0 2.2 %collective-permute-start = (f32[128,1024]{1,0:T(8,128)}, f32[128,1024]{1,0:T(8,128)S(1)}, u32[]{:S(2)}, u32[]{:S(2)}) collective-permute-start(f32[128,1024]{1,0:T(8,128)} %bitcast.1), channel_id=1, source_target_pairs={{0,1},{1,0},{2,3},{3,2},{4,5},{5,4},{6,7},{7,6},{8,9},{9,8},{10,11... | collective-permute-start | bytes 1572872 | tf_op jit(solution)/shard_map/ppermute | solution.py:312
  0.5 1.0 %copy-start = (f32[8,16,1024]{2,1,0:T(8,128)S(1)}, f32[8,16,1024]{2,1,0:T(8,128)}, u32[]{:S(2)}) copy-start(f32[8,16,1024]{2,1,0:T(8,128)} %param.2) | copy-start | bytes 1572868
  2.2 5.4 %copy-start.2 = (f32[1024,128]{1,0:T(8,128)S(1)}, f32[1024,128]{1,0:T(8,128)}, u32[]{:S(2)}) copy-start(f32[1024,128]{1,0:T(8,128)} %start_ref.1) | copy-start | bytes 1572868
  3.2 10.2 %collective-permute-start.1 = (f32[144,512]{1,0:T(8,128)S(1)}, f32[144,512]{1,0:T(8,128)S(1)}, u32[]{:S(2)}, u32[]{:S(2)}) collective-permute-start(f32[144,512]{1,0:T(8,128)S(1)} %get-tuple-element.29), channel_id=1, source_target_pairs={{0,2},{1,3},{2,0},{3,1},{4,6},{5,7},{6,4},{7,5},{8,10},{9,11},{10,... | collective-permute-start | bytes 884744 | tf_op jit(solution)/shard_map/ppermute | solution.py:312
  6.1 8.8 %collective-permute-start.2 = (f32[144,512]{1,0:T(8,128)S(1)}, f32[144,512]{1,0:T(8,128)S(1)}, u32[]{:S(2)}, u32[]{:S(2)}) collective-permute-start(f32[144,512]{1,0:T(8,128)S(1)} %get-tuple-element.31), channel_id=1, source_target_pairs={{0,4},{1,5},{2,6},{3,7},{4,0},{5,1},{6,2},{7,3},{8,12},{9,13},{10,... | collective-permute-start | bytes 884744 | tf_op jit(solution)/shard_map/ppermute | solution.py:312
  14.9 5.2 %collective-permute-start.3 = (f32[72,512]{1,0:T(8,128)S(1)}, f32[72,512]{1,0:T(8,128)S(1)}, u32[]{:S(2)}, u32[]{:S(2)}) collective-permute-start(f32[72,512]{1,0:T(8,128)S(1)} %get-tuple-element.33), channel_id=1, source_target_pairs={{0,4},{1,5},{2,6},{3,7},{4,0},{5,1},{6,2},{7,3},{8,12},{9,13},{10,... | collective-permute-start | bytes 442376 | tf_op jit(solution)/shard_map/ppermute | solution.py:312
  16.5 5.1 %collective-permute-start.4 = (f32[72,512]{1,0:T(8,128)S(1)}, f32[72,512]{1,0:T(8,128)S(1)}, u32[]{:S(2)}, u32[]{:S(2)}) collective-permute-start(f32[72,512]{1,0:T(8,128)S(1)} %get-tuple-element.35), channel_id=1, source_target_pairs={{0,2},{1,3},{2,0},{3,1},{4,6},{5,7},{6,4},{7,5},{8,10},{9,11},{10,... | collective-permute-start | bytes 442376 | tf_op jit(solution)/shard_map/ppermute | solution.py:312
  21.8 4.5 %collective-permute-start.5 = (f32[144,128]{1,0:T(8,128)S(1)}, f32[144,128]{1,0:T(8,128)S(1)}, u32[]{:S(2)}, u32[]{:S(2)}) collective-permute-start(f32[144,128]{1,0:T(8,128)S(1)} %get-tuple-element.37), channel_id=1, source_target_pairs={{0,8},{8,0},{16,24},{24,16},{1,9},{9,1},{17,25},{25,17},{2,10},{10... | collective-permute-start | bytes 221192 | tf_op jit(solution)/shard_map/ppermute | solution.py:312
  23.4 6.8 %collective-permute-start.6 = (f32[144,128]{1,0:T(8,128)S(1)}, f32[144,128]{1,0:T(8,128)S(1)}, u32[]{:S(2)}, u32[]{:S(2)}) collective-permute-start(f32[144,128]{1,0:T(8,128)S(1)} %get-tuple-element.38), channel_id=1, source_target_pairs={{0,16},{8,24},{16,0},{24,8},{1,17},{9,25},{17,1},{25,9},{2,18},{10... | collective-permute-start | bytes 221192 | tf_op jit(solution)/shard_map/ppermute | solution.py:312
  26.0 6.3 %collective-permute-start.7 = (f32[144,128]{1,0:T(8,128)S(1)}, f32[144,128]{1,0:T(8,128)S(1)}, u32[]{:S(2)}, u32[]{:S(2)}) collective-permute-start(f32[144,128]{1,0:T(8,128)S(1)} %get-tuple-element.39), channel_id=1, source_target_pairs={{0,24},{8,16},{16,8},{24,0},{1,25},{9,17},{17,9},{25,1},{2,26},{10... | collective-permute-start | bytes 221192 | tf_op jit(solution)/shard_map/ppermute | solution.py:312
  32.3 23.3 %copy-start.1 = (f32[8,16,1024]{2,1,0:T(8,128)S(1)}, f32[8,16,1024]{2,1,0:T(8,128)}, u32[]{:S(2)}) copy-start(f32[8,16,1024]{2,1,0:T(8,128)} %param.2) | copy-start | bytes 1572868
  32.3 6.2 %collective-permute-start.10 = (f32[144,128]{1,0:T(8,128)S(1)}, f32[144,128]{1,0:T(8,128)S(1)}, u32[]{:S(2)}, u32[]{:S(2)}) collective-permute-start(f32[144,128]{1,0:T(8,128)S(1)} %sum_planes.1.refs_0_), channel_id=1, source_target_pairs={{0,24},{8,16},{16,8},{24,0},{1,25},{9,17},{17,9},{25,1},{2,26},{10... | collective-permute-start | bytes 221192 | tf_op jit(solution)/shard_map/ppermute | solution.py:312
  33.1 5.4 %collective-permute-start.8 = (f32[144,128]{1,0:T(8,128)S(1)}, f32[144,128]{1,0:T(8,128)S(1)}, u32[]{:S(2)}, u32[]{:S(2)}) collective-permute-start(f32[144,128]{1,0:T(8,128)S(1)} %sum_planes.1.refs_0_), channel_id=1, source_target_pairs={{0,8},{8,0},{16,24},{24,16},{1,9},{9,1},{17,25},{25,17},{2,10},{10... | collective-permute-start | bytes 221192 | tf_op jit(solution)/shard_map/ppermute | solution.py:312
  33.7 5.6 %collective-permute-start.9 = (f32[144,128]{1,0:T(8,128)S(1)}, f32[144,128]{1,0:T(8,128)S(1)}, u32[]{:S(2)}, u32[]{:S(2)}) collective-permute-start(f32[144,128]{1,0:T(8,128)S(1)} %sum_planes.1.refs_0_), channel_id=1, source_target_pairs={{0,16},{8,24},{16,0},{24,8},{1,17},{9,25},{17,1},{25,9},{2,18},{10... | collective-permute-start | bytes 221192 | tf_op jit(solution)/shard_map/ppermute | solution.py:312
  39.3 6.7 %collective-permute-start.11 = (f32[72,512]{1,0:T(8,128)S(1)}, f32[72,512]{1,0:T(8,128)S(1)}, u32[]{:S(2)}, u32[]{:S(2)}) collective-permute-start(f32[72,512]{1,0:T(8,128)S(1)} %get-tuple-element.40.first), channel_id=1, source_target_pairs={{0,4},{1,5},{2,6},{3,7},{4,0},{5,1},{6,2},{7,3},{8,12},{9,13},{10,... | collective-permute-start | bytes 442376 | tf_op jit(solution)/shard_map/ppermute | solution.py:312
  39.9 6.8 %collective-permute-start.12 = (f32[72,512]{1,0:T(8,128)S(1)}, f32[72,512]{1,0:T(8,128)S(1)}, u32[]{:S(2)}, u32[]{:S(2)}) collective-permute-start(f32[72,512]{1,0:T(8,128)S(1)} %get-tuple-element.41.second), channel_id=1, source_target_pairs={{0,2},{1,3},{2,0},{3,1},{4,6},{5,7},{6,4},{7,5},{8,10},{9,11},{10,... | collective-permute-start | bytes 442376 | tf_op jit(solution)/shard_map/ppermute | solution.py:312
  46.7 6.8 %collective-permute-start.13 = (f32[144,512]{1,0:T(8,128)S(1)}, f32[144,512]{1,0:T(8,128)S(1)}, u32[]{:S(2)}, u32[]{:S(2)}) collective-permute-start(f32[144,512]{1,0:T(8,128)S(1)} %get-tuple-element.42.refs_0_), channel_id=1, source_target_pairs={{0,2},{1,3},{2,0},{3,1},{4,6},{5,7},{6,4},{7,5},{8,10},{9,11},{10,... | collective-permute-start | bytes 884744 | tf_op jit(solution)/shard_map/ppermute | solution.py:312
  47.3 6.7 %collective-permute-start.14 = (f32[144,512]{1,0:T(8,128)S(1)}, f32[144,512]{1,0:T(8,128)S(1)}, u32[]{:S(2)}, u32[]{:S(2)}) collective-permute-start(f32[144,512]{1,0:T(8,128)S(1)} %get-tuple-element.43.refs_1_), channel_id=1, source_target_pairs={{0,4},{1,5},{2,6},{3,7},{4,0},{5,1},{6,2},{7,3},{8,12},{9,13},{10,... | collective-permute-start | bytes 884744 | tf_op jit(solution)/shard_map/ppermute | solution.py:312
  48.8 5.2 %collective-permute-start.15 = (f32[144,512]{1,0:T(8,128)S(1)}, f32[144,512]{1,0:T(8,128)S(1)}, u32[]{:S(2)}, u32[]{:S(2)}) collective-permute-start(f32[144,512]{1,0:T(8,128)S(1)} %get-tuple-element.42.refs_0_), channel_id=1, source_target_pairs={{0,1},{1,0},{2,3},{3,2},{4,5},{5,4},{6,7},{7,6},{8,9},{9,8},{10,11... | collective-permute-start | bytes 884744 | tf_op jit(solution)/shard_map/ppermute | solution.py:312
  48.8 5.2 %collective-permute-start.16 = (f32[144,512]{1,0:T(8,128)S(1)}, f32[144,512]{1,0:T(8,128)S(1)}, u32[]{:S(2)}, u32[]{:S(2)}) collective-permute-start(f32[144,512]{1,0:T(8,128)S(1)} %get-tuple-element.43.refs_1_), channel_id=1, source_target_pairs={{0,1},{1,0},{2,3},{3,2},{4,5},{5,4},{6,7},{7,6},{8,9},{9,8},{10,11... | collective-permute-start | bytes 884744 | tf_op jit(solution)/shard_map/ppermute | solution.py:312
  53.5 1.6 %collective-permute-start.17 = (f32[144,512]{1,0:T(8,128)S(1)}, f32[144,512]{1,0:T(8,128)S(1)}, u32[]{:S(2)}, u32[]{:S(2)}) collective-permute-start(f32[144,512]{1,0:T(8,128)S(1)} %collective-permute-done.13.refs_2_), channel_id=1, source_target_pairs={{0,1},{1,0},{2,3},{3,2},{4,5},{5,4},{6,7},{7,6},{8,9},{9,8},{10,11... | collective-permute-start | bytes 884744 | tf_op jit(solution)/shard_map/ppermute | solution.py:312
  54.0 1.6 %collective-permute-start.18 = (f32[144,512]{1,0:T(8,128)S(1)}, f32[144,512]{1,0:T(8,128)S(1)}, u32[]{:S(2)}, u32[]{:S(2)}) collective-permute-start(f32[144,512]{1,0:T(8,128)S(1)} %collective-permute-done.14.refs_3_), channel_id=1, source_target_pairs={{0,1},{1,0},{2,3},{3,2},{4,5},{5,4},{6,7},{7,6},{8,9},{9,8},{10,11... | collective-permute-start | bytes 884744 | tf_op jit(solution)/shard_map/ppermute | solution.py:312
  71.4 9.3 %collective-permute-start.19 = (f32[128,128]{1,0:T(8,128)S(1)}, f32[128,128]{1,0:T(8,128)S(1)}, u32[]{:S(2)}, u32[]{:S(2)}) collective-permute-start(f32[128,128]{1,0:T(8,128)S(1)} %get-tuple-element.46.refs_0_), channel_id=1, source_target_pairs={{0,8},{8,0},{16,24},{24,16},{1,9},{9,1},{17,25},{25,17},{2,10},{10... | collective-permute-start | bytes 196616 | tf_op jit(solution)/shard_map/ppermute | solution.py:312
  72.8 8.2 %collective-permute-start.20 = (f32[128,128]{1,0:T(8,128)S(1)}, f32[128,128]{1,0:T(8,128)S(1)}, u32[]{:S(2)}, u32[]{:S(2)}) collective-permute-start(f32[128,128]{1,0:T(8,128)S(1)} %get-tuple-element.46.refs_0_), channel_id=1, source_target_pairs={{0,16},{8,24},{16,0},{24,8},{1,17},{9,25},{17,1},{25,9},{2,18},{10... | collective-permute-start | bytes 196616 | tf_op jit(solution)/shard_map/ppermute | solution.py:312
  74.2 6.9 %collective-permute-start.21 = (f32[128,128]{1,0:T(8,128)S(1)}, f32[128,128]{1,0:T(8,128)S(1)}, u32[]{:S(2)}, u32[]{:S(2)}) collective-permute-start(f32[128,128]{1,0:T(8,128)S(1)} %get-tuple-element.46.refs_0_), channel_id=1, source_target_pairs={{0,24},{8,16},{16,8},{24,0},{1,25},{9,17},{17,9},{25,1},{2,26},{10... | collective-permute-start | bytes 196616 | tf_op jit(solution)/shard_map/ppermute | solution.py:312
  82.3 1.9 %collective-permute-start.22 = (f32[8,32]{1,0:T(8,128)S(1)}, f32[8,32]{1,0:T(8,128)S(1)}, u32[]{:S(2)}, u32[]{:S(2)}) collective-permute-start(f32[8,32]{1,0:T(8,128)S(1)} %core_pairs.1), channel_id=1, source_target_pairs={{0,1},{1,0},{2,3},{3,2},{4,5},{5,4},{6,7},{7,6},{8,9},{9,8},{10,11... | collective-permute-start | bytes 3080 | tf_op jit(solution)/shard_map/ppermute | solution.py:312
  82.3 3.6 %collective-permute-start.23 = (f32[8,32]{1,0:T(8,128)S(1)}, f32[8,32]{1,0:T(8,128)S(1)}, u32[]{:S(2)}, u32[]{:S(2)}) collective-permute-start(f32[8,32]{1,0:T(8,128)S(1)} %core_pairs.1), channel_id=1, source_target_pairs={{0,2},{1,3},{2,0},{3,1},{4,6},{5,7},{6,4},{7,5},{8,10},{9,11},{10,... | collective-permute-start | bytes 3080 | tf_op jit(solution)/shard_map/ppermute | solution.py:312
  83.9 3.0 %collective-permute-start.24 = (f32[8,32]{1,0:T(8,128)S(1)}, f32[8,32]{1,0:T(8,128)S(1)}, u32[]{:S(2)}, u32[]{:S(2)}) collective-permute-start(f32[8,32]{1,0:T(8,128)S(1)} %core_pairs.1), channel_id=1, source_target_pairs={{0,3},{1,2},{2,1},{3,0},{4,7},{5,6},{6,5},{7,4},{8,11},{9,10},{10,... | collective-permute-start | bytes 3080 | tf_op jit(solution)/shard_map/ppermute | solution.py:312
  86.9 3.6 %collective-permute-start.25 = (f32[8,32]{1,0:T(8,128)S(1)}, f32[8,32]{1,0:T(8,128)S(1)}, u32[]{:S(2)}, u32[]{:S(2)}) collective-permute-start(f32[8,32]{1,0:T(8,128)S(1)} %add_add_fusion), channel_id=1, source_target_pairs={{0,4},{1,5},{2,6},{3,7},{4,0},{5,1},{6,2},{7,3},{8,12},{9,13},{10,... | collective-permute-start | bytes 3080 | tf_op jit(solution)/shard_map/ppermute | solution.py:312

commit v5 on v4

--- a/solution.py
+++ b/solution.py
@@ -153,8 +153,8 @@
         lower[k][half * (k % 2) : half * (k % 2 + 1), :] = whole[half:]
 
 
-def halve_kernel(after_ref, kept_first, got_first, kept_second, got_second, *outs):
-    del after_ref
+def halve_kernel(after_ref, cells_ref, kept_first, got_first, kept_second, got_second, *outs):
+    del after_ref, cells_ref
     half = kept_first.shape[0] // 2
     for kept, got, (own, send) in ((kept_first, got_first, outs[:2]), (kept_second, got_second, outs[2:])):
         own[...] = kept[:half, :] + got[:half, :]
@@ -194,42 +194,45 @@
         out[half:, :] = got[...]
 
 
-def sweeps(basis_ref, field_ref, image_ref, factor_ref, raw_ref, high_ref, low_ref, spread_ref, basis_scratch):
+def sweeps(basis_ref, field_ref, image_ref, factor_ref, raw_ref, high_ref, low_ref, spread_ref):
     def times_gram(rows):
         return dot_split(split(rows), (high_ref[...], low_ref[...]), NN)
 
-    def step(image):
+    image = times_gram(basis_ref[...])
+    for number in range(ITERS - 1):
         halves = split(image)
         inner = dot_split(halves, halves, NT)
         following = times_gram(image)
+        if number == ITERS - 2:
+            image_ref[...] = following
+            raw_ref[...] = dot_full(field_ref[...], following, NT)
         inverse_factor(inner, factor_ref, spread_ref)
-        return following
-
-    def body(number, carry):
-        following = step(basis_scratch[...])
-        basis_scratch[...] = dot_split(split(factor_ref[...]), split(following), NN)
-        return carry
-
-    basis_scratch[...] = times_gram(basis_ref[...])
-    lax.fori_loop(0, ITERS - 2, body, 0)
-    image = basis_scratch[...]
-    inner = dot_full(image, image, NT)
-    following = times_gram(image)
-    image_ref[...] = following
-    raw_ref[...] = dot_full(field_ref[...], following, NT)
-    inverse_factor(inner, factor_ref, spread_ref)
-
-
-def last_kernel(image_ref, before_ref, out_ref, factor_ref, spread_ref):
+        image = dot_split(split(factor_ref[...]), split(following), NN)
+
+
+def halves_kernel(own_field, other_field, sent_ref, rest_ref):
+    size = own_field.shape[0] // 2
+    core = chip_and_core()[1]
+    for part, out in ((core, sent_ref), (1 - core, rest_ref)):
+        rows = pl.ds(pl.multiple_of(part * size, size), size)
+        out[:size, :] = own_field[rows, :]
+        out[size:, :] = other_field[rows, :]
+
+
+def last_kernel(image_ref, before_ref, *refs):
+    count = len(refs) // 2 - 1
+    fields, (out_ref, *rest_ref, factor_ref, spread_ref) = refs[:count], refs[count:]
     before = before_ref[...]
     image = dot_full(before, image_ref[...], NN)
-    inverse_factor(dot_full(image, image, NT), factor_ref, spread_ref)
+    inner = dot_full(image, image, NT)
+    if fields:
+        rest_ref[0][...] = dot_full(fields[0][...], image_ref[...], NT)
+    inverse_factor(inner, factor_ref, spread_ref)
     out_ref[...] = dot_full(factor_ref[...], before, NN)
 
 
 def banded_kernel(blocks, basis_ref, field_ref, *refs):
-    bands, rest = refs[:-7], refs[-7:]
-    high_ref, low_ref = rest[3:5]
+    bands, (image_ref, before_ref, raw_ref, high_ref, low_ref, spread_ref) = refs[:-6], refs[-6:]
     group, core = chip_and_core()
     opposite = blocks // 2
 
@@ -261,34 +264,38 @@
             part = jnp.concatenate([jnp.where(near, here, across), jnp.where(near, across, here)], axis=0)
             row = lax.rem(row, opposite)
             store(row, row + opposite, part, True)
-    sweeps(basis_ref, field_ref, *rest)
-
-
-def whole_kernel(basis_ref, field_ref, gram_ref, *rest):
-    rest[3][...], rest[4][...] = split(gram_ref[...])
-    sweeps(basis_ref, field_ref, *rest)
-
-
-def tail_kernel(cells_three, factor_ref, *refs):
+    sweeps(basis_ref, field_ref, image_ref, before_ref, raw_ref, high_ref, low_ref, spread_ref)
+
+
+def whole_kernel(basis_ref, field_ref, gram_ref, image_ref, before_ref, raw_ref, high_ref, low_ref, spread_ref):
+    high_ref[...], low_ref[...] = split(gram_ref[...])
+    sweeps(basis_ref, field_ref, image_ref, before_ref, raw_ref, high_ref, low_ref, spread_ref)
+
+
+def tail_kernel(cells_three, factor_ref, rest_ref, *refs):
     raw, (out_ref, own_ref, all_ref) = refs[:-3], refs[-3:]
-    size = raw[0].shape[0]
+    size = rest_ref.shape[0]
     cells_two = size // cells_three
+    half = size // 2
     planes = len(raw)
-    factor = factor_ref[...]
-    plane = lax.axis_index("narrow")
-    for k, part in enumerate(raw):
-        core = dot_full(part[...], factor, NT)
-        if k == 0:
-            own_ref[...] = core
-        place = pl.multiple_of(jnp.bitwise_xor(plane, k) * size, size)
-        all_ref[pl.ds(place, size), :] = core
-    own = [own_ref[pl.ds(k, cells_two, stride=cells_three), :] for k in range(cells_three)]
-    every = [
-        jnp.concatenate(
-            [all_ref[pl.ds(size * q + k, cells_two, stride=cells_three), :] for q in range(planes)], axis=0
-        )
-        for k in range(cells_three)
-    ]
+    plane, core = lax.axis_index("narrow"), chip_and_core()[1]
+    cores = dot_full(jnp.concatenate([part[...] for part in (rest_ref, *raw)], axis=0), factor_ref[...], NT)
+    for k in range(planes + 1):
+        part = cores[size * k : size * (k + 1)]
+        if k < 2:
+            place = pl.multiple_of((core if k else 1 - core) * half, half)
+            own_ref[pl.ds(place, half), :] = part[:half]
+            own_ref[pl.ds(size + place, half), :] = part[half:]
+        if k > 0:
+            place = pl.multiple_of(jnp.bitwise_xor(plane, k - 1) * half, half)
+            all_ref[pl.ds(place, half), :] = part[:half]
+            all_ref[pl.ds(planes * half + place, half), :] = part[half:]
+    own, every = [], []
+    for side in range(2):
+        for k in range(cells_three):
+            own.append(own_ref[pl.ds(size * side + k, cells_two, stride=cells_three), :])
+            rows = planes * half // cells_three
+            every.append(all_ref[pl.ds(planes * half * side + k, rows, stride=cells_three), :])
     out_ref[...] = dot_full(jnp.concatenate(own, axis=1), jnp.concatenate(every, axis=1), NT)
 
 
@@ -332,12 +339,12 @@
             flops=10**9,
         )
 
-    def last_factors(image, before):
+    def last_factors(image, before, *fields):
         return call(
             last_kernel,
-            [(rank, rank)],
+            [(rank, rank)] + [(cells, rank)] * len(fields),
             "last_factors",
-            [image, before],
+            [image, before, *fields],
             [pltpu.VMEM((rank, rank), jnp.float32), spread],
             flops=10**9,
         )
@@ -346,11 +353,10 @@
         pltpu.VMEM((order, order), jnp.bfloat16),
         pltpu.VMEM((order, order), jnp.bfloat16),
         spread,
-        pltpu.VMEM((rank, order), jnp.float32),
     ]
     results = [(rank, order), (rank, rank), (cells, rank)]
     blocks = order // BLOCK
-    if wide == blocks and narrow & (narrow - 1) == 0 and blocks // 2 % narrow == 0:
+    if wide == blocks == 2 * narrow and narrow & (narrow - 1) == 0 and blocks // 2 % narrow == 0:
         groups = wide // 2
         band = order // 2
         half = (BLOCK + BLOCK // blocks) // 2
@@ -367,12 +373,13 @@
         )
         first_got, second_got = swap(first_sent, "wide", 2), swap(second_sent, "wide", 4)
         basis = orthonormal_start(first_kept)
+        sent_cells, rest_cells = call(halves_kernel, [(cells, order)] * 2, "half_cells", [unfolded, other])
         first, first_sent, second, second_sent = call(
             halve_kernel,
             [(half, band)] * 4,
             "sum_pairs",
             [first_kept, first_got, second_kept, second_got],
-            order_only=[basis],
+            order_only=[basis, sent_cells],
         )
         cuts = call(
             cut_kernel,
@@ -401,22 +408,21 @@
             functools.partial(banded_kernel, blocks),
             results,
             "sweeps",
-            [basis, unfolded, *bands],
+            [basis, sent_cells, *bands],
             scratch,
         )
         raws = [raw] + [swap(raw, "narrow", k) for k in range(1, narrow)]
-        factor = last_factors(image, before)
+        factor, rest = last_factors(image, before, rest_cells)
         total = call(
             functools.partial(tail_kernel, cells_three),
-            [(cells_two, narrow * cells_two)],
+            [(cells_two, narrow * cells_two // 2)],
             "core_pairs",
-            [factor, *raws],
-            [pltpu.VMEM((cells, rank), jnp.float32), pltpu.VMEM((narrow * cells, rank), jnp.float32)],
-        )
-        total = add_pairs([total] + [swap(total, "wide", k) for k in range(1, 4)])
-        total = total + swap(total, "wide", 4)
+            [factor, rest, *raws],
+            [pltpu.VMEM((2 * cells, rank), jnp.float32), pltpu.VMEM((narrow * cells, rank), jnp.float32)],
+        )
+        total = add_pairs([total] + [swap(total, "wide", 2 * k) for k in range(1, groups)])
         columns = narrow * cells_two // wide
-        finished = lax.dynamic_slice_in_dim(total, place * columns, columns, 1)
+        finished = lax.dynamic_slice_in_dim(total, place // 2 * columns, columns, 1)
     else:
         basis = orthonormal_start(start_block)
         gram = lax.dot_general(unfolded, unfolded, (((0,), (0,)), ((), ())), precision=HIGHEST)

time: 91.4 us -> 90.2 us (0.987)
    ppermute x26 -> x25, waiting for transfers between devices: 33.6 us -> 32.7 us  [swap(): lax.ppermute(array, axis, [(i, i ^ mask) for i in range(lax.axis_size(axi...]
    pallas_call x11 -> x12, Pallas kernels: 28.3 us -> 27.9 us  [call(): pl.pallas_call(kernel, out_shape=shapes, in_specs=[pl.BlockSpec(memory_sp...]
    ppermute x26 -> x25, starting transfers between devices: 27.5 us -> 27.6 us  [swap(): lax.ppermute(array, axis, [(i, i ^ mask) for i in range(lax.axis_size(axi...]
  transfers between devices with their start and end apart: 26 -> 25, of which waited for: 19 -> 19; matrix products, arithmetic and copies ran while one was open for 0% -> 0% of each run, Pallas kernels for 11% -> 11%
where the time goes in v5:
time: 90.2 us; the launch traced here: 90 us
  waiting for transfers between devices  32.7 us (36%)
  Pallas kernels  27.9 us (31%)
  starting transfers between devices  27.6 us (31%)
  local copies, waits for them, and re-layouts  1.71 us (2%)
    ppermute x25, waiting for transfers between devices, swap(): lax.ppermute(array, axis, [(i, i ^ mask) for i in range(lax.axis_size(axi...  32.7 us
    pallas_call x12, Pallas kernels, call(): pl.pallas_call(kernel, out_shape=shapes, in_specs=[pl.BlockSpec(memory_sp...  27.9 us
    ppermute x25, starting transfers between devices, swap(): lax.ppermute(array, axis, [(i, i ^ mask) for i in range(lax.axis_size(axi...  27.6 us
  transfers between devices with their start and end apart: 25, of which 19 were waited for; matrix products, arithmetic and copies ran while one was open for 0% of the time, Pallas kernels for 11%

profile of v5, /device:TPU:0, one launch (start us, length us, event | category | flops | bytes accessed | tf_op | source)
XLA Modules:
  0.0 90.0 jit_solution(9211230567508325059)
XLA Ops:
  0.0 0.5 collective-permute-start
  0.5 1.0 %copy-done = f32[8,16,1024]{2,1,0:T(8,128)S(1)} copy-done((f32[8,16,1024]{2,1,0:T(8,128)S(1)}, f32[8,16,1024]{2,1,0:T(8,128)}, u32[]{:S(2)}) %copy-start) | copy-done | bytes 524312
  1.6 0.6 collective-permute-done.other_ref.other_field
  2.2 1.0 %gram_band.1 = (f32[144,512]{1,0:T(8,128)S(1)}, f32[144,512]{1,0:T(8,128)S(1)}, f32[144,512]{1,0:T(8,128)S(1)}, f32[144,512]{1,0:T(8,128)S(1)}) custom-call(bf16[128,1408]{1,0:T(8,128)(2,1)S(1)} %get-tuple-element.30.own_high, bf16[128,1408]{1,0:T(8,128)(2,1)S(1)} %get-tuple-element.31.own_low, f32[128,1024]{1,0:T(8,128)S(1)} %collective-permute-done.other_ref.other_field), custom_call_target="tpu_custom_call" | custom-call | flops 1000000000 | bytes 3145728 | tf_op jit(solution)/shard_map/gram_band/pallas_call | solution.py:305
  3.2 2.9 %collective-permute-start.1 = (f32[144,512]{1,0:T(8,128)S(1)}, f32[144,512]{1,0:T(8,128)S(1)}, u32[]{:S(2)}, u32[]{:S(2)}) collective-permute-start(f32[144,512]{1,0:T(8,128)S(1)} %get-tuple-element.34), channel_id=1, source_target_pairs={{0,2},{1,3},{2,0},{3,1},{4,6},{5,7},{6,4},{7,5},{8,10},{9,11},{10,... | collective-permute-start | bytes 884744 | tf_op jit(solution)/shard_map/ppermute | solution.py:319
  6.1 1.5 %collective-permute-start.2 = (f32[144,512]{1,0:T(8,128)S(1)}, f32[144,512]{1,0:T(8,128)S(1)}, u32[]{:S(2)}, u32[]{:S(2)}) collective-permute-start(f32[144,512]{1,0:T(8,128)S(1)} %get-tuple-element.36), channel_id=1, source_target_pairs={{0,4},{1,5},{2,6},{3,7},{4,0},{5,1},{6,2},{7,3},{8,12},{9,13},{10,... | collective-permute-start | bytes 884744 | tf_op jit(solution)/shard_map/ppermute | solution.py:319
  7.7 5.1 %orth_start.1.after_ref.basis_ref = f32[128,1024]{1,0:T(8,128)S(1)} custom-call(f32[144,512]{1,0:T(8,128)S(1)} %get-tuple-element.32.after_ref.kept_first, f32[1024,128]{1,0:T(8,128)S(1)} %copy-done.2), custom_call_target="tpu_custom_call" | custom-call | flops 1000000000 | bytes 1048576 | tf_op jit(solution)/shard_map/orth_start/pallas_call | solution.py:305
  12.8 0.6 collective-permute-done.1.got_first
  13.4 1.5 %collective-permute-done.2.got_second = f32[144,512]{1,0:T(8,128)S(1)} collective-permute-done((f32[144,512]{1,0:T(8,128)S(1)}, f32[144,512]{1,0:T(8,128)S(1)}, u32[]{:S(2)}, u32[]{:S(2)}) %collective-permute-start.2) | collective-permute-done | bytes 294944 | tf_op jit(solution)/shard_map/ppermute | solution.py:319
  14.9 1.6 %collective-permute-start.3 = (f32[72,512]{1,0:T(8,128)S(1)}, f32[72,512]{1,0:T(8,128)S(1)}, u32[]{:S(2)}, u32[]{:S(2)}) collective-permute-start(f32[72,512]{1,0:T(8,128)S(1)} %get-tuple-element.38), channel_id=1, source_target_pairs={{0,4},{1,5},{2,6},{3,7},{4,0},{5,1},{6,2},{7,3},{8,12},{9,13},{10,... | collective-permute-start | bytes 442376 | tf_op jit(solution)/shard_map/ppermute | solution.py:319
  16.5 0.5 collective-permute-start.4
  17.1 3.1 %collective-permute-done.3.got_first = f32[72,512]{1,0:T(8,128)S(1)} collective-permute-done((f32[72,512]{1,0:T(8,128)S(1)}, f32[72,512]{1,0:T(8,128)S(1)}, u32[]{:S(2)}, u32[]{:S(2)}) %collective-permute-start.3) | collective-permute-done | bytes 147488 | tf_op jit(solution)/shard_map/ppermute | solution.py:319
  20.2 1.5 %collective-permute-done.4.got_second = f32[72,512]{1,0:T(8,128)S(1)} collective-permute-done((f32[72,512]{1,0:T(8,128)S(1)}, f32[72,512]{1,0:T(8,128)S(1)}, u32[]{:S(2)}, u32[]{:S(2)}) %collective-permute-start.4) | collective-permute-done | bytes 147488 | tf_op jit(solution)/shard_map/ppermute | solution.py:319
  21.8 1.6 %collective-permute-start.5 = (f32[144,128]{1,0:T(8,128)S(1)}, f32[144,128]{1,0:T(8,128)S(1)}, u32[]{:S(2)}, u32[]{:S(2)}) collective-permute-start(f32[144,128]{1,0:T(8,128)S(1)} %get-tuple-element.42), channel_id=1, source_target_pairs={{0,8},{8,0},{16,24},{24,16},{1,9},{9,1},{17,25},{25,17},{2,10},{10... | collective-permute-start | bytes 221192 | tf_op jit(solution)/shard_map/ppermute | solution.py:319
  23.4 2.6 %collective-permute-start.6 = (f32[144,128]{1,0:T(8,128)S(1)}, f32[144,128]{1,0:T(8,128)S(1)}, u32[]{:S(2)}, u32[]{:S(2)}) collective-permute-start(f32[144,128]{1,0:T(8,128)S(1)} %get-tuple-element.43), channel_id=1, source_target_pairs={{0,16},{8,24},{16,0},{24,8},{1,17},{9,25},{17,1},{25,9},{2,18},{10... | collective-permute-start | bytes 221192 | tf_op jit(solution)/shard_map/ppermute | solution.py:319
  26.0 0.2 collective-permute-start.7
  26.2 4.0 %collective-permute-done.6.refs_2_ = f32[144,128]{1,0:T(8,128)S(1)} collective-permute-done((f32[144,128]{1,0:T(8,128)S(1)}, f32[144,128]{1,0:T(8,128)S(1)}, u32[]{:S(2)}, u32[]{:S(2)}) %collective-permute-start.6) | collective-permute-done | bytes 73760 | tf_op jit(solution)/shard_map/ppermute | solution.py:319
  30.2 2.0 %collective-permute-done.7.refs_3_ = f32[144,128]{1,0:T(8,128)S(1)} collective-permute-done((f32[144,128]{1,0:T(8,128)S(1)}, f32[144,128]{1,0:T(8,128)S(1)}, u32[]{:S(2)}, u32[]{:S(2)}) %collective-permute-start.7) | collective-permute-done | bytes 73760 | tf_op jit(solution)/shard_map/ppermute | solution.py:319
  32.3 0.9 collective-permute-start.10
  33.1 0.5 collective-permute-start.8
  33.6 3.1 %collective-permute-start.9 = (f32[144,128]{1,0:T(8,128)S(1)}, f32[144,128]{1,0:T(8,128)S(1)}, u32[]{:S(2)}, u32[]{:S(2)}) collective-permute-start(f32[144,128]{1,0:T(8,128)S(1)} %sum_planes.1.refs_0_), channel_id=1, source_target_pairs={{0,16},{8,24},{16,0},{24,8},{1,17},{9,25},{17,1},{25,9},{2,18},{10... | collective-permute-start | bytes 221192 | tf_op jit(solution)/shard_map/ppermute | solution.py:319
  36.7 1.8 %collective-permute-done.10.refs_3_ = f32[144,128]{1,0:T(8,128)S(1)} collective-permute-done((f32[144,128]{1,0:T(8,128)S(1)}, f32[144,128]{1,0:T(8,128)S(1)}, u32[]{:S(2)}, u32[]{:S(2)}) %collective-permute-start.10) | collective-permute-done | bytes 73760 | tf_op jit(solution)/shard_map/ppermute | solution.py:319
  38.5 0.8 collective-permute-done.9.refs_2_
  39.3 0.6 collective-permute-start.11
  39.9 0.5 collective-permute-start.12
  40.4 5.6 %collective-permute-done.11.got_first = f32[72,512]{1,0:T(8,128)S(1)} collective-permute-done((f32[72,512]{1,0:T(8,128)S(1)}, f32[72,512]{1,0:T(8,128)S(1)}, u32[]{:S(2)}, u32[]{:S(2)}) %collective-permute-start.11) | collective-permute-done | bytes 147488 | tf_op jit(solution)/shard_map/ppermute | solution.py:319
  46.1 0.6 collective-permute-done.12.got_second
  46.7 0.6 collective-permute-start.13
  47.3 1.5 %collective-permute-start.14 = (f32[144,512]{1,0:T(8,128)S(1)}, f32[144,512]{1,0:T(8,128)S(1)}, u32[]{:S(2)}, u32[]{:S(2)}) collective-permute-start(f32[144,512]{1,0:T(8,128)S(1)} %get-tuple-element.48.refs_1_), channel_id=1, source_target_pairs={{0,4},{1,5},{2,6},{3,7},{4,0},{5,1},{6,2},{7,3},{8,12},{9,13},{10,... | collective-permute-start | bytes 884744 | tf_op jit(solution)/shard_map/ppermute | solution.py:319
  48.8 0.5 collective-permute-start.16
  49.3 4.2 %collective-permute-done.13.refs_2_ = f32[144,512]{1,0:T(8,128)S(1)} collective-permute-done((f32[144,512]{1,0:T(8,128)S(1)}, f32[144,512]{1,0:T(8,128)S(1)}, u32[]{:S(2)}, u32[]{:S(2)}) %collective-permute-start.13) | collective-permute-done | bytes 294944 | tf_op jit(solution)/shard_map/ppermute | solution.py:319
  53.5 0.5 collective-permute-done.14.refs_3_
  54.0 1.0 %collective-permute-done.17.refs_6_ = f32[144,512]{1,0:T(8,128)S(1)} collective-permute-done((f32[144,512]{1,0:T(8,128)S(1)}, f32[144,512]{1,0:T(8,128)S(1)}, u32[]{:S(2)}, u32[]{:S(2)}) %collective-permute-start.17) | collective-permute-done | bytes 294944 | tf_op jit(solution)/shard_map/ppermute | solution.py:319
  55.1 0.5 collective-permute-done.18.refs_7_
  55.6 15.3 %sweeps.1 = (f32[128,1024]{1,0:T(8,128)S(1)}, f32[128,128]{1,0:T(8,128)S(1)}, f32[128,128]{1,0:T(8,128)S(1)}) custom-call(f32[128,1024]{1,0:T(8,128)S(1)} %orth_start.1.after_ref.basis_ref, f32[128,1024]{1,0:T(8,128)S(1)} %get-tuple-element.33.cells_ref.field_ref, f32[144,512]{1,0:T(8,128)S(1)} %get-tuple-element.47.refs_0_, ...), custom_call_target="tpu_custom_call" | custom-call | bytes 4063232 | tf_op jit(solution)/shard_map/sweeps/pallas_call | solution.py:305
  70.9 1.4 %collective-permute-start.19 = (f32[128,128]{1,0:T(8,128)S(1)}, f32[128,128]{1,0:T(8,128)S(1)}, u32[]{:S(2)}, u32[]{:S(2)}) collective-permute-start(f32[128,128]{1,0:T(8,128)S(1)} %get-tuple-element.54.refs_0_), channel_id=1, source_target_pairs={{0,8},{8,0},{16,24},{24,16},{1,9},{9,1},{17,25},{25,17},{2,10},{10... | collective-permute-start | bytes 196616 | tf_op jit(solution)/shard_map/ppermute | solution.py:319
  72.3 1.4 %collective-permute-start.20 = (f32[128,128]{1,0:T(8,128)S(1)}, f32[128,128]{1,0:T(8,128)S(1)}, u32[]{:S(2)}, u32[]{:S(2)}) collective-permute-start(f32[128,128]{1,0:T(8,128)S(1)} %get-tuple-element.54.refs_0_), channel_id=1, source_target_pairs={{0,16},{8,24},{16,0},{24,8},{1,17},{9,25},{17,1},{25,9},{2,18},{10... | collective-permute-start | bytes 196616 | tf_op jit(solution)/shard_map/ppermute | solution.py:319
  73.7 1.7 %collective-permute-start.21 = (f32[128,128]{1,0:T(8,128)S(1)}, f32[128,128]{1,0:T(8,128)S(1)}, u32[]{:S(2)}, u32[]{:S(2)}) collective-permute-start(f32[128,128]{1,0:T(8,128)S(1)} %get-tuple-element.54.refs_0_), channel_id=1, source_target_pairs={{0,24},{8,16},{16,8},{24,0},{1,25},{9,17},{17,9},{25,1},{2,26},{10... | collective-permute-start | bytes 196616 | tf_op jit(solution)/shard_map/ppermute | solution.py:319
  75.3 4.9 %last_factors.1 = (f32[128,128]{1,0:T(8,128)S(1)}, f32[128,128]{1,0:T(8,128)S(1)}) custom-call(f32[128,1024]{1,0:T(8,128)S(1)} %get-tuple-element.49.image_ref, f32[128,128]{1,0:T(8,128)S(1)} %get-tuple-element.50.before_ref, f32[128,1024]{1,0:T(8,128)S(1)} %copy-done.4), custom_call_target="tpu_custom_call" | custom-call | flops 1000000000 | bytes 1245184 | tf_op jit(solution)/shard_map/last_factors/pallas_call | solution.py:305
  80.3 0.2 collective-permute-done.20.refs_2_
  80.5 1.2 %core_pairs.1 = f32[8,16]{1,0:T(8,128)S(1)} custom-call(f32[128,128]{1,0:T(8,128)S(1)} %get-tuple-element.52.factor_ref, f32[128,128]{1,0:T(8,128)S(1)} %get-tuple-element.53.rest_ref, f32[128,128]{1,0:T(8,128)S(1)} %get-tuple-element.54.refs_0_, f32[128,128]{1,0:T(8,128)S(1)} %collective-permute-done.19.refs_1_, ...), custom_call_target="tpu_custom_call" | custom-call | bytes 393728 | tf_op jit(solution)/shard_map/core_pairs/pallas_call | solution.py:305
  81.8 1.5 %collective-permute-start.22 = (f32[8,16]{1,0:T(8,128)S(1)}, f32[8,16]{1,0:T(8,128)S(1)}, u32[]{:S(2)}, u32[]{:S(2)}) collective-permute-start(f32[8,16]{1,0:T(8,128)S(1)} %core_pairs.1), channel_id=1, source_target_pairs={{0,2},{1,3},{2,0},{3,1},{4,6},{5,7},{6,4},{7,5},{8,10},{9,11},{10,... | collective-permute-start | bytes 1544 | tf_op jit(solution)/shard_map/ppermute | solution.py:319
  83.3 1.5 %collective-permute-start.23 = (f32[8,16]{1,0:T(8,128)S(1)}, f32[8,16]{1,0:T(8,128)S(1)}, u32[]{:S(2)}, u32[]{:S(2)}) collective-permute-start(f32[8,16]{1,0:T(8,128)S(1)} %core_pairs.1), channel_id=1, source_target_pairs={{0,4},{1,5},{2,6},{3,7},{4,0},{5,1},{6,2},{7,3},{8,12},{9,13},{10,... | collective-permute-start | bytes 1544 | tf_op jit(solution)/shard_map/ppermute | solution.py:319
  84.8 0.5 collective-permute-start.24
  85.3 0.1 collective-permute-done.22
  85.4 1.5 %collective-permute-done.23 = f32[8,16]{1,0:T(8,128)S(1)} collective-permute-done((f32[8,16]{1,0:T(8,128)S(1)}, f32[8,16]{1,0:T(8,128)S(1)}, u32[]{:S(2)}, u32[]{:S(2)}) %collective-permute-start.23) | collective-permute-done | bytes 544 | tf_op jit(solution)/shard_map/ppermute | solution.py:319
  86.9 2.4 %collective-permute-done.24 = f32[8,16]{1,0:T(8,128)S(1)} collective-permute-done((f32[8,16]{1,0:T(8,128)S(1)}, f32[8,16]{1,0:T(8,128)S(1)}, u32[]{:S(2)}, u32[]{:S(2)}) %collective-permute-start.24) | collective-permute-done | bytes 544 | tf_op jit(solution)/shard_map/ppermute | solution.py:319
  89.4 0.7 copy.3
  (27 shorter events, 0.6 us)
Async XLA Ops:
  0.0 2.2 %collective-permute-start = (f32[128,1024]{1,0:T(8,128)}, f32[128,1024]{1,0:T(8,128)S(1)}, u32[]{:S(2)}, u32[]{:S(2)}) collective-permute-start(f32[128,1024]{1,0:T(8,128)} %bitcast.1), channel_id=1, source_target_pairs={{0,1},{1,0},{2,3},{3,2},{4,5},{5,4},{6,7},{7,6},{8,9},{9,8},{10,11... | collective-permute-start | bytes 1572872 | tf_op jit(solution)/shard_map/ppermute | solution.py:319
  0.5 1.0 %copy-start = (f32[8,16,1024]{2,1,0:T(8,128)S(1)}, f32[8,16,1024]{2,1,0:T(8,128)}, u32[]{:S(2)}) copy-start(f32[8,16,1024]{2,1,0:T(8,128)} %param.2) | copy-start | bytes 1572868
  2.2 5.4 %copy-start.1 = (f32[8,16,1024]{2,1,0:T(8,128)S(1)}, f32[8,16,1024]{2,1,0:T(8,128)}, u32[]{:S(2)}) copy-start(f32[8,16,1024]{2,1,0:T(8,128)} %param.2) | copy-start | bytes 1572868
  3.2 10.2 %collective-permute-start.1 = (f32[144,512]{1,0:T(8,128)S(1)}, f32[144,512]{1,0:T(8,128)S(1)}, u32[]{:S(2)}, u32[]{:S(2)}) collective-permute-start(f32[144,512]{1,0:T(8,128)S(1)} %get-tuple-element.34), channel_id=1, source_target_pairs={{0,2},{1,3},{2,0},{3,1},{4,6},{5,7},{6,4},{7,5},{8,10},{9,11},{10,... | collective-permute-start | bytes 884744 | tf_op jit(solution)/shard_map/ppermute | solution.py:319
  6.1 1.6 %copy-start.2 = (f32[1024,128]{1,0:T(8,128)S(1)}, f32[1024,128]{1,0:T(8,128)}, u32[]{:S(2)}) copy-start(f32[1024,128]{1,0:T(8,128)} %start_ref.1) | copy-start | bytes 1572868
  6.1 8.8 %collective-permute-start.2 = (f32[144,512]{1,0:T(8,128)S(1)}, f32[144,512]{1,0:T(8,128)S(1)}, u32[]{:S(2)}, u32[]{:S(2)}) collective-permute-start(f32[144,512]{1,0:T(8,128)S(1)} %get-tuple-element.36), channel_id=1, source_target_pairs={{0,4},{1,5},{2,6},{3,7},{4,0},{5,1},{6,2},{7,3},{8,12},{9,13},{10,... | collective-permute-start | bytes 884744 | tf_op jit(solution)/shard_map/ppermute | solution.py:319
  7.7 5.1 %copy-start.3 = (f32[128,1024]{1,0:T(8,128)}, f32[128,1024]{1,0:T(8,128)S(1)}, u32[]{:S(2)}) copy-start(f32[128,1024]{1,0:T(8,128)S(1)} %get-tuple-element.51.refs_0_) | copy-start | bytes 1572868
  14.9 5.2 %collective-permute-start.3 = (f32[72,512]{1,0:T(8,128)S(1)}, f32[72,512]{1,0:T(8,128)S(1)}, u32[]{:S(2)}, u32[]{:S(2)}) collective-permute-start(f32[72,512]{1,0:T(8,128)S(1)} %get-tuple-element.38), channel_id=1, source_target_pairs={{0,4},{1,5},{2,6},{3,7},{4,0},{5,1},{6,2},{7,3},{8,12},{9,13},{10,... | collective-permute-start | bytes 442376 | tf_op jit(solution)/shard_map/ppermute | solution.py:319
  16.5 5.1 %collective-permute-start.4 = (f32[72,512]{1,0:T(8,128)S(1)}, f32[72,512]{1,0:T(8,128)S(1)}, u32[]{:S(2)}, u32[]{:S(2)}) collective-permute-start(f32[72,512]{1,0:T(8,128)S(1)} %get-tuple-element.40), channel_id=1, source_target_pairs={{0,2},{1,3},{2,0},{3,1},{4,6},{5,7},{6,4},{7,5},{8,10},{9,11},{10,... | collective-permute-start | bytes 442376 | tf_op jit(solution)/shard_map/ppermute | solution.py:319
  21.8 4.5 %collective-permute-start.5 = (f32[144,128]{1,0:T(8,128)S(1)}, f32[144,128]{1,0:T(8,128)S(1)}, u32[]{:S(2)}, u32[]{:S(2)}) collective-permute-start(f32[144,128]{1,0:T(8,128)S(1)} %get-tuple-element.42), channel_id=1, source_target_pairs={{0,8},{8,0},{16,24},{24,16},{1,9},{9,1},{17,25},{25,17},{2,10},{10... | collective-permute-start | bytes 221192 | tf_op jit(solution)/shard_map/ppermute | solution.py:319
  23.4 6.8 %collective-permute-start.6 = (f32[144,128]{1,0:T(8,128)S(1)}, f32[144,128]{1,0:T(8,128)S(1)}, u32[]{:S(2)}, u32[]{:S(2)}) collective-permute-start(f32[144,128]{1,0:T(8,128)S(1)} %get-tuple-element.43), channel_id=1, source_target_pairs={{0,16},{8,24},{16,0},{24,8},{1,17},{9,25},{17,1},{25,9},{2,18},{10... | collective-permute-start | bytes 221192 | tf_op jit(solution)/shard_map/ppermute | solution.py:319
  26.0 6.3 %collective-permute-start.7 = (f32[144,128]{1,0:T(8,128)S(1)}, f32[144,128]{1,0:T(8,128)S(1)}, u32[]{:S(2)}, u32[]{:S(2)}) collective-permute-start(f32[144,128]{1,0:T(8,128)S(1)} %get-tuple-element.44), channel_id=1, source_target_pairs={{0,24},{8,16},{16,8},{24,0},{1,25},{9,17},{17,9},{25,1},{2,26},{10... | collective-permute-start | bytes 221192 | tf_op jit(solution)/shard_map/ppermute | solution.py:319
  32.3 6.2 %collective-permute-start.10 = (f32[144,128]{1,0:T(8,128)S(1)}, f32[144,128]{1,0:T(8,128)S(1)}, u32[]{:S(2)}, u32[]{:S(2)}) collective-permute-start(f32[144,128]{1,0:T(8,128)S(1)} %sum_planes.1.refs_0_), channel_id=1, source_target_pairs={{0,24},{8,16},{16,8},{24,0},{1,25},{9,17},{17,9},{25,1},{2,26},{10... | collective-permute-start | bytes 221192 | tf_op jit(solution)/shard_map/ppermute | solution.py:319
  33.1 5.4 %collective-permute-start.8 = (f32[144,128]{1,0:T(8,128)S(1)}, f32[144,128]{1,0:T(8,128)S(1)}, u32[]{:S(2)}, u32[]{:S(2)}) collective-permute-start(f32[144,128]{1,0:T(8,128)S(1)} %sum_planes.1.refs_0_), channel_id=1, source_target_pairs={{0,8},{8,0},{16,24},{24,16},{1,9},{9,1},{17,25},{25,17},{2,10},{10... | collective-permute-start | bytes 221192 | tf_op jit(solution)/shard_map/ppermute | solution.py:319
  33.6 5.6 %collective-permute-start.9 = (f32[144,128]{1,0:T(8,128)S(1)}, f32[144,128]{1,0:T(8,128)S(1)}, u32[]{:S(2)}, u32[]{:S(2)}) collective-permute-start(f32[144,128]{1,0:T(8,128)S(1)} %sum_planes.1.refs_0_), channel_id=1, source_target_pairs={{0,16},{8,24},{16,0},{24,8},{1,17},{9,25},{17,1},{25,9},{2,18},{10... | collective-permute-start | bytes 221192 | tf_op jit(solution)/shard_map/ppermute | solution.py:319
  39.3 6.7 %collective-permute-start.11 = (f32[72,512]{1,0:T(8,128)S(1)}, f32[72,512]{1,0:T(8,128)S(1)}, u32[]{:S(2)}, u32[]{:S(2)}) collective-permute-start(f32[72,512]{1,0:T(8,128)S(1)} %get-tuple-element.45.first), channel_id=1, source_target_pairs={{0,4},{1,5},{2,6},{3,7},{4,0},{5,1},{6,2},{7,3},{8,12},{9,13},{10,... | collective-permute-start | bytes 442376 | tf_op jit(solution)/shard_map/ppermute | solution.py:319
  39.9 6.8 %collective-permute-start.12 = (f32[72,512]{1,0:T(8,128)S(1)}, f32[72,512]{1,0:T(8,128)S(1)}, u32[]{:S(2)}, u32[]{:S(2)}) collective-permute-start(f32[72,512]{1,0:T(8,128)S(1)} %get-tuple-element.46.second), channel_id=1, source_target_pairs={{0,2},{1,3},{2,0},{3,1},{4,6},{5,7},{6,4},{7,5},{8,10},{9,11},{10,... | collective-permute-start | bytes 442376 | tf_op jit(solution)/shard_map/ppermute | solution.py:319
  46.7 6.8 %collective-permute-start.13 = (f32[144,512]{1,0:T(8,128)S(1)}, f32[144,512]{1,0:T(8,128)S(1)}, u32[]{:S(2)}, u32[]{:S(2)}) collective-permute-start(f32[144,512]{1,0:T(8,128)S(1)} %get-tuple-element.47.refs_0_), channel_id=1, source_target_pairs={{0,2},{1,3},{2,0},{3,1},{4,6},{5,7},{6,4},{7,5},{8,10},{9,11},{10,... | collective-permute-start | bytes 884744 | tf_op jit(solution)/shard_map/ppermute | solution.py:319
  47.3 6.7 %collective-permute-start.14 = (f32[144,512]{1,0:T(8,128)S(1)}, f32[144,512]{1,0:T(8,128)S(1)}, u32[]{:S(2)}, u32[]{:S(2)}) collective-permute-start(f32[144,512]{1,0:T(8,128)S(1)} %get-tuple-element.48.refs_1_), channel_id=1, source_target_pairs={{0,4},{1,5},{2,6},{3,7},{4,0},{5,1},{6,2},{7,3},{8,12},{9,13},{10,... | collective-permute-start | bytes 884744 | tf_op jit(solution)/shard_map/ppermute | solution.py:319
  48.8 5.2 %collective-permute-start.15 = (f32[144,512]{1,0:T(8,128)S(1)}, f32[144,512]{1,0:T(8,128)S(1)}, u32[]{:S(2)}, u32[]{:S(2)}) collective-permute-start(f32[144,512]{1,0:T(8,128)S(1)} %get-tuple-element.47.refs_0_), channel_id=1, source_target_pairs={{0,1},{1,0},{2,3},{3,2},{4,5},{5,4},{6,7},{7,6},{8,9},{9,8},{10,11... | collective-permute-start | bytes 884744 | tf_op jit(solution)/shard_map/ppermute | solution.py:319
  48.8 5.2 %collective-permute-start.16 = (f32[144,512]{1,0:T(8,128)S(1)}, f32[144,512]{1,0:T(8,128)S(1)}, u32[]{:S(2)}, u32[]{:S(2)}) collective-permute-start(f32[144,512]{1,0:T(8,128)S(1)} %get-tuple-element.48.refs_1_), channel_id=1, source_target_pairs={{0,1},{1,0},{2,3},{3,2},{4,5},{5,4},{6,7},{7,6},{8,9},{9,8},{10,11... | collective-permute-start | bytes 884744 | tf_op jit(solution)/shard_map/ppermute | solution.py:319
  53.5 1.6 %collective-permute-start.17 = (f32[144,512]{1,0:T(8,128)S(1)}, f32[144,512]{1,0:T(8,128)S(1)}, u32[]{:S(2)}, u32[]{:S(2)}) collective-permute-start(f32[144,512]{1,0:T(8,128)S(1)} %collective-permute-done.13.refs_2_), channel_id=1, source_target_pairs={{0,1},{1,0},{2,3},{3,2},{4,5},{5,4},{6,7},{7,6},{8,9},{9,8},{10,11... | collective-permute-start | bytes 884744 | tf_op jit(solution)/shard_map/ppermute | solution.py:319
  54.0 1.6 %collective-permute-start.18 = (f32[144,512]{1,0:T(8,128)S(1)}, f32[144,512]{1,0:T(8,128)S(1)}, u32[]{:S(2)}, u32[]{:S(2)}) collective-permute-start(f32[144,512]{1,0:T(8,128)S(1)} %collective-permute-done.14.refs_3_), channel_id=1, source_target_pairs={{0,1},{1,0},{2,3},{3,2},{4,5},{5,4},{6,7},{7,6},{8,9},{9,8},{10,11... | collective-permute-start | bytes 884744 | tf_op jit(solution)/shard_map/ppermute | solution.py:319
  54.0 21.3 %copy-start.4 = (f32[128,1024]{1,0:T(8,128)S(1)}, f32[128,1024]{1,0:T(8,128)}, u32[]{:S(2)}) copy-start(f32[128,1024]{1,0:T(8,128)} %copy-done.3) | copy-start | bytes 1572868
  70.9 9.4 %collective-permute-start.19 = (f32[128,128]{1,0:T(8,128)S(1)}, f32[128,128]{1,0:T(8,128)S(1)}, u32[]{:S(2)}, u32[]{:S(2)}) collective-permute-start(f32[128,128]{1,0:T(8,128)S(1)} %get-tuple-element.54.refs_0_), channel_id=1, source_target_pairs={{0,8},{8,0},{16,24},{24,16},{1,9},{9,1},{17,25},{25,17},{2,10},{10... | collective-permute-start | bytes 196616 | tf_op jit(solution)/shard_map/ppermute | solution.py:319
  72.3 8.2 %collective-permute-start.20 = (f32[128,128]{1,0:T(8,128)S(1)}, f32[128,128]{1,0:T(8,128)S(1)}, u32[]{:S(2)}, u32[]{:S(2)}) collective-permute-start(f32[128,128]{1,0:T(8,128)S(1)} %get-tuple-element.54.refs_0_), channel_id=1, source_target_pairs={{0,16},{8,24},{16,0},{24,8},{1,17},{9,25},{17,1},{25,9},{2,18},{10... | collective-permute-start | bytes 196616 | tf_op jit(solution)/shard_map/ppermute | solution.py:319
  73.7 6.9 %collective-permute-start.21 = (f32[128,128]{1,0:T(8,128)S(1)}, f32[128,128]{1,0:T(8,128)S(1)}, u32[]{:S(2)}, u32[]{:S(2)}) collective-permute-start(f32[128,128]{1,0:T(8,128)S(1)} %get-tuple-element.54.refs_0_), channel_id=1, source_target_pairs={{0,24},{8,16},{16,8},{24,0},{1,25},{9,17},{17,9},{25,1},{2,26},{10... | collective-permute-start | bytes 196616 | tf_op jit(solution)/shard_map/ppermute | solution.py:319
  81.8 3.6 %collective-permute-start.22 = (f32[8,16]{1,0:T(8,128)S(1)}, f32[8,16]{1,0:T(8,128)S(1)}, u32[]{:S(2)}, u32[]{:S(2)}) collective-permute-start(f32[8,16]{1,0:T(8,128)S(1)} %core_pairs.1), channel_id=1, source_target_pairs={{0,2},{1,3},{2,0},{3,1},{4,6},{5,7},{6,4},{7,5},{8,10},{9,11},{10,... | collective-permute-start | bytes 1544 | tf_op jit(solution)/shard_map/ppermute | solution.py:319
  83.3 3.6 %collective-permute-start.23 = (f32[8,16]{1,0:T(8,128)S(1)}, f32[8,16]{1,0:T(8,128)S(1)}, u32[]{:S(2)}, u32[]{:S(2)}) collective-permute-start(f32[8,16]{1,0:T(8,128)S(1)} %core_pairs.1), channel_id=1, source_target_pairs={{0,4},{1,5},{2,6},{3,7},{4,0},{5,1},{6,2},{7,3},{8,12},{9,13},{10,... | collective-permute-start | bytes 1544 | tf_op jit(solution)/shard_map/ppermute | solution.py:319
  84.8 4.5 %collective-permute-start.24 = (f32[8,16]{1,0:T(8,128)S(1)}, f32[8,16]{1,0:T(8,128)S(1)}, u32[]{:S(2)}, u32[]{:S(2)}) collective-permute-start(f32[8,16]{1,0:T(8,128)S(1)} %core_pairs.1), channel_id=1, source_target_pairs={{0,6},{1,7},{2,4},{3,5},{4,2},{5,3},{6,0},{7,1},{8,14},{9,15},{10,... | collective-permute-start | bytes 1544 | tf_op jit(solution)/shard_map/ppermute | solution.py:319

commit v6 on v5

--- a/solution.py
+++ b/solution.py
@@ -201,13 +201,13 @@
     image = times_gram(basis_ref[...])
     for number in range(ITERS - 1):
         halves = split(image)
-        inner = dot_split(halves, halves, NT)
+        inner = dot_split(halves, halves, NT) + dot_bf16(halves[1], halves[1], NT)
         following = times_gram(image)
         if number == ITERS - 2:
             image_ref[...] = following
             raw_ref[...] = dot_full(field_ref[...], following, NT)
         inverse_factor(inner, factor_ref, spread_ref)
-        image = dot_split(split(factor_ref[...]), split(following), NN)
+        image = dot_full(factor_ref[...], following, NN)
 
 
 def halves_kernel(own_field, other_field, sent_ref, rest_ref):

time: 90.2 us -> 90.9 us (level)
  no operation moved by 1% of the time
where the time goes in v6:
time: 90.9 us; the launch traced here: 90.8 us
  waiting for transfers between devices  32.7 us (36%)
  Pallas kernels  28.6 us (31%)
  starting transfers between devices  27.6 us (30%)
  local copies, waits for them, and re-layouts  1.71 us (2%)
    ppermute x25, waiting for transfers between devices, swap(): lax.ppermute(array, axis, [(i, i ^ mask) for i in range(lax.axis_size(axi...  32.7 us
    pallas_call x12, Pallas kernels, call(): pl.pallas_call(kernel, out_shape=shapes, in_specs=[pl.BlockSpec(memory_sp...  28.6 us
    ppermute x25, starting transfers between devices, swap(): lax.ppermute(array, axis, [(i, i ^ mask) for i in range(lax.axis_size(axi...  27.6 us
  transfers between devices with their start and end apart: 25, of which 19 were waited for; matrix products, arithmetic and copies ran while one was open for 0% of the time, Pallas kernels for 11%

profile of v6, /device:TPU:0, one launch (start us, length us, event | category | flops | bytes accessed | tf_op | source)
XLA Modules:
  0.0 90.8 jit_solution(5141378692395063585)
XLA Ops:
  0.0 0.5 collective-permute-start
  0.5 1.0 %copy-done = f32[8,16,1024]{2,1,0:T(8,128)S(1)} copy-done((f32[8,16,1024]{2,1,0:T(8,128)S(1)}, f32[8,16,1024]{2,1,0:T(8,128)}, u32[]{:S(2)}) %copy-start) | copy-done | bytes 524312
  1.6 0.6 collective-permute-done.other_ref.other_field
  2.2 1.0 %gram_band.1 = (f32[144,512]{1,0:T(8,128)S(1)}, f32[144,512]{1,0:T(8,128)S(1)}, f32[144,512]{1,0:T(8,128)S(1)}, f32[144,512]{1,0:T(8,128)S(1)}) custom-call(bf16[128,1408]{1,0:T(8,128)(2,1)S(1)} %get-tuple-element.30.own_high, bf16[128,1408]{1,0:T(8,128)(2,1)S(1)} %get-tuple-element.31.own_low, f32[128,1024]{1,0:T(8,128)S(1)} %collective-permute-done.other_ref.other_field), custom_call_target="tpu_custom_call" | custom-call | flops 1000000000 | bytes 3145728 | tf_op jit(solution)/shard_map/gram_band/pallas_call | solution.py:305
  3.2 2.9 %collective-permute-start.1 = (f32[144,512]{1,0:T(8,128)S(1)}, f32[144,512]{1,0:T(8,128)S(1)}, u32[]{:S(2)}, u32[]{:S(2)}) collective-permute-start(f32[144,512]{1,0:T(8,128)S(1)} %get-tuple-element.34), channel_id=1, source_target_pairs={{0,2},{1,3},{2,0},{3,1},{4,6},{5,7},{6,4},{7,5},{8,10},{9,11},{10,... | collective-permute-start | bytes 884744 | tf_op jit(solution)/shard_map/ppermute | solution.py:319
  6.1 1.5 %collective-permute-start.2 = (f32[144,512]{1,0:T(8,128)S(1)}, f32[144,512]{1,0:T(8,128)S(1)}, u32[]{:S(2)}, u32[]{:S(2)}) collective-permute-start(f32[144,512]{1,0:T(8,128)S(1)} %get-tuple-element.36), channel_id=1, source_target_pairs={{0,4},{1,5},{2,6},{3,7},{4,0},{5,1},{6,2},{7,3},{8,12},{9,13},{10,... | collective-permute-start | bytes 884744 | tf_op jit(solution)/shard_map/ppermute | solution.py:319
  7.7 5.1 %orth_start.1.after_ref.basis_ref = f32[128,1024]{1,0:T(8,128)S(1)} custom-call(f32[144,512]{1,0:T(8,128)S(1)} %get-tuple-element.32.after_ref.kept_first, f32[1024,128]{1,0:T(8,128)S(1)} %copy-done.2), custom_call_target="tpu_custom_call" | custom-call | flops 1000000000 | bytes 1048576 | tf_op jit(solution)/shard_map/orth_start/pallas_call | solution.py:305
  12.8 0.6 collective-permute-done.1.got_first
  13.4 1.5 %collective-permute-done.2.got_second = f32[144,512]{1,0:T(8,128)S(1)} collective-permute-done((f32[144,512]{1,0:T(8,128)S(1)}, f32[144,512]{1,0:T(8,128)S(1)}, u32[]{:S(2)}, u32[]{:S(2)}) %collective-permute-start.2) | collective-permute-done | bytes 294944 | tf_op jit(solution)/shard_map/ppermute | solution.py:319
  14.9 1.6 %collective-permute-start.3 = (f32[72,512]{1,0:T(8,128)S(1)}, f32[72,512]{1,0:T(8,128)S(1)}, u32[]{:S(2)}, u32[]{:S(2)}) collective-permute-start(f32[72,512]{1,0:T(8,128)S(1)} %get-tuple-element.38), channel_id=1, source_target_pairs={{0,4},{1,5},{2,6},{3,7},{4,0},{5,1},{6,2},{7,3},{8,12},{9,13},{10,... | collective-permute-start | bytes 442376 | tf_op jit(solution)/shard_map/ppermute | solution.py:319
  16.5 0.5 collective-permute-start.4
  17.1 3.1 %collective-permute-done.3.got_first = f32[72,512]{1,0:T(8,128)S(1)} collective-permute-done((f32[72,512]{1,0:T(8,128)S(1)}, f32[72,512]{1,0:T(8,128)S(1)}, u32[]{:S(2)}, u32[]{:S(2)}) %collective-permute-start.3) | collective-permute-done | bytes 147488 | tf_op jit(solution)/shard_map/ppermute | solution.py:319
  20.2 1.5 %collective-permute-done.4.got_second = f32[72,512]{1,0:T(8,128)S(1)} collective-permute-done((f32[72,512]{1,0:T(8,128)S(1)}, f32[72,512]{1,0:T(8,128)S(1)}, u32[]{:S(2)}, u32[]{:S(2)}) %collective-permute-start.4) | collective-permute-done | bytes 147488 | tf_op jit(solution)/shard_map/ppermute | solution.py:319
  21.8 1.6 %collective-permute-start.5 = (f32[144,128]{1,0:T(8,128)S(1)}, f32[144,128]{1,0:T(8,128)S(1)}, u32[]{:S(2)}, u32[]{:S(2)}) collective-permute-start(f32[144,128]{1,0:T(8,128)S(1)} %get-tuple-element.42), channel_id=1, source_target_pairs={{0,8},{8,0},{16,24},{24,16},{1,9},{9,1},{17,25},{25,17},{2,10},{10... | collective-permute-start | bytes 221192 | tf_op jit(solution)/shard_map/ppermute | solution.py:319
  23.4 2.6 %collective-permute-start.6 = (f32[144,128]{1,0:T(8,128)S(1)}, f32[144,128]{1,0:T(8,128)S(1)}, u32[]{:S(2)}, u32[]{:S(2)}) collective-permute-start(f32[144,128]{1,0:T(8,128)S(1)} %get-tuple-element.43), channel_id=1, source_target_pairs={{0,16},{8,24},{16,0},{24,8},{1,17},{9,25},{17,1},{25,9},{2,18},{10... | collective-permute-start | bytes 221192 | tf_op jit(solution)/shard_map/ppermute | solution.py:319
  26.0 0.2 collective-permute-start.7
  26.2 4.0 %collective-permute-done.6.refs_2_ = f32[144,128]{1,0:T(8,128)S(1)} collective-permute-done((f32[144,128]{1,0:T(8,128)S(1)}, f32[144,128]{1,0:T(8,128)S(1)}, u32[]{:S(2)}, u32[]{:S(2)}) %collective-permute-start.6) | collective-permute-done | bytes 73760 | tf_op jit(solution)/shard_map/ppermute | solution.py:319
  30.2 2.0 %collective-permute-done.7.refs_3_ = f32[144,128]{1,0:T(8,128)S(1)} collective-permute-done((f32[144,128]{1,0:T(8,128)S(1)}, f32[144,128]{1,0:T(8,128)S(1)}, u32[]{:S(2)}, u32[]{:S(2)}) %collective-permute-start.7) | collective-permute-done | bytes 73760 | tf_op jit(solution)/shard_map/ppermute | solution.py:319
  32.3 0.9 collective-permute-start.10
  33.1 0.5 collective-permute-start.8
  33.6 3.1 %collective-permute-start.9 = (f32[144,128]{1,0:T(8,128)S(1)}, f32[144,128]{1,0:T(8,128)S(1)}, u32[]{:S(2)}, u32[]{:S(2)}) collective-permute-start(f32[144,128]{1,0:T(8,128)S(1)} %sum_planes.1.refs_0_), channel_id=1, source_target_pairs={{0,16},{8,24},{16,0},{24,8},{1,17},{9,25},{17,1},{25,9},{2,18},{10... | collective-permute-start | bytes 221192 | tf_op jit(solution)/shard_map/ppermute | solution.py:319
  36.7 1.8 %collective-permute-done.10.refs_3_ = f32[144,128]{1,0:T(8,128)S(1)} collective-permute-done((f32[144,128]{1,0:T(8,128)S(1)}, f32[144,128]{1,0:T(8,128)S(1)}, u32[]{:S(2)}, u32[]{:S(2)}) %collective-permute-start.10) | collective-permute-done | bytes 73760 | tf_op jit(solution)/shard_map/ppermute | solution.py:319
  38.5 0.8 collective-permute-done.9.refs_2_
  39.3 0.6 collective-permute-start.11
  39.9 0.5 collective-permute-start.12
  40.4 5.6 %collective-permute-done.11.got_first = f32[72,512]{1,0:T(8,128)S(1)} collective-permute-done((f32[72,512]{1,0:T(8,128)S(1)}, f32[72,512]{1,0:T(8,128)S(1)}, u32[]{:S(2)}, u32[]{:S(2)}) %collective-permute-start.11) | collective-permute-done | bytes 147488 | tf_op jit(solution)/shard_map/ppermute | solution.py:319
  46.1 0.6 collective-permute-done.12.got_second
  46.7 0.6 collective-permute-start.13
  47.3 1.5 %collective-permute-start.14 = (f32[144,512]{1,0:T(8,128)S(1)}, f32[144,512]{1,0:T(8,128)S(1)}, u32[]{:S(2)}, u32[]{:S(2)}) collective-permute-start(f32[144,512]{1,0:T(8,128)S(1)} %get-tuple-element.48.refs_1_), channel_id=1, source_target_pairs={{0,4},{1,5},{2,6},{3,7},{4,0},{5,1},{6,2},{7,3},{8,12},{9,13},{10,... | collective-permute-start | bytes 884744 | tf_op jit(solution)/shard_map/ppermute | solution.py:319
  48.8 0.5 collective-permute-start.16
  49.3 4.2 %collective-permute-done.13.refs_2_ = f32[144,512]{1,0:T(8,128)S(1)} collective-permute-done((f32[144,512]{1,0:T(8,128)S(1)}, f32[144,512]{1,0:T(8,128)S(1)}, u32[]{:S(2)}, u32[]{:S(2)}) %collective-permute-start.13) | collective-permute-done | bytes 294944 | tf_op jit(solution)/shard_map/ppermute | solution.py:319
  53.5 0.5 collective-permute-done.14.refs_3_
  54.0 1.0 %collective-permute-done.17.refs_6_ = f32[144,512]{1,0:T(8,128)S(1)} collective-permute-done((f32[144,512]{1,0:T(8,128)S(1)}, f32[144,512]{1,0:T(8,128)S(1)}, u32[]{:S(2)}, u32[]{:S(2)}) %collective-permute-start.17) | collective-permute-done | bytes 294944 | tf_op jit(solution)/shard_map/ppermute | solution.py:319
  55.1 0.5 collective-permute-done.18.refs_7_
  55.6 16.0 %sweeps.1 = (f32[128,1024]{1,0:T(8,128)S(1)}, f32[128,128]{1,0:T(8,128)S(1)}, f32[128,128]{1,0:T(8,128)S(1)}) custom-call(f32[128,1024]{1,0:T(8,128)S(1)} %orth_start.1.after_ref.basis_ref, f32[128,1024]{1,0:T(8,128)S(1)} %get-tuple-element.33.cells_ref.field_ref, f32[144,512]{1,0:T(8,128)S(1)} %get-tuple-element.47.refs_0_, ...), custom_call_target="tpu_custom_call" | custom-call | bytes 4063232 | tf_op jit(solution)/shard_map/sweeps/pallas_call | solution.py:305
  71.6 1.4 %collective-permute-start.19 = (f32[128,128]{1,0:T(8,128)S(1)}, f32[128,128]{1,0:T(8,128)S(1)}, u32[]{:S(2)}, u32[]{:S(2)}) collective-permute-start(f32[128,128]{1,0:T(8,128)S(1)} %get-tuple-element.54.refs_0_), channel_id=1, source_target_pairs={{0,8},{8,0},{16,24},{24,16},{1,9},{9,1},{17,25},{25,17},{2,10},{10... | collective-permute-start | bytes 196616 | tf_op jit(solution)/shard_map/ppermute | solution.py:319
  73.0 1.4 %collective-permute-start.20 = (f32[128,128]{1,0:T(8,128)S(1)}, f32[128,128]{1,0:T(8,128)S(1)}, u32[]{:S(2)}, u32[]{:S(2)}) collective-permute-start(f32[128,128]{1,0:T(8,128)S(1)} %get-tuple-element.54.refs_0_), channel_id=1, source_target_pairs={{0,16},{8,24},{16,0},{24,8},{1,17},{9,25},{17,1},{25,9},{2,18},{10... | collective-permute-start | bytes 196616 | tf_op jit(solution)/shard_map/ppermute | solution.py:319
  74.4 1.7 %collective-permute-start.21 = (f32[128,128]{1,0:T(8,128)S(1)}, f32[128,128]{1,0:T(8,128)S(1)}, u32[]{:S(2)}, u32[]{:S(2)}) collective-permute-start(f32[128,128]{1,0:T(8,128)S(1)} %get-tuple-element.54.refs_0_), channel_id=1, source_target_pairs={{0,24},{8,16},{16,8},{24,0},{1,25},{9,17},{17,9},{25,1},{2,26},{10... | collective-permute-start | bytes 196616 | tf_op jit(solution)/shard_map/ppermute | solution.py:319
  76.1 4.9 %last_factors.1 = (f32[128,128]{1,0:T(8,128)S(1)}, f32[128,128]{1,0:T(8,128)S(1)}) custom-call(f32[128,1024]{1,0:T(8,128)S(1)} %get-tuple-element.49.image_ref, f32[128,128]{1,0:T(8,128)S(1)} %get-tuple-element.50.before_ref, f32[128,1024]{1,0:T(8,128)S(1)} %copy-done.4), custom_call_target="tpu_custom_call" | custom-call | flops 1000000000 | bytes 1245184 | tf_op jit(solution)/shard_map/last_factors/pallas_call | solution.py:305
  81.0 0.2 collective-permute-done.20.refs_2_
  81.3 1.2 %core_pairs.1 = f32[8,16]{1,0:T(8,128)S(1)} custom-call(f32[128,128]{1,0:T(8,128)S(1)} %get-tuple-element.52.factor_ref, f32[128,128]{1,0:T(8,128)S(1)} %get-tuple-element.53.rest_ref, f32[128,128]{1,0:T(8,128)S(1)} %get-tuple-element.54.refs_0_, f32[128,128]{1,0:T(8,128)S(1)} %collective-permute-done.19.refs_1_, ...), custom_call_target="tpu_custom_call" | custom-call | bytes 393728 | tf_op jit(solution)/shard_map/core_pairs/pallas_call | solution.py:305
  82.5 1.5 %collective-permute-start.22 = (f32[8,16]{1,0:T(8,128)S(1)}, f32[8,16]{1,0:T(8,128)S(1)}, u32[]{:S(2)}, u32[]{:S(2)}) collective-permute-start(f32[8,16]{1,0:T(8,128)S(1)} %core_pairs.1), channel_id=1, source_target_pairs={{0,2},{1,3},{2,0},{3,1},{4,6},{5,7},{6,4},{7,5},{8,10},{9,11},{10,... | collective-permute-start | bytes 1544 | tf_op jit(solution)/shard_map/ppermute | solution.py:319
  84.0 1.5 %collective-permute-start.23 = (f32[8,16]{1,0:T(8,128)S(1)}, f32[8,16]{1,0:T(8,128)S(1)}, u32[]{:S(2)}, u32[]{:S(2)}) collective-permute-start(f32[8,16]{1,0:T(8,128)S(1)} %core_pairs.1), channel_id=1, source_target_pairs={{0,4},{1,5},{2,6},{3,7},{4,0},{5,1},{6,2},{7,3},{8,12},{9,13},{10,... | collective-permute-start | bytes 1544 | tf_op jit(solution)/shard_map/ppermute | solution.py:319
  85.5 0.5 collective-permute-start.24
  86.0 0.1 collective-permute-done.22
  86.1 1.5 %collective-permute-done.23 = f32[8,16]{1,0:T(8,128)S(1)} collective-permute-done((f32[8,16]{1,0:T(8,128)S(1)}, f32[8,16]{1,0:T(8,128)S(1)}, u32[]{:S(2)}, u32[]{:S(2)}) %collective-permute-start.23) | collective-permute-done | bytes 544 | tf_op jit(solution)/shard_map/ppermute | solution.py:319
  87.6 2.4 %collective-permute-done.24 = f32[8,16]{1,0:T(8,128)S(1)} collective-permute-done((f32[8,16]{1,0:T(8,128)S(1)}, f32[8,16]{1,0:T(8,128)S(1)}, u32[]{:S(2)}, u32[]{:S(2)}) %collective-permute-start.24) | collective-permute-done | bytes 544 | tf_op jit(solution)/shard_map/ppermute | solution.py:319
  90.1 0.7 copy.3
  (27 shorter events, 0.6 us)
Async XLA Ops:
  0.0 2.2 %collective-permute-start = (f32[128,1024]{1,0:T(8,128)}, f32[128,1024]{1,0:T(8,128)S(1)}, u32[]{:S(2)}, u32[]{:S(2)}) collective-permute-start(f32[128,1024]{1,0:T(8,128)} %bitcast.1), channel_id=1, source_target_pairs={{0,1},{1,0},{2,3},{3,2},{4,5},{5,4},{6,7},{7,6},{8,9},{9,8},{10,11... | collective-permute-start | bytes 1572872 | tf_op jit(solution)/shard_map/ppermute | solution.py:319
  0.5 1.0 %copy-start = (f32[8,16,1024]{2,1,0:T(8,128)S(1)}, f32[8,16,1024]{2,1,0:T(8,128)}, u32[]{:S(2)}) copy-start(f32[8,16,1024]{2,1,0:T(8,128)} %param.2) | copy-start | bytes 1572868
  2.2 5.4 %copy-start.1 = (f32[8,16,1024]{2,1,0:T(8,128)S(1)}, f32[8,16,1024]{2,1,0:T(8,128)}, u32[]{:S(2)}) copy-start(f32[8,16,1024]{2,1,0:T(8,128)} %param.2) | copy-start | bytes 1572868
  3.2 10.2 %collective-permute-start.1 = (f32[144,512]{1,0:T(8,128)S(1)}, f32[144,512]{1,0:T(8,128)S(1)}, u32[]{:S(2)}, u32[]{:S(2)}) collective-permute-start(f32[144,512]{1,0:T(8,128)S(1)} %get-tuple-element.34), channel_id=1, source_target_pairs={{0,2},{1,3},{2,0},{3,1},{4,6},{5,7},{6,4},{7,5},{8,10},{9,11},{10,... | collective-permute-start | bytes 884744 | tf_op jit(solution)/shard_map/ppermute | solution.py:319
  6.1 1.6 %copy-start.2 = (f32[1024,128]{1,0:T(8,128)S(1)}, f32[1024,128]{1,0:T(8,128)}, u32[]{:S(2)}) copy-start(f32[1024,128]{1,0:T(8,128)} %start_ref.1) | copy-start | bytes 1572868
  6.1 8.8 %collective-permute-start.2 = (f32[144,512]{1,0:T(8,128)S(1)}, f32[144,512]{1,0:T(8,128)S(1)}, u32[]{:S(2)}, u32[]{:S(2)}) collective-permute-start(f32[144,512]{1,0:T(8,128)S(1)} %get-tuple-element.36), channel_id=1, source_target_pairs={{0,4},{1,5},{2,6},{3,7},{4,0},{5,1},{6,2},{7,3},{8,12},{9,13},{10,... | collective-permute-start | bytes 884744 | tf_op jit(solution)/shard_map/ppermute | solution.py:319
  7.7 5.1 %copy-start.3 = (f32[128,1024]{1,0:T(8,128)}, f32[128,1024]{1,0:T(8,128)S(1)}, u32[]{:S(2)}) copy-start(f32[128,1024]{1,0:T(8,128)S(1)} %get-tuple-element.51.refs_0_) | copy-start | bytes 1572868
  14.9 5.2 %collective-permute-start.3 = (f32[72,512]{1,0:T(8,128)S(1)}, f32[72,512]{1,0:T(8,128)S(1)}, u32[]{:S(2)}, u32[]{:S(2)}) collective-permute-start(f32[72,512]{1,0:T(8,128)S(1)} %get-tuple-element.38), channel_id=1, source_target_pairs={{0,4},{1,5},{2,6},{3,7},{4,0},{5,1},{6,2},{7,3},{8,12},{9,13},{10,... | collective-permute-start | bytes 442376 | tf_op jit(solution)/shard_map/ppermute | solution.py:319
  16.5 5.1 %collective-permute-start.4 = (f32[72,512]{1,0:T(8,128)S(1)}, f32[72,512]{1,0:T(8,128)S(1)}, u32[]{:S(2)}, u32[]{:S(2)}) collective-permute-start(f32[72,512]{1,0:T(8,128)S(1)} %get-tuple-element.40), channel_id=1, source_target_pairs={{0,2},{1,3},{2,0},{3,1},{4,6},{5,7},{6,4},{7,5},{8,10},{9,11},{10,... | collective-permute-start | bytes 442376 | tf_op jit(solution)/shard_map/ppermute | solution.py:319
  21.8 4.5 %collective-permute-start.5 = (f32[144,128]{1,0:T(8,128)S(1)}, f32[144,128]{1,0:T(8,128)S(1)}, u32[]{:S(2)}, u32[]{:S(2)}) collective-permute-start(f32[144,128]{1,0:T(8,128)S(1)} %get-tuple-element.42), channel_id=1, source_target_pairs={{0,8},{8,0},{16,24},{24,16},{1,9},{9,1},{17,25},{25,17},{2,10},{10... | collective-permute-start | bytes 221192 | tf_op jit(solution)/shard_map/ppermute | solution.py:319
  23.4 6.8 %collective-permute-start.6 = (f32[144,128]{1,0:T(8,128)S(1)}, f32[144,128]{1,0:T(8,128)S(1)}, u32[]{:S(2)}, u32[]{:S(2)}) collective-permute-start(f32[144,128]{1,0:T(8,128)S(1)} %get-tuple-element.43), channel_id=1, source_target_pairs={{0,16},{8,24},{16,0},{24,8},{1,17},{9,25},{17,1},{25,9},{2,18},{10... | collective-permute-start | bytes 221192 | tf_op jit(solution)/shard_map/ppermute | solution.py:319
  26.0 6.3 %collective-permute-start.7 = (f32[144,128]{1,0:T(8,128)S(1)}, f32[144,128]{1,0:T(8,128)S(1)}, u32[]{:S(2)}, u32[]{:S(2)}) collective-permute-start(f32[144,128]{1,0:T(8,128)S(1)} %get-tuple-element.44), channel_id=1, source_target_pairs={{0,24},{8,16},{16,8},{24,0},{1,25},{9,17},{17,9},{25,1},{2,26},{10... | collective-permute-start | bytes 221192 | tf_op jit(solution)/shard_map/ppermute | solution.py:319
  32.3 6.2 %collective-permute-start.10 = (f32[144,128]{1,0:T(8,128)S(1)}, f32[144,128]{1,0:T(8,128)S(1)}, u32[]{:S(2)}, u32[]{:S(2)}) collective-permute-start(f32[144,128]{1,0:T(8,128)S(1)} %sum_planes.1.refs_0_), channel_id=1, source_target_pairs={{0,24},{8,16},{16,8},{24,0},{1,25},{9,17},{17,9},{25,1},{2,26},{10... | collective-permute-start | bytes 221192 | tf_op jit(solution)/shard_map/ppermute | solution.py:319
  33.1 5.4 %collective-permute-start.8 = (f32[144,128]{1,0:T(8,128)S(1)}, f32[144,128]{1,0:T(8,128)S(1)}, u32[]{:S(2)}, u32[]{:S(2)}) collective-permute-start(f32[144,128]{1,0:T(8,128)S(1)} %sum_planes.1.refs_0_), channel_id=1, source_target_pairs={{0,8},{8,0},{16,24},{24,16},{1,9},{9,1},{17,25},{25,17},{2,10},{10... | collective-permute-start | bytes 221192 | tf_op jit(solution)/shard_map/ppermute | solution.py:319
  33.6 5.6 %collective-permute-start.9 = (f32[144,128]{1,0:T(8,128)S(1)}, f32[144,128]{1,0:T(8,128)S(1)}, u32[]{:S(2)}, u32[]{:S(2)}) collective-permute-start(f32[144,128]{1,0:T(8,128)S(1)} %sum_planes.1.refs_0_), channel_id=1, source_target_pairs={{0,16},{8,24},{16,0},{24,8},{1,17},{9,25},{17,1},{25,9},{2,18},{10... | collective-permute-start | bytes 221192 | tf_op jit(solution)/shard_map/ppermute | solution.py:319
  39.3 6.7 %collective-permute-start.11 = (f32[72,512]{1,0:T(8,128)S(1)}, f32[72,512]{1,0:T(8,128)S(1)}, u32[]{:S(2)}, u32[]{:S(2)}) collective-permute-start(f32[72,512]{1,0:T(8,128)S(1)} %get-tuple-element.45.first), channel_id=1, source_target_pairs={{0,4},{1,5},{2,6},{3,7},{4,0},{5,1},{6,2},{7,3},{8,12},{9,13},{10,... | collective-permute-start | bytes 442376 | tf_op jit(solution)/shard_map/ppermute | solution.py:319
  39.9 6.8 %collective-permute-start.12 = (f32[72,512]{1,0:T(8,128)S(1)}, f32[72,512]{1,0:T(8,128)S(1)}, u32[]{:S(2)}, u32[]{:S(2)}) collective-permute-start(f32[72,512]{1,0:T(8,128)S(1)} %get-tuple-element.46.second), channel_id=1, source_target_pairs={{0,2},{1,3},{2,0},{3,1},{4,6},{5,7},{6,4},{7,5},{8,10},{9,11},{10,... | collective-permute-start | bytes 442376 | tf_op jit(solution)/shard_map/ppermute | solution.py:319
  46.7 6.8 %collective-permute-start.13 = (f32[144,512]{1,0:T(8,128)S(1)}, f32[144,512]{1,0:T(8,128)S(1)}, u32[]{:S(2)}, u32[]{:S(2)}) collective-permute-start(f32[144,512]{1,0:T(8,128)S(1)} %get-tuple-element.47.refs_0_), channel_id=1, source_target_pairs={{0,2},{1,3},{2,0},{3,1},{4,6},{5,7},{6,4},{7,5},{8,10},{9,11},{10,... | collective-permute-start | bytes 884744 | tf_op jit(solution)/shard_map/ppermute | solution.py:319
  47.3 6.7 %collective-permute-start.14 = (f32[144,512]{1,0:T(8,128)S(1)}, f32[144,512]{1,0:T(8,128)S(1)}, u32[]{:S(2)}, u32[]{:S(2)}) collective-permute-start(f32[144,512]{1,0:T(8,128)S(1)} %get-tuple-element.48.refs_1_), channel_id=1, source_target_pairs={{0,4},{1,5},{2,6},{3,7},{4,0},{5,1},{6,2},{7,3},{8,12},{9,13},{10,... | collective-permute-start | bytes 884744 | tf_op jit(solution)/shard_map/ppermute | solution.py:319
  48.8 5.2 %collective-permute-start.15 = (f32[144,512]{1,0:T(8,128)S(1)}, f32[144,512]{1,0:T(8,128)S(1)}, u32[]{:S(2)}, u32[]{:S(2)}) collective-permute-start(f32[144,512]{1,0:T(8,128)S(1)} %get-tuple-element.47.refs_0_), channel_id=1, source_target_pairs={{0,1},{1,0},{2,3},{3,2},{4,5},{5,4},{6,7},{7,6},{8,9},{9,8},{10,11... | collective-permute-start | bytes 884744 | tf_op jit(solution)/shard_map/ppermute | solution.py:319
  48.8 5.2 %collective-permute-start.16 = (f32[144,512]{1,0:T(8,128)S(1)}, f32[144,512]{1,0:T(8,128)S(1)}, u32[]{:S(2)}, u32[]{:S(2)}) collective-permute-start(f32[144,512]{1,0:T(8,128)S(1)} %get-tuple-element.48.refs_1_), channel_id=1, source_target_pairs={{0,1},{1,0},{2,3},{3,2},{4,5},{5,4},{6,7},{7,6},{8,9},{9,8},{10,11... | collective-permute-start | bytes 884744 | tf_op jit(solution)/shard_map/ppermute | solution.py:319
  53.5 1.6 %collective-permute-start.17 = (f32[144,512]{1,0:T(8,128)S(1)}, f32[144,512]{1,0:T(8,128)S(1)}, u32[]{:S(2)}, u32[]{:S(2)}) collective-permute-start(f32[144,512]{1,0:T(8,128)S(1)} %collective-permute-done.13.refs_2_), channel_id=1, source_target_pairs={{0,1},{1,0},{2,3},{3,2},{4,5},{5,4},{6,7},{7,6},{8,9},{9,8},{10,11... | collective-permute-start | bytes 884744 | tf_op jit(solution)/shard_map/ppermute | solution.py:319
  54.0 1.6 %collective-permute-start.18 = (f32[144,512]{1,0:T(8,128)S(1)}, f32[144,512]{1,0:T(8,128)S(1)}, u32[]{:S(2)}, u32[]{:S(2)}) collective-permute-start(f32[144,512]{1,0:T(8,128)S(1)} %collective-permute-done.14.refs_3_), channel_id=1, source_target_pairs={{0,1},{1,0},{2,3},{3,2},{4,5},{5,4},{6,7},{7,6},{8,9},{9,8},{10,11... | collective-permute-start | bytes 884744 | tf_op jit(solution)/shard_map/ppermute | solution.py:319
  54.0 22.0 %copy-start.4 = (f32[128,1024]{1,0:T(8,128)S(1)}, f32[128,1024]{1,0:T(8,128)}, u32[]{:S(2)}) copy-start(f32[128,1024]{1,0:T(8,128)} %copy-done.3) | copy-start | bytes 1572868
  71.6 9.4 %collective-permute-start.19 = (f32[128,128]{1,0:T(8,128)S(1)}, f32[128,128]{1,0:T(8,128)S(1)}, u32[]{:S(2)}, u32[]{:S(2)}) collective-permute-start(f32[128,128]{1,0:T(8,128)S(1)} %get-tuple-element.54.refs_0_), channel_id=1, source_target_pairs={{0,8},{8,0},{16,24},{24,16},{1,9},{9,1},{17,25},{25,17},{2,10},{10... | collective-permute-start | bytes 196616 | tf_op jit(solution)/shard_map/ppermute | solution.py:319
  73.0 8.2 %collective-permute-start.20 = (f32[128,128]{1,0:T(8,128)S(1)}, f32[128,128]{1,0:T(8,128)S(1)}, u32[]{:S(2)}, u32[]{:S(2)}) collective-permute-start(f32[128,128]{1,0:T(8,128)S(1)} %get-tuple-element.54.refs_0_), channel_id=1, source_target_pairs={{0,16},{8,24},{16,0},{24,8},{1,17},{9,25},{17,1},{25,9},{2,18},{10... | collective-permute-start | bytes 196616 | tf_op jit(solution)/shard_map/ppermute | solution.py:319
  74.4 6.9 %collective-permute-start.21 = (f32[128,128]{1,0:T(8,128)S(1)}, f32[128,128]{1,0:T(8,128)S(1)}, u32[]{:S(2)}, u32[]{:S(2)}) collective-permute-start(f32[128,128]{1,0:T(8,128)S(1)} %get-tuple-element.54.refs_0_), channel_id=1, source_target_pairs={{0,24},{8,16},{16,8},{24,0},{1,25},{9,17},{17,9},{25,1},{2,26},{10... | collective-permute-start | bytes 196616 | tf_op jit(solution)/shard_map/ppermute | solution.py:319
  82.5 3.6 %collective-permute-start.22 = (f32[8,16]{1,0:T(8,128)S(1)}, f32[8,16]{1,0:T(8,128)S(1)}, u32[]{:S(2)}, u32[]{:S(2)}) collective-permute-start(f32[8,16]{1,0:T(8,128)S(1)} %core_pairs.1), channel_id=1, source_target_pairs={{0,2},{1,3},{2,0},{3,1},{4,6},{5,7},{6,4},{7,5},{8,10},{9,11},{10,... | collective-permute-start | bytes 1544 | tf_op jit(solution)/shard_map/ppermute | solution.py:319
  84.0 3.6 %collective-permute-start.23 = (f32[8,16]{1,0:T(8,128)S(1)}, f32[8,16]{1,0:T(8,128)S(1)}, u32[]{:S(2)}, u32[]{:S(2)}) collective-permute-start(f32[8,16]{1,0:T(8,128)S(1)} %core_pairs.1), channel_id=1, source_target_pairs={{0,4},{1,5},{2,6},{3,7},{4,0},{5,1},{6,2},{7,3},{8,12},{9,13},{10,... | collective-permute-start | bytes 1544 | tf_op jit(solution)/shard_map/ppermute | solution.py:319
  85.5 4.5 %collective-permute-start.24 = (f32[8,16]{1,0:T(8,128)S(1)}, f32[8,16]{1,0:T(8,128)S(1)}, u32[]{:S(2)}, u32[]{:S(2)}) collective-permute-start(f32[8,16]{1,0:T(8,128)S(1)} %core_pairs.1), channel_id=1, source_target_pairs={{0,6},{1,7},{2,4},{3,5},{4,2},{5,3},{6,0},{7,1},{8,14},{9,15},{10,... | collective-permute-start | bytes 1544 | tf_op jit(solution)/shard_map/ppermute | solution.py:319
